TPU v7x, 256 devices: a whole 4x4x8 slice. The times are simulated.
256 devices in a mesh: dp: 8 (over y, core), fsdp: 4 (over x), tensor: 8 (over z).
Axes of the slice: x: 4, y: 4, z: 8, core: 2. Of those that a mesh axis runs over, the one named last changes fastest.
Arguments:
- gradients: bfloat16 [8, 4096, 14336], P('dp', 'fsdp', 'tensor'), may hold values from -40 to 40
- errors: bfloat16 [8, 4096, 14336], P('dp', 'fsdp', 'tensor'), may hold values from -3 to 3
- start_factor: float32 [14336, 128], P('tensor'), may hold values from -6 to 6
Outputs:
- right_factor: float32 [14336, 128], P('tensor')
- new_errors: bfloat16 [8, 4096, 14336], P('dp', 'fsdp', 'tensor')
All inputs are finite; a program needn't handle non-finite values.
Results may differ from a plain program's by a relative error of at most 0.0014.
Values sent between devices are 32-bit elements; how exact they have to be, the bound alone decides.
No kernel may reach another device: no remote copies, remote signals or barrier semaphores. Data moves between devices by JAX's collectives and lax.ppermute only.
A program may use at most 64 MiB of HBM per device.

v0:
```python
import jax
import jax.numpy as jnp
from jax import lax
from jax.sharding import PartitionSpec as P


def cholesky_pass(sketch, gram_matrix):
    lower_factor = jnp.linalg.cholesky(gram_matrix)
    return lax.linalg.triangular_solve(
        lower_factor, sketch, left_side=False, lower=True, transpose_a=True
    )


def local_gram(sketch):
    return jnp.dot(
        sketch.T, sketch, precision=lax.Precision.HIGHEST, preferred_element_type=jnp.float32
    )


def whole_gram(sketch):
    return lax.psum(local_gram(sketch), "fsdp")


def shards(gradients, errors, start_factor):
    merged = gradients[0].astype(jnp.float32) + errors[0].astype(jnp.float32)
    local_sketch = jnp.dot(
        merged, start_factor, precision=lax.Precision.HIGHEST, preferred_element_type=jnp.float32
    )
    basis_cols = lax.psum(local_sketch, ("dp", "tensor"))
    for turn in range(2):
        basis_cols = cholesky_pass(basis_cols, whole_gram(basis_cols))
    factor_term = lax.dot_general(
        merged,
        basis_cols,
        (((0,), (0,)), ((), ())),
        precision=lax.Precision.HIGHEST,
        preferred_element_type=jnp.float32,
    )
    right_factor = lax.psum(factor_term, ("dp", "fsdp")) / lax.axis_size("dp")
    update = jnp.dot(
        basis_cols,
        right_factor.T,
        precision=lax.Precision.HIGHEST,
        preferred_element_type=jnp.float32,
    )
    new_errors = (merged - update).astype(jnp.bfloat16)
    return (right_factor, new_errors[None])


def solution(mesh):
    return jax.shard_map(
        shards,
        mesh=mesh,
        in_specs=(P("dp", "fsdp", "tensor"), P("dp", "fsdp", "tensor"), P("tensor", None)),
        out_specs=(P("tensor", None), P("dp", "fsdp", "tensor")),
        check_vma=False,
    )
```

profile of v0, /device:TPU:1, one launch (start us, length us, event | category | flops | bytes accessed | tf_op | source)
XLA Modules:
  0.0 496.0 jit_solution(17884165214768616740)
XLA Ops:
  7.2 0.0 all-reduce.5.cloned.1.call-start
  7.2 1.1 copy-done
  8.3 9.0 %fusion.2 = f32[1024,128]{1,0:T(8,128)} fusion(f32[1792,128]{1,0:T(8,128)S(1)} %copy-done, bf16[1,1024,1792]{2,1,0:T(8,128)(2,1)} %param.7, bf16[1,1024,1792]{2,1,0:T(8,128)(2,1)} %param.6), kind=kOutput, calls=%fused_computation.3 | convolution fusion | flops 2824077312 | bytes 8781824 | tf_op jit(solution)/shard_map/dot_general | solution.py:26
  17.4 0.0 all-reduce.5.cloned.1.call-update
  17.4 0.0 all-reduce.7.cloned.1.call-start
  17.4 183.3 %all-reduce.5.cloned.1.call-done = f32[1024,128]{1,0:T(8,128)} async-done(((f32[1024,128]{1,0:T(8,128)}), f32[1024,128]{1,0:T(8,128)}) %all-reduce.5.cloned.1.call-update) | async-done | bytes 524304 | tf_op jit(solution)/shard_map/psum | solution.py:29
  200.7 2.8 fusion.14
  203.5 0.0 all-reduce.7.cloned.1.call-update
  203.5 0.0 all-reduce.9.cloned.1.call-start
  203.6 43.3 %all-reduce.7.cloned.1.call-done = f32[128,128]{0,1:T(8,128)} async-done(((f32[128,128]{0,1:T(8,128)}), f32[128,128]{0,1:T(8,128)}) %all-reduce.7.cloned.1.call-update) | async-done | bytes 65552 | tf_op jit(solution)/shard_map/psum | solution.py:21
  246.9 0.9 copy.6
  247.8 0.9 fusion.11
  248.6 11.7 %cholesky.44 = f32[128,128]{1,0:T(8,128)S(1)} custom-call(f32[128,128]{1,0:T(8,128)S(1)} %fusion.11), custom_call_target="Cholesky" | custom-call | tf_op jit(solution)/shard_map/jit(cholesky)/cholesky | solution.py:8
  260.4 0.6 compare_reduce_fusion.1
  261.0 0.7 fusion.6
  261.7 9.8 %custom-call.6 = f32[1,128,128]{1,2,0:T(8,128)S(1)} custom-call(f32[1,128,128]{2,1,0:T(8,128)S(1)} %fusion.6), custom_call_target="InvertDiagBlocksLowerTriangular" | custom-call | tf_op jit(solution)/shard_map/triangular_solve/custom-call.0 | solution.py:9
  271.5 1.7 convolution_bitcast_fusion.1
  273.2 1.2 fusion.15
  274.4 0.0 all-reduce.9.cloned.1.call-update
  274.4 0.2 all-reduce.11.cloned.1.call-start
  274.7 46.3 %all-reduce.9.cloned.1.call-done = f32[128,128]{0,1:T(8,128)} async-done(((f32[128,128]{0,1:T(8,128)}), f32[128,128]{0,1:T(8,128)}) %all-reduce.9.cloned.1.call-update) | async-done | bytes 65552 | tf_op jit(solution)/shard_map/psum | solution.py:21
  320.9 0.9 copy.8
  321.9 0.9 fusion.9
  322.7 11.7 %cholesky.55 = f32[128,128]{1,0:T(8,128)S(1)} custom-call(f32[128,128]{1,0:T(8,128)S(1)} %fusion.9), custom_call_target="Cholesky" | custom-call | tf_op jit(solution)/shard_map/jit(cholesky)/cholesky | solution.py:8
  334.5 0.6 compare_reduce_fusion
  335.1 0.7 fusion.7
  335.8 9.8 %custom-call.7 = f32[1,128,128]{1,2,0:T(8,128)S(1)} custom-call(f32[1,128,128]{2,1,0:T(8,128)S(1)} %fusion.7), custom_call_target="InvertDiagBlocksLowerTriangular" | custom-call | tf_op jit(solution)/shard_map/triangular_solve/custom-call.0 | solution.py:9
  345.6 0.6 convolution_bitcast_fusion
  346.2 14.8 %fusion = f32[1792,128]{1,0:T(8,128)} fusion(f32[1024,128]{0,1:T(8,128)S(1)} %convolution_bitcast_fusion, bf16[1,1024,1792]{2,1,0:T(8,128)(2,1)} %param.7, bf16[1,1024,1792]{2,1,0:T(8,128)(2,1)} %param.6), kind=kOutput, calls=%fused_computation.1 | convolution fusion | flops 2824077312 | bytes 8781824 | tf_op jit(solution)/shard_map/dot_general | solution.py:32
  361.0 116.6 %all-reduce.11.cloned.1.call-done = f32[1792,128]{1,0:T(8,128)} async-done(((f32[1792,128]{1,0:T(8,128)}), f32[1792,128]{1,0:T(8,128)}) %all-reduce.11.cloned.1.call-update) | async-done | bytes 917520 | tf_op jit(solution)/shard_map/psum | solution.py:39
  477.7 1.2 broadcast_multiply_fusion
  479.0 10.5 %fusion.5 = bf16[1,1024,1792]{2,1,0:T(8,128)(2,1)} fusion(f32[1024,128]{0,1:T(8,128)S(1)} %convolution_bitcast_fusion, f32[1792,128]{1,0:T(8,128)S(1)} %broadcast_multiply_fusion, bf16[1,1024,1792]{2,1,0:T(8,128)(2,1)} %param.7, bf16[1,1024,1792]{2,1,0:T(8,128)(2,1)} %param.6), kind=kOutput, calls=%fused_computation.7 | convolution fusion | flops 2827747328 | bytes 12451840 | tf_op jit(solution)/shard_map/dot_general | solution.py:40
  (6 shorter events, 0.1 us)
Async XLA Ops:
  7.2 1.2 copy-start
  7.2 193.5 %all-reduce.5.cloned.1.call-start = ((), (), s32[]{:S(2)}) async-start(), calls=%async_computation | async-start | bytes 1048576 | tf_op jit(solution)/shard_map/psum | solution.py:29
  17.4 229.5 %all-reduce.7.cloned.1.call-start = ((), (), s32[]{:S(2)}) async-start(), calls=%async_computation.1 | async-start | bytes 131072 | tf_op jit(solution)/shard_map/psum | solution.py:21
  203.5 117.4 %all-reduce.9.cloned.1.call-start = ((), (), s32[]{:S(2)}) async-start(), calls=%async_computation.2 | async-start | bytes 131072 | tf_op jit(solution)/shard_map/psum | solution.py:21
  274.4 203.2 %all-reduce.11.cloned.1.call-start = ((), (), s32[]{:S(2)}) async-start(), calls=%async_computation.3 | async-start | bytes 1835008 | tf_op jit(solution)/shard_map/psum | solution.py:39
  478.9 10.5 %copy-start.1 = (f32[1792,128]{1,0:T(8,128)}, f32[1792,128]{1,0:T(8,128)S(1)}, u32[]{:S(2)}) copy-start(f32[1792,128]{1,0:T(8,128)S(1)} %broadcast_multiply_fusion) | copy-start | bytes 2752516
Sparse Core Ops, SparseCore 0:
  17.5 183.1 all-reduce.4
  203.7 43.1 all-reduce.6
  274.6 46.3 all-reduce.8
  361.2 116.4 all-reduce.10
where the time goes:
time: 496 us
  waiting for transfers between devices  389 us (78%)
  other arithmetic  48.7 us (10%)
  matrix products  40.6 us (8%)
  between operations  13.9 us (3%)
    psum x1, waiting for transfers between devices, shards(): basis_cols = lax.psum(local_sketch, ('dp', 'tensor'))  183 us
    psum x1, waiting for transfers between devices, shards(): right_factor = lax.psum(factor_term, ('dp', 'fsdp')) / lax.axis_size('dp')  117 us
    psum x2, waiting for transfers between devices, whole_gram(): return lax.psum(local_gram(sketch), 'fsdp')  89.5 us
    another operation x6, other arithmetic, cholesky_pass(): lower_factor = jnp.linalg.cholesky(gram_matrix)  24.8 us
    another operation x4, other arithmetic, cholesky_pass(): lax.linalg.triangular_solve(lower_factor, sketch, left_side=False, lower=...  20.9 us
    dot_general x1, matrix products, shards(): lax.dot_general(merged, basis_cols, (((0,), (0,)), ((), ())), precision=l...  14.8 us
    dot_general x1, matrix products, shards(): jnp.dot(basis_cols, right_factor.T, precision=lax.Precision.HIGHEST, pref...  10.5 us
  transfers between devices with their start and end apart: 4, of which 4 were waited for; matrix products, arithmetic and copies ran while one was open for 0% of the time, Pallas kernels for 0%

commit v1 on v0

v1 whole, which is shorter than its diff:
```python
import functools

import jax
import jax.numpy as jnp
from jax import lax
from jax.experimental import pallas as pl
from jax.experimental.pallas import tpu as pltpu
from jax.sharding import Mesh, PartitionSpec as P

F32, BF16 = jnp.float32, jnp.bfloat16
RANK = 128
ROWS = 256
COLS = 256
VMEM_LIMIT = 40 * 1024 * 1024
NT = (((1,), (1,)), ((), ()))
NN = (((1,), (0,)), ((), ()))
TN = (((0,), (0,)), ((), ()))


def mm(a, b, dims=NN):
    return lax.dot_general(a, b, dims, preferred_element_type=F32)


def mm32(a, b, dims=NN):
    return lax.dot_general(a, b, dims, precision=lax.Precision.HIGHEST, preferred_element_type=F32)


def split3(x):
    hi = x.astype(BF16)
    rest = x - hi.astype(F32)
    mid = rest.astype(BF16)
    low = (rest - mid.astype(F32)).astype(BF16)
    return hi, mid, low


def params():
    return pltpu.CompilerParams(vmem_limit_bytes=VMEM_LIMIT)


def sketch_kernel(g_ref, e_ref, p_ref, keep_ref, send_ref, p12, p3):
    step = pl.program_id(0)
    half_steps = pl.num_programs(0) // 2

    @pl.when(step == 0)
    def _():
        hi, mid, low = split3(p_ref[...])
        p12[:, :RANK] = hi
        p12[:, RANK:] = mid
        p3[...] = low

    g, e = g_ref[...], e_ref[...]
    both = mm(g, p12[...]) + mm(e, p12[...])
    block = both[:, :RANK] + both[:, RANK:] + mm(g + e, p3[...])
    mine = step // half_steps == lax.axis_index("core")
    rows = pl.ds(pl.multiple_of(lax.rem(step, half_steps) * ROWS, ROWS), ROWS)

    @pl.when(mine)
    def _():
        keep_ref[rows, :] = block

    @pl.when(jnp.logical_not(mine))
    def _():
        send_ref[rows, :] = block


def local_sketch(g, e, p):
    n, m = g.shape
    whole = pl.BlockSpec((n // 2, RANK), lambda i: (0, 0))
    out = jax.ShapeDtypeStruct((n // 2, RANK), F32)
    rows = min(ROWS, n // 2)
    return pl.pallas_call(
        sketch_kernel,
        grid=(n // rows,),
        in_specs=[
            pl.BlockSpec((rows, m), lambda i: (i, 0)),
            pl.BlockSpec((rows, m), lambda i: (i, 0)),
            pl.BlockSpec((m, RANK), lambda i: (0, 0)),
        ],
        out_specs=[whole, whole],
        out_shape=[out, out],
        scratch_shapes=[pltpu.VMEM((m, 2 * RANK), BF16), pltpu.VMEM((m, RANK), BF16)],
        compiler_params=params(),
        name="local_sketch",
    )(g, e, p)


def total_kernel(parts_ref, out_ref):
    total = parts_ref[0]
    for i in range(1, parts_ref.shape[0]):
        total = total + parts_ref[i]
    for i in range(parts_ref.shape[0]):
        out_ref[i] = total


def total_for_all(parts):
    return pl.pallas_call(
        total_kernel,
        out_shape=jax.ShapeDtypeStruct(parts.shape, F32),
        compiler_params=params(),
        name="sketch_total",
    )(parts)


def factor_kernel(own_ref, other_ref, g_ref, e_ref, sketch_ref, keep_ref, send_ref, gram_ref, s12, s3, turned):
    core = lax.axis_index("core")

    @pl.when(pl.program_id(0) == 0)
    def _():
        half = own_ref.shape[0]
        sketch_ref[pl.ds(pl.multiple_of(core * half, half), half), :] = own_ref[...]
        sketch_ref[pl.ds(pl.multiple_of((1 - core) * half, half), half), :] = other_ref[...]
        hi, mid, low = split3(sketch_ref[...].T)
        s12[:RANK, :] = hi
        s12[RANK:, :] = mid
        s3[...] = low
        square = mm(s12[...], s12[...], NT)
        cross = mm(s12[:RANK, :], s3[...], NT)
        gram_ref[...] = (
            square[:RANK, :RANK] + square[RANK:, RANK:]
            + (square[:RANK, RANK:] + square[RANK:, :RANK])
            + (cross + cross.T)
        )

    g, e = g_ref[...], e_ref[...]
    both = mm(s12[...], g) + mm(s12[...], e)
    block = both[:RANK] + both[RANK:] + mm(s3[...], g + e)
    turned[...] = block.T
    keep_ref[...] = turned[pl.ds(pl.multiple_of(core * RANK, RANK), RANK), :]
    send_ref[...] = turned[pl.ds(pl.multiple_of((1 - core) * RANK, RANK), RANK), :]


def factor_terms(own, other, g, e):
    n, m = g.shape
    half = pl.BlockSpec((n // 2, RANK), lambda j: (0, 0))
    block = pl.BlockSpec((n, COLS), lambda j: (0, j))
    rows = pl.BlockSpec((RANK, RANK), lambda j: (j, 0))
    return pl.pallas_call(
        factor_kernel,
        grid=(m // COLS,),
        in_specs=[half, half, block, block],
        out_specs=[
            pl.BlockSpec((n, RANK), lambda j: (0, 0)),
            rows,
            rows,
            pl.BlockSpec((RANK, RANK), lambda j: (0, 0)),
        ],
        out_shape=[
            jax.ShapeDtypeStruct((n, RANK), F32),
            jax.ShapeDtypeStruct((m // 2, RANK), F32),
            jax.ShapeDtypeStruct((m // 2, RANK), F32),
            jax.ShapeDtypeStruct((RANK, RANK), F32),
        ],
        scratch_shapes=[
            pltpu.VMEM((2 * RANK, n), BF16),
            pltpu.VMEM((RANK, n), BF16),
            pltpu.VMEM((COLS, RANK), F32),
        ],
        compiler_params=params(),
        name="factor_terms",
    )(own, other, g, e)


def pack_kernel(keep_ref, got_ref, gram_ref, out_ref):
    count, chunk = out_ref.shape[0], out_ref.shape[1]
    strip = RANK // lax.axis_size("y")
    piece = chunk - strip
    gram_rows = gram_ref[pl.ds(pl.multiple_of(lax.axis_index("y") * strip, strip), strip), :]
    for i in range(count):
        rows = pl.ds(i * piece, piece)
        out_ref[i, :piece] = keep_ref[rows, :] + got_ref[rows, :]
        out_ref[i, piece:] = gram_rows


def pack(keep, got, gram, count, strip):
    piece = keep.shape[0] // count
    return pl.pallas_call(
        pack_kernel,
        out_shape=jax.ShapeDtypeStruct((count, piece + strip, RANK), F32),
        compiler_params=params(),
        name="pack",
    )(keep, got, gram)


def gather_gram(parts_ref, gram_ref):
    strips, columns = lax.axis_size("y"), lax.axis_size("fsdp")
    strip = RANK // strips
    piece = parts_ref.shape[1] - strip
    for i in range(strips):
        total = parts_ref[i * columns, piece:]
        for k in range(1, columns):
            total = total + parts_ref[i * columns + k, piece:]
        gram_ref[i * strip : (i + 1) * strip, :] = total


def across(tile, lane):
    return jnp.broadcast_to(tile[:, lane : lane + 1], tile.shape)


def down(tile, row):
    return jnp.broadcast_to(tile[row : row + 1, :], tile.shape)


def invert_cholesky(a_ref, b_ref, out_ref):
    tiles = RANK // 8
    lane = lax.broadcasted_iota(jnp.int32, (8, RANK), 1)
    row = lax.broadcasted_iota(jnp.int32, (8, RANK), 0)
    for t in range(tiles):
        b_ref[8 * t : 8 * t + 8, :] = jnp.where(lane == row + 8 * t, 1.0, 0.0)
    for t in range(tiles):
        here = slice(8 * t, 8 * t + 8)
        a_tile, b_tile = a_ref[here, :], b_ref[here, :]
        columns = [across(a_tile, 8 * t + k) for k in range(8)]
        value = {(i, k): down(columns[k], i) for k in range(8) for i in range(k, 8)}
        factor, inverse, root = {}, [], []
        for k in range(8):
            inverse.append(1.0 / value[k, k])
            root.append(lax.rsqrt(value[k, k]))
            for i in range(k + 1, 8):
                factor[i, k] = value[i, k] * inverse[k]
            for j in range(k + 1, 8):
                for i in range(j, 8):
                    value[i, j] = value[i, j] - factor[j, k] * value[i, k]
        a_rows = [down(a_tile, k) for k in range(8)]
        b_rows = [down(b_tile, k) for k in range(8)]
        for k in range(8):
            for i in range(k + 1, 8):
                a_rows[i] = a_rows[i] - factor[i, k] * a_rows[k]
                b_rows[i] = b_rows[i] - factor[i, k] * b_rows[k]
        for k in range(8):
            out_ref[8 * t + k : 8 * t + k + 1, :] = (b_rows[k] * root[k])[:1, :]
        for u in range(t + 1, tiles):
            there = slice(8 * u, 8 * u + 8)
            a_low, b_low = a_ref[there, :], b_ref[there, :]
            left = [across(a_low, 8 * t + k) for k in range(8)]
            for k in range(8):
                for i in range(k + 1, 8):
                    left[i] = left[i] - factor[i, k] * left[k]
                scaled = left[k] * inverse[k]
                a_low = a_low - scaled * a_rows[k]
                b_low = b_low - scaled * b_rows[k]
            a_ref[there, :] = a_low
            b_ref[there, :] = b_low


def first_pass_kernel(parts_ref, sketch_ref, basis_ref, inv_ref, out_ref, a_ref, b_ref, gram_ref):
    strip = RANK // lax.axis_size("y")
    count, chunk = parts_ref.shape[0], parts_ref.shape[1]
    piece = chunk - strip
    gather_gram(parts_ref, a_ref)
    invert_cholesky(a_ref, b_ref, inv_ref)
    basis = mm32(sketch_ref[...], inv_ref[...], NT)
    basis_ref[...] = basis
    gram_ref[...] = mm32(basis, basis, TN)
    total = parts_ref[0, :piece]
    for i in range(1, count):
        total = total + parts_ref[i, :piece]
    gram_rows = gram_ref[pl.ds(pl.multiple_of(lax.axis_index("y") * strip, strip), strip), :]
    for i in range(count):
        out_ref[i, :piece] = total
        out_ref[i, piece:] = gram_rows


def first_pass(parts, sketch):
    square = jax.ShapeDtypeStruct((RANK, RANK), F32)
    return pl.pallas_call(
        first_pass_kernel,
        out_shape=[
            jax.ShapeDtypeStruct(sketch.shape, F32),
            square,
            jax.ShapeDtypeStruct(parts.shape, F32),
        ],
        scratch_shapes=[pltpu.VMEM((RANK, RANK), F32)] * 3,
        compiler_params=params(),
        name="first_pass",
    )(parts, sketch)


def second_pass_kernel(parts_ref, basis_one_ref, inv_one_ref, basis_ref, inv_ref, a_ref, b_ref, two_ref):
    gather_gram(parts_ref, a_ref)
    invert_cholesky(a_ref, b_ref, two_ref)
    basis_ref[...] = mm32(basis_one_ref[...], two_ref[...], NT)
    inv_ref[...] = mm32(two_ref[...], inv_one_ref[...])


def second_pass(parts, basis_one, inv_one):
    return pl.pallas_call(
        second_pass_kernel,
        out_shape=[
            jax.ShapeDtypeStruct(basis_one.shape, F32),
            jax.ShapeDtypeStruct(inv_one.shape, F32),
        ],
        scratch_shapes=[pltpu.VMEM((RANK, RANK), F32)] * 3,
        compiler_params=params(),
        name="second_pass",
    )(parts, basis_one, inv_one)


def residue_kernel(replicas, own_ref, other_ref, basis_ref, inv_ref, g_ref, e_ref, right_ref, new_ref, halves, q12):
    step = pl.program_id(0)

    @pl.when(step == 0)
    def _():
        core = lax.axis_index("core")
        strip = RANK // lax.axis_size("y")
        count, chunk = own_ref.shape[0], own_ref.shape[1]
        piece = chunk - strip
        for i in range(count):
            halves[core, i * piece : (i + 1) * piece, :] = own_ref[i, :piece]
            halves[1 - core, i * piece : (i + 1) * piece, :] = other_ref[i, :piece]
        basis = basis_ref[...]
        hi = basis.astype(BF16)
        q12[:, :RANK] = hi
        q12[:, RANK:] = (basis - hi.astype(F32)).astype(BF16)

    rows = pl.ds(pl.multiple_of(step * RANK, RANK), RANK)
    raw = jnp.concatenate([halves[0, rows, :], halves[1, rows, :]], axis=0)
    right = mm32(raw, inv_ref[...], NT) * (1.0 / replicas)
    right_ref[...] = right
    hi = right.astype(BF16)
    low = (right - hi.astype(F32)).astype(BF16)
    update = mm(q12[...], jnp.concatenate([hi, hi], axis=1), NT) + mm(q12[:, :RANK], low, NT)
    new_ref[...] = (g_ref[...].astype(F32) + e_ref[...].astype(F32) - update).astype(BF16)


def residue(own, other, basis, inv, g, e, replicas):
    n, m = g.shape
    parts = pl.BlockSpec(own.shape, lambda j: (0, 0, 0))
    block = pl.BlockSpec((n, COLS), lambda j: (0, j))
    return pl.pallas_call(
        functools.partial(residue_kernel, replicas),
        grid=(m // COLS,),
        in_specs=[
            parts,
            parts,
            pl.BlockSpec((n, RANK), lambda j: (0, 0)),
            pl.BlockSpec((RANK, RANK), lambda j: (0, 0)),
            block,
            block,
        ],
        out_specs=[pl.BlockSpec((COLS, RANK), lambda j: (j, 0)), block],
        out_shape=[jax.ShapeDtypeStruct((m, RANK), F32), jax.ShapeDtypeStruct((n, m), BF16)],
        scratch_shapes=[
            pltpu.VMEM((2, m // 2, RANK), F32),
            pltpu.VMEM((n, 2 * RANK), BF16),
        ],
        compiler_params=params(),
        name="residue",
    )(own, other, basis, inv, g, e)


def swap(x):
    return lax.ppermute(x, "core", [(0, 1), (1, 0)])


def shards(gradients, errors, start_factor):
    g, e = gradients[0], errors[0]
    n = g.shape[0]
    ny, nx, nz = lax.axis_size("y"), lax.axis_size("fsdp"), lax.axis_size("tensor")
    keep, send = local_sketch(g, e, start_factor)
    pieces = (keep + swap(send)).reshape(ny * nz, -1, RANK)
    pieces = lax.all_to_all(pieces, ("y", "tensor"), 0, 0)
    own = lax.all_to_all(total_for_all(pieces), ("y", "tensor"), 0, 0).reshape(n // 2, RANK)
    sketch, keep, send, gram = factor_terms(own, swap(own), g, e)
    parts = pack(keep, swap(send), gram, ny * nx, RANK // ny)
    parts = lax.all_to_all(parts, ("y", "fsdp"), 0, 0)
    basis_one, inv_one, parts = first_pass(parts, sketch)
    parts = lax.all_to_all(parts, ("y", "fsdp"), 0, 0)
    other = swap(parts)
    basis, inv = second_pass(parts, basis_one, inv_one)
    right_factor, new_errors = residue(parts, other, basis, inv, g, e, 2 * ny)
    return (right_factor, new_errors[None])


def solution(mesh):
    shape = mesh.devices.shape
    split = Mesh(
        mesh.devices.reshape(shape[0] // 2, 2, *shape[1:]), ("y", "core", "fsdp", "tensor")
    )
    big = P(("y", "core"), "fsdp", "tensor")
    return jax.shard_map(
        shards,
        mesh=split,
        in_specs=(big, big, P("tensor", None)),
        out_specs=(P("tensor", None), big),
        check_vma=False,
    )
```

time: 496 us -> 118 us (0.24)
  waiting for transfers between devices: 389 us -> 3.78 us
  blocking collectives: 0 us -> 68.4 us
  other arithmetic: 48.7 us -> 0.03 us
  matrix products: 40.6 us -> 0 us
  Pallas kernels: 0 us -> 29.4 us
  between operations: 13.9 us -> 0.7 us
  starting transfers between devices: 0.34 us -> 9.84 us
    psum x4 -> x0, waiting for transfers between devices: 389 us -> none  [the longest x1 183 us: shards(): basis_cols = lax.psum(local_sketch, ('dp', 'tensor'))]
    all_to_all x0 -> x4, blocking collectives: none -> 68.4 us  [the longest x2 33.3 us: shards(): parts = lax.all_to_all(parts, ('y', 'fsdp'), 0, 0)]
    another operation x10 -> x0, other arithmetic: 45.7 us -> none  [the longest x6 24.8 us: cholesky_pass(): lower_factor = jnp.linalg.cholesky(gram_matrix)]
    dot_general x5 -> x0, matrix products: 38.3 us -> none  [the longest x1 14.8 us: shards(): lax.dot_general(merged, basis_cols, (((0,), (0,)), ((), ())), precision=l...]
    pallas_call x0 -> x7, Pallas kernels: none -> 29.4 us  [the longest x1 7.73 us: residue(): pl.pallas_call(functools.partial(residue_kernel, replicas), grid=(m // CO...]
    ppermute x0 -> x4, starting transfers between devices: none -> 9.84 us  [swap(): return lax.ppermute(x, 'core', [(0, 1), (1, 0)])]
  transfers between devices with their start and end apart: 4 -> 4, of which waited for: 4 -> 3; matrix products, arithmetic and copies ran while one was open for 0% -> 0% of each run, Pallas kernels for 0% -> 5%
where the time goes in v1:
time: 118 us; the launch traced here: 117 us
  blocking collectives  68.4 us (58%)
  Pallas kernels  29.4 us (25%)
  starting transfers between devices  9.84 us (8%)
  local copies, waits for them, and re-layouts  5.25 us (4%)
  waiting for transfers between devices  3.78 us (3%)
    all_to_all x2, blocking collectives, shards(): parts = lax.all_to_all(parts, ('y', 'fsdp'), 0, 0)  33.3 us
    all_to_all x1, blocking collectives, shards(): pieces = lax.all_to_all(pieces, ('y', 'tensor'), 0, 0)  18.9 us
    all_to_all x1, blocking collectives, shards(): lax.all_to_all(total_for_all(pieces), ('y', 'tensor'), 0, 0)  16.2 us
    ppermute x4, starting transfers between devices, swap(): return lax.ppermute(x, 'core', [(0, 1), (1, 0)])  9.84 us
    pallas_call x1, Pallas kernels, residue(): pl.pallas_call(functools.partial(residue_kernel, replicas), grid=(m // CO...  7.73 us
    pallas_call x1, Pallas kernels, first_pass(): pl.pallas_call(first_pass_kernel, out_shape=[jax.ShapeDtypeStruct(sketch....  6.74 us
    pallas_call x1, Pallas kernels, factor_terms(): pl.pallas_call(factor_kernel, grid=(m // COLS,), in_specs=[half, half, bl...  5.46 us
    pallas_call x1, Pallas kernels, second_pass(): pl.pallas_call(second_pass_kernel, out_shape=[jax.ShapeDtypeStruct(basis_...  5.42 us
  transfers between devices with their start and end apart: 4, of which 3 were waited for; matrix products, arithmetic and copies ran while one was open for 0% of the time, Pallas kernels for 5%

profile of v1, /device:TPU:1, one launch (start us, length us, event | category | flops | bytes accessed | tf_op | source)
XLA Modules:
  0.0 117.4 jit_solution(9274859173980846674)
XLA Ops:
  0.6 0.0 copy-start
  0.6 2.0 %copy-done = bf16[1,1024,1792]{2,1,0:T(8,128)(2,1)S(1)} copy-done((bf16[1,1024,1792]{2,1,0:T(8,128)(2,1)S(1)}, bf16[1,1024,1792]{2,1,0:T(8,128)(2,1)}, u32[]{:S(2)}) %copy-start) | copy-done | bytes 3670040
  2.7 0.0 copy-start.2
  2.7 2.0 %copy-done.2 = bf16[1,1024,1792]{2,1,0:T(8,128)(2,1)S(1)} copy-done((bf16[1,1024,1792]{2,1,0:T(8,128)(2,1)S(1)}, bf16[1,1024,1792]{2,1,0:T(8,128)(2,1)}, u32[]{:S(2)}) %copy-start.2) | copy-done | bytes 3670040
  4.7 0.0 copy-start.3
  4.7 1.2 %copy-done.3 = f32[1792,128]{1,0:T(8,128)S(1)} copy-done((f32[1792,128]{1,0:T(8,128)S(1)}, f32[1792,128]{1,0:T(8,128)}, u32[]{:S(2)}) %copy-start.3) | copy-done | bytes 917528
  5.9 0.0 copy-start.1
  5.9 3.9 %local_sketch.1 = (f32[512,128]{1,0:T(8,128)S(1)}, f32[512,128]{1,0:T(8,128)S(1)}) custom-call(bf16[1024,1792]{1,0:T(8,128)(2,1)S(1)} %bitcast.5, bf16[1024,1792]{1,0:T(8,128)(2,1)S(1)} %bitcast.8, f32[1792,128]{1,0:T(8,128)S(1)} %copy-done.3), custom_call_target="tpu_custom_call" | custom-call | tf_op jit(solution)/shard_map/local_sketch/pallas_call | solution.py:71
  9.8 3.3 %collective-permute-start = (f32[512,128]{1,0:T(8,128)S(1)}, f32[512,128]{1,0:T(8,128)S(1)}, u32[]{:S(2)}, u32[]{:S(2)}) collective-permute-start(f32[512,128]{1,0:T(8,128)S(1)} %get-tuple-element.16), channel_id=1, source_target_pairs={{0,32},{32,0},{1,33},{33,1},{2,34},{34,2},{3,35},{35,3},{4,36},{36... | collective-permute-start | bytes 786440 | tf_op jit(solution)/shard_map/ppermute | solution.py:352
  13.1 1.2 collective-permute-done
  14.3 18.9 %all_to_all.20.parts_ref = f32[32,16,128]{2,1,0:T(8,128)S(1)} all-to-all(f32[32,16,128]{2,1,0:T(8,128)S(1)} %bitcast.13), channel_id=1, replica_groups=mesh['y'=4,'core'=2,'fsdp'=4,'tensor'=8] {'y','tensor'}, dimensions={0} | all-to-all | bytes 524288 | tf_op jit(solution)/shard_map/all_to_all | solution.py:361
  33.3 0.1 sketch_total.1
  33.3 16.2 %all_to_all.21 = f32[32,16,128]{2,1,0:T(8,128)S(1)} all-to-all(f32[32,16,128]{2,1,0:T(8,128)S(1)} %sketch_total.1), channel_id=1, replica_groups=mesh['y'=4,'core'=2,'fsdp'=4,'tensor'=8] {'y','tensor'}, dimensions={0} | all-to-all | bytes 524288 | tf_op jit(solution)/shard_map/all_to_all | solution.py:362
  49.5 3.6 %collective-permute-start.1 = (f32[512,128]{1,0:T(8,128)S(1)}, f32[512,128]{1,0:T(8,128)S(1)}, u32[]{:S(2)}, u32[]{:S(2)}) collective-permute-start(f32[512,128]{1,0:T(8,128)S(1)} %bitcast.11), channel_id=1, source_target_pairs={{0,32},{32,0},{1,33},{33,1},{2,34},{34,2},{3,35},{35,3},{4,36},{36... | collective-permute-start | bytes 786440 | tf_op jit(solution)/shard_map/ppermute | solution.py:352
  53.1 1.2 collective-permute-done.1.other_ref
  54.3 0.0 copy-done.1
  54.3 5.5 %factor_terms.1 = (f32[1024,128]{1,0:T(8,128)S(1)}, f32[896,128]{1,0:T(8,128)S(1)}, f32[896,128]{1,0:T(8,128)S(1)}, f32[128,128]{1,0:T(8,128)S(1)}) custom-call(f32[512,128]{1,0:T(8,128)S(1)} %bitcast.12, f32[512,128]{1,0:T(8,128)S(1)} %collective-permute-done.1.other_ref, bf16[1024,1792]{1,0:T(8,128)(2,1)S(1)} %bitcast.6, bf16[1024,1792]{1,0:T(8,128)(2,1)S(1)} %bitcast.9), custom_call_target="tpu_custom_call" | custom-call | tf_op jit(solution)/shard_map/factor_terms/pallas_call | solution.py:137
  59.7 0.5 collective-permute-start.2
  60.2 1.5 %collective-permute-done.2.got_ref = f32[896,128]{1,0:T(8,128)S(1)} collective-permute-done((f32[896,128]{1,0:T(8,128)S(1)}, f32[896,128]{1,0:T(8,128)S(1)}, u32[]{:S(2)}, u32[]{:S(2)}) %collective-permute-start.2) | collective-permute-done | bytes 458784 | tf_op jit(solution)/shard_map/ppermute | solution.py:352
  61.6 0.1 pack.1
  61.7 18.0 %all_to_all.22.parts_ref = f32[16,88,128]{2,1,0:T(8,128)S(1)} all-to-all(f32[16,88,128]{2,1,0:T(8,128)S(1)} %pack.1), channel_id=1, replica_groups=mesh['y'=4,'core'=2,'fsdp'=4,'tensor'=8] {'y','fsdp'}, dimensions={0} | all-to-all | bytes 1441792 | tf_op jit(solution)/shard_map/all_to_all | solution.py:365
  79.7 6.7 %first_pass.1 = (f32[1024,128]{1,0:T(8,128)S(1)}, f32[128,128]{1,0:T(8,128)S(1)}, f32[16,88,128]{2,1,0:T(8,128)S(1)}) custom-call(f32[16,88,128]{2,1,0:T(8,128)S(1)} %all_to_all.22.parts_ref, f32[1024,128]{1,0:T(8,128)S(1)} %get-tuple-element.20.sketch_ref), custom_call_target="tpu_custom_call" | custom-call | tf_op jit(solution)/shard_map/first_pass/pallas_call | solution.py:265
  86.4 15.3 %all_to_all.23.parts_ref.own_ref = f32[16,88,128]{2,1,0:T(8,128)S(1)} all-to-all(f32[16,88,128]{2,1,0:T(8,128)S(1)} %get-tuple-element.21), channel_id=1, replica_groups=mesh['y'=4,'core'=2,'fsdp'=4,'tensor'=8] {'y','fsdp'}, dimensions={0} | all-to-all | bytes 1441792 | tf_op jit(solution)/shard_map/all_to_all | solution.py:367
  101.7 2.5 %collective-permute-start.3 = (f32[16,88,128]{2,1,0:T(8,128)S(1)}, f32[16,88,128]{2,1,0:T(8,128)S(1)}, u32[]{:S(2)}, u32[]{:S(2)}) collective-permute-start(f32[16,88,128]{2,1,0:T(8,128)S(1)} %all_to_all.23.parts_ref.own_ref), channel_id=1, source_target_pairs={{0,32},{32,0},{1,33},{33,1},{2,34},{34,2},{3,35},{35,3},{4,36},{36... | collective-permute-start | bytes 2162696 | tf_op jit(solution)/shard_map/ppermute | solution.py:352
  104.2 5.4 %second_pass.1 = (f32[1024,128]{1,0:T(8,128)S(1)}, f32[128,128]{1,0:T(8,128)S(1)}) custom-call(f32[16,88,128]{2,1,0:T(8,128)S(1)} %all_to_all.23.parts_ref.own_ref, f32[1024,128]{1,0:T(8,128)S(1)} %get-tuple-element.22.basis_one_ref, f32[128,128]{1,0:T(8,128)S(1)} %get-tuple-element.23.inv_one_ref), custom_call_target="tpu_custom_call" | custom-call | tf_op jit(solution)/shard_map/second_pass/pallas_call | solution.py:286
  109.6 0.0 collective-permute-done.3.other_ref
  109.6 7.7 %residue.1 = (f32[1792,128]{1,0:T(8,128)}, bf16[1024,1792]{1,0:T(8,128)(2,1)}) custom-call(f32[16,88,128]{2,1,0:T(8,128)S(1)} %all_to_all.23.parts_ref.own_ref, f32[16,88,128]{2,1,0:T(8,128)S(1)} %collective-permute-done.3.other_ref, f32[1024,128]{1,0:T(8,128)S(1)} %get-tuple-element.24.basis_ref, f32[128,128]{1,0:T(8,128)S(1)} %get-tuple-element.25.inv_ref, ...), custom_call_target="tpu_custom_call" | custom-call | tf_op jit(solution)/shard_map/residue/pallas_call | solution.py:329
  (1 shorter events, 0.0 us)
Async XLA Ops:
  0.6 2.0 %copy-start = (bf16[1,1024,1792]{2,1,0:T(8,128)(2,1)S(1)}, bf16[1,1024,1792]{2,1,0:T(8,128)(2,1)}, u32[]{:S(2)}) copy-start(bf16[1,1024,1792]{2,1,0:T(8,128)(2,1)} %param.3) | copy-start | bytes 11010052
  2.7 2.0 %copy-start.2 = (bf16[1,1024,1792]{2,1,0:T(8,128)(2,1)S(1)}, bf16[1,1024,1792]{2,1,0:T(8,128)(2,1)}, u32[]{:S(2)}) copy-start(bf16[1,1024,1792]{2,1,0:T(8,128)(2,1)} %param.4) | copy-start | bytes 11010052
  4.7 1.2 %copy-start.3 = (f32[1792,128]{1,0:T(8,128)S(1)}, f32[1792,128]{1,0:T(8,128)}, u32[]{:S(2)}) copy-start(f32[1792,128]{1,0:T(8,128)} %p_ref.1) | copy-start | bytes 2752516
  5.9 48.4 %copy-start.1 = (bf16[1,1024,1792]{2,1,0:T(8,128)(2,1)S(1)}, bf16[1,1024,1792]{2,1,0:T(8,128)(2,1)}, u32[]{:S(2)}) copy-start(bf16[1,1024,1792]{2,1,0:T(8,128)(2,1)} %param.3) | copy-start | bytes 11010052
  9.8 4.5 %collective-permute-start = (f32[512,128]{1,0:T(8,128)S(1)}, f32[512,128]{1,0:T(8,128)S(1)}, u32[]{:S(2)}, u32[]{:S(2)}) collective-permute-start(f32[512,128]{1,0:T(8,128)S(1)} %get-tuple-element.16), channel_id=1, source_target_pairs={{0,32},{32,0},{1,33},{33,1},{2,34},{34,2},{3,35},{35,3},{4,36},{36... | collective-permute-start | bytes 786440 | tf_op jit(solution)/shard_map/ppermute | solution.py:352
  49.5 4.8 %collective-permute-start.1 = (f32[512,128]{1,0:T(8,128)S(1)}, f32[512,128]{1,0:T(8,128)S(1)}, u32[]{:S(2)}, u32[]{:S(2)}) collective-permute-start(f32[512,128]{1,0:T(8,128)S(1)} %bitcast.11), channel_id=1, source_target_pairs={{0,32},{32,0},{1,33},{33,1},{2,34},{34,2},{3,35},{35,3},{4,36},{36... | collective-permute-start | bytes 786440 | tf_op jit(solution)/shard_map/ppermute | solution.py:352
  59.7 1.9 %collective-permute-start.2 = (f32[896,128]{1,0:T(8,128)S(1)}, f32[896,128]{1,0:T(8,128)S(1)}, u32[]{:S(2)}, u32[]{:S(2)}) collective-permute-start(f32[896,128]{1,0:T(8,128)S(1)} %get-tuple-element.18), channel_id=1, source_target_pairs={{0,32},{32,0},{1,33},{33,1},{2,34},{34,2},{3,35},{35,3},{4,36},{36... | collective-permute-start | bytes 1376264 | tf_op jit(solution)/shard_map/ppermute | solution.py:352
  101.7 7.9 %collective-permute-start.3 = (f32[16,88,128]{2,1,0:T(8,128)S(1)}, f32[16,88,128]{2,1,0:T(8,128)S(1)}, u32[]{:S(2)}, u32[]{:S(2)}) collective-permute-start(f32[16,88,128]{2,1,0:T(8,128)S(1)} %all_to_all.23.parts_ref.own_ref), channel_id=1, source_target_pairs={{0,32},{32,0},{1,33},{33,1},{2,34},{34,2},{3,35},{35,3},{4,36},{36... | collective-permute-start | bytes 2162696 | tf_op jit(solution)/shard_map/ppermute | solution.py:352

commit v2 on v1

--- a/solution.py
+++ b/solution.py
@@ -11,7 +11,8 @@
 RANK = 128
 ROWS = 256
 COLS = 256
-VMEM_LIMIT = 40 * 1024 * 1024
+VMEM_LIMIT = 24 * 1024 * 1024
+STREAM_LIMIT = 55500000
 NT = (((1,), (1,)), ((), ()))
 NN = (((1,), (0,)), ((), ()))
 TN = (((0,), (0,)), ((), ()))
@@ -33,53 +34,72 @@
     return hi, mid, low
 
 
-def params():
-    return pltpu.CompilerParams(vmem_limit_bytes=VMEM_LIMIT)
-
-
-def sketch_kernel(g_ref, e_ref, p_ref, keep_ref, send_ref, p12, p3):
-    step = pl.program_id(0)
-    half_steps = pl.num_programs(0) // 2
-
-    @pl.when(step == 0)
-    def _():
-        hi, mid, low = split3(p_ref[...])
-        p12[:, :RANK] = hi
-        p12[:, RANK:] = mid
-        p3[...] = low
-
-    g, e = g_ref[...], e_ref[...]
-    both = mm(g, p12[...]) + mm(e, p12[...])
-    block = both[:, :RANK] + both[:, RANK:] + mm(g + e, p3[...])
-    mine = step // half_steps == lax.axis_index("core")
-    rows = pl.ds(pl.multiple_of(lax.rem(step, half_steps) * ROWS, ROWS), ROWS)
-
-    @pl.when(mine)
-    def _():
-        keep_ref[rows, :] = block
-
-    @pl.when(jnp.logical_not(mine))
-    def _():
-        send_ref[rows, :] = block
+def params(limit=VMEM_LIMIT):
+    return pltpu.CompilerParams(vmem_limit_bytes=limit)
+
+
+def sketch_kernel(g_hbm, e_hbm, p_hbm, keep_ref, send_ref, g_ref, e_ref, p_ref, p12, p3, sems):
+    n = g_ref.shape[0]
+    steps, ahead = n // ROWS, 2
+    core = lax.axis_index("core")
+
+    def load(i):
+        rows = pl.ds(i * ROWS, ROWS)
+        return (
+            pltpu.make_async_copy(g_hbm.at[rows], g_ref.at[rows], sems.at[2 * i]),
+            pltpu.make_async_copy(e_hbm.at[rows], e_ref.at[rows], sems.at[2 * i + 1]),
+        )
+
+    first = pltpu.make_async_copy(p_hbm, p_ref, sems.at[2 * steps])
+    first.start()
+    copies = [load(i) for i in range(steps)]
+    for i in range(ahead):
+        copies[i][0].start()
+        copies[i][1].start()
+    first.wait()
+    hi, mid, low = split3(p_ref[...])
+    p12[:, :RANK] = hi
+    p12[:, RANK:] = mid
+    p3[...] = low
+    for i in range(steps):
+        copies[i][0].wait()
+        copies[i][1].wait()
+        if i + ahead < steps:
+            copies[i + ahead][0].start()
+            copies[i + ahead][1].start()
+        rows = pl.ds(i * ROWS, ROWS)
+        g, e = g_ref[rows, :], e_ref[rows, :]
+        both = mm(g, p12[...]) + mm(e, p12[...])
+        block = both[:, :RANK] + both[:, RANK:] + mm(g + e, p3[...])
+        half = i // (steps // 2)
+        place = pl.ds((i - half * (steps // 2)) * ROWS, ROWS)
+
+        @pl.when(core == half)
+        def _():
+            keep_ref[place, :] = block
+
+        @pl.when(core != half)
+        def _():
+            send_ref[place, :] = block
 
 
 def local_sketch(g, e, p):
     n, m = g.shape
-    whole = pl.BlockSpec((n // 2, RANK), lambda i: (0, 0))
-    out = jax.ShapeDtypeStruct((n // 2, RANK), F32)
-    rows = min(ROWS, n // 2)
+    half = jax.ShapeDtypeStruct((n // 2, RANK), F32)
     return pl.pallas_call(
         sketch_kernel,
-        grid=(n // rows,),
-        in_specs=[
-            pl.BlockSpec((rows, m), lambda i: (i, 0)),
-            pl.BlockSpec((rows, m), lambda i: (i, 0)),
-            pl.BlockSpec((m, RANK), lambda i: (0, 0)),
+        in_specs=[pl.BlockSpec(memory_space=pltpu.HBM)] * 3,
+        out_specs=[pl.BlockSpec(memory_space=pltpu.VMEM)] * 2,
+        out_shape=[half, half],
+        scratch_shapes=[
+            pltpu.VMEM((n, m), BF16),
+            pltpu.VMEM((n, m), BF16),
+            pltpu.VMEM((m, RANK), F32),
+            pltpu.VMEM((m, 2 * RANK), BF16),
+            pltpu.VMEM((m, RANK), BF16),
+            pltpu.SemaphoreType.DMA((2 * (n // ROWS) + 1,)),
         ],
-        out_specs=[whole, whole],
-        out_shape=[out, out],
-        scratch_shapes=[pltpu.VMEM((m, 2 * RANK), BF16), pltpu.VMEM((m, RANK), BF16)],
-        compiler_params=params(),
+        compiler_params=params(STREAM_LIMIT),
         name="local_sketch",
     )(g, e, p)
 
@@ -97,67 +117,68 @@
         total_kernel,
         out_shape=jax.ShapeDtypeStruct(parts.shape, F32),
         compiler_params=params(),
+        cost_estimate=pl.CostEstimate(flops=2 * 10**10, bytes_accessed=5 * 10**7, transcendentals=0),
         name="sketch_total",
     )(parts)
 
 
-def factor_kernel(own_ref, other_ref, g_ref, e_ref, sketch_ref, keep_ref, send_ref, gram_ref, s12, s3, turned):
+def factor_block(s12, s3, g_ref, e_ref, out_ref, side):
+    width = out_ref.shape[0]
+    for start in range(0, width, COLS):
+        size = min(COLS, width - start)
+        cols = pl.ds(pl.multiple_of(side * width + start, RANK), size)
+        g, e = g_ref[:, cols], e_ref[:, cols]
+        both = mm(s12, g) + mm(s12, e)
+        out_ref[start : start + size, :] = (both[:RANK] + both[RANK:] + mm(s3, g + e)).T
+
+
+def factor_send_kernel(own_ref, other_ref, g_ref, e_ref, sketch_ref, s12_ref, s3_ref, gram_ref, send_ref):
     core = lax.axis_index("core")
-
-    @pl.when(pl.program_id(0) == 0)
-    def _():
-        half = own_ref.shape[0]
-        sketch_ref[pl.ds(pl.multiple_of(core * half, half), half), :] = own_ref[...]
-        sketch_ref[pl.ds(pl.multiple_of((1 - core) * half, half), half), :] = other_ref[...]
-        hi, mid, low = split3(sketch_ref[...].T)
-        s12[:RANK, :] = hi
-        s12[RANK:, :] = mid
-        s3[...] = low
-        square = mm(s12[...], s12[...], NT)
-        cross = mm(s12[:RANK, :], s3[...], NT)
-        gram_ref[...] = (
-            square[:RANK, :RANK] + square[RANK:, RANK:]
-            + (square[:RANK, RANK:] + square[RANK:, :RANK])
-            + (cross + cross.T)
-        )
-
-    g, e = g_ref[...], e_ref[...]
-    both = mm(s12[...], g) + mm(s12[...], e)
-    block = both[:RANK] + both[RANK:] + mm(s3[...], g + e)
-    turned[...] = block.T
-    keep_ref[...] = turned[pl.ds(pl.multiple_of(core * RANK, RANK), RANK), :]
-    send_ref[...] = turned[pl.ds(pl.multiple_of((1 - core) * RANK, RANK), RANK), :]
-
-
-def factor_terms(own, other, g, e):
+    half = own_ref.shape[0]
+    sketch_ref[pl.ds(pl.multiple_of(core * half, half), half), :] = own_ref[...]
+    sketch_ref[pl.ds(pl.multiple_of((1 - core) * half, half), half), :] = other_ref[...]
+    hi, mid, low = split3(sketch_ref[...].T)
+    s12_ref[:RANK, :] = hi
+    s12_ref[RANK:, :] = mid
+    s3_ref[...] = low
+    square = mm(s12_ref[...], s12_ref[...], NT)
+    cross = mm(hi, low, NT)
+    gram_ref[...] = (
+        square[:RANK, :RANK] + square[RANK:, RANK:]
+        + (square[:RANK, RANK:] + square[RANK:, :RANK])
+        + (cross + cross.T)
+    )
+    factor_block(s12_ref[...], s3_ref[...], g_ref, e_ref, send_ref, 1 - core)
+
+
+def factor_keep_kernel(s12_ref, s3_ref, g_ref, e_ref, keep_ref):
+    factor_block(s12_ref[...], s3_ref[...], g_ref, e_ref, keep_ref, lax.axis_index("core"))
+
+
+def factor_send(own, other, g, e):
     n, m = g.shape
-    half = pl.BlockSpec((n // 2, RANK), lambda j: (0, 0))
-    block = pl.BlockSpec((n, COLS), lambda j: (0, j))
-    rows = pl.BlockSpec((RANK, RANK), lambda j: (j, 0))
-    return pl.pallas_call(
-        factor_kernel,
-        grid=(m // COLS,),
-        in_specs=[half, half, block, block],
-        out_specs=[
-            pl.BlockSpec((n, RANK), lambda j: (0, 0)),
-            rows,
-            rows,
-            pl.BlockSpec((RANK, RANK), lambda j: (0, 0)),
-        ],
+    return pl.pallas_call(
+        factor_send_kernel,
         out_shape=[
             jax.ShapeDtypeStruct((n, RANK), F32),
+            jax.ShapeDtypeStruct((2 * RANK, n), BF16),
+            jax.ShapeDtypeStruct((RANK, n), BF16),
+            jax.ShapeDtypeStruct((RANK, RANK), F32),
             jax.ShapeDtypeStruct((m // 2, RANK), F32),
-            jax.ShapeDtypeStruct((m // 2, RANK), F32),
-            jax.ShapeDtypeStruct((RANK, RANK), F32),
         ],
-        scratch_shapes=[
-            pltpu.VMEM((2 * RANK, n), BF16),
-            pltpu.VMEM((RANK, n), BF16),
-            pltpu.VMEM((COLS, RANK), F32),
-        ],
-        compiler_params=params(),
-        name="factor_terms",
+        compiler_params=params(),
+        name="factor_send",
     )(own, other, g, e)
+
+
+def factor_keep(s12, s3, g, e):
+    return pl.pallas_call(
+        factor_keep_kernel,
+        out_shape=jax.ShapeDtypeStruct((g.shape[1] // 2, RANK), F32),
+        compiler_params=params(),
+        cost_estimate=pl.CostEstimate(flops=10**9, bytes_accessed=8 * 10**6, transcendentals=0),
+        name="factor_keep",
+    )(s12, s3, g, e)
 
 
 def pack_kernel(keep_ref, got_ref, gram_ref, out_ref):
@@ -295,53 +316,50 @@
     )(parts, basis_one, inv_one)
 
 
-def residue_kernel(replicas, own_ref, other_ref, basis_ref, inv_ref, g_ref, e_ref, right_ref, new_ref, halves, q12):
-    step = pl.program_id(0)
-
-    @pl.when(step == 0)
-    def _():
-        core = lax.axis_index("core")
-        strip = RANK // lax.axis_size("y")
-        count, chunk = own_ref.shape[0], own_ref.shape[1]
-        piece = chunk - strip
-        for i in range(count):
-            halves[core, i * piece : (i + 1) * piece, :] = own_ref[i, :piece]
-            halves[1 - core, i * piece : (i + 1) * piece, :] = other_ref[i, :piece]
-        basis = basis_ref[...]
-        hi = basis.astype(BF16)
-        q12[:, :RANK] = hi
-        q12[:, RANK:] = (basis - hi.astype(F32)).astype(BF16)
-
-    rows = pl.ds(pl.multiple_of(step * RANK, RANK), RANK)
-    raw = jnp.concatenate([halves[0, rows, :], halves[1, rows, :]], axis=0)
-    right = mm32(raw, inv_ref[...], NT) * (1.0 / replicas)
-    right_ref[...] = right
-    hi = right.astype(BF16)
-    low = (right - hi.astype(F32)).astype(BF16)
-    update = mm(q12[...], jnp.concatenate([hi, hi], axis=1), NT) + mm(q12[:, :RANK], low, NT)
-    new_ref[...] = (g_ref[...].astype(F32) + e_ref[...].astype(F32) - update).astype(BF16)
+def residue_kernel(replicas, own_ref, other_ref, basis_ref, inv_ref, g_ref, e_ref, right_hbm, new_hbm, halves, q12, right_ref, new_ref, sems):
+    core = lax.axis_index("core")
+    strip = RANK // lax.axis_size("y")
+    count, chunk = own_ref.shape[0], own_ref.shape[1]
+    piece = chunk - strip
+    m = g_ref.shape[1]
+    for i in range(count):
+        halves[pl.ds(pl.multiple_of(core * (m // 2), 8) + i * piece, piece), :] = own_ref[i, :piece]
+        halves[pl.ds(pl.multiple_of((1 - core) * (m // 2), 8) + i * piece, piece), :] = other_ref[i, :piece]
+    basis = basis_ref[...]
+    hi = basis.astype(BF16)
+    q12[:, :RANK] = hi
+    q12[:, RANK:] = (basis - hi.astype(F32)).astype(BF16)
+    steps = m // COLS
+    copies = []
+    for j in range(steps):
+        cols = pl.ds(j * COLS, COLS)
+        right = mm32(halves[cols, :], inv_ref[...], NT) * (1.0 / replicas)
+        right_ref[cols, :] = right
+        hi = right.astype(BF16)
+        low = (right - hi.astype(F32)).astype(BF16)
+        update = mm(q12[...], jnp.concatenate([hi, hi], axis=1), NT) + mm(q12[:, :RANK], low, NT)
+        new_ref[:, cols] = (g_ref[:, cols].astype(F32) + e_ref[:, cols].astype(F32) - update).astype(BF16)
+        copies.append(pltpu.make_async_copy(right_ref.at[cols], right_hbm.at[cols], sems.at[2 * j]))
+        copies.append(pltpu.make_async_copy(new_ref.at[:, cols], new_hbm.at[:, cols], sems.at[2 * j + 1]))
+        copies[-2].start()
+        copies[-1].start()
+    for copy in copies:
+        copy.wait()
 
 
 def residue(own, other, basis, inv, g, e, replicas):
     n, m = g.shape
-    parts = pl.BlockSpec(own.shape, lambda j: (0, 0, 0))
-    block = pl.BlockSpec((n, COLS), lambda j: (0, j))
     return pl.pallas_call(
         functools.partial(residue_kernel, replicas),
-        grid=(m // COLS,),
-        in_specs=[
-            parts,
-            parts,
-            pl.BlockSpec((n, RANK), lambda j: (0, 0)),
-            pl.BlockSpec((RANK, RANK), lambda j: (0, 0)),
-            block,
-            block,
-        ],
-        out_specs=[pl.BlockSpec((COLS, RANK), lambda j: (j, 0)), block],
+        in_specs=[pl.BlockSpec(memory_space=pltpu.VMEM)] * 6,
+        out_specs=[pl.BlockSpec(memory_space=pltpu.HBM)] * 2,
         out_shape=[jax.ShapeDtypeStruct((m, RANK), F32), jax.ShapeDtypeStruct((n, m), BF16)],
         scratch_shapes=[
-            pltpu.VMEM((2, m // 2, RANK), F32),
+            pltpu.VMEM((m, RANK), F32),
             pltpu.VMEM((n, 2 * RANK), BF16),
+            pltpu.VMEM((m, RANK), F32),
+            pltpu.VMEM((n, m), BF16),
+            pltpu.SemaphoreType.DMA((2 * (m // COLS),)),
         ],
         compiler_params=params(),
         name="residue",
@@ -360,8 +378,9 @@
     pieces = (keep + swap(send)).reshape(ny * nz, -1, RANK)
     pieces = lax.all_to_all(pieces, ("y", "tensor"), 0, 0)
     own = lax.all_to_all(total_for_all(pieces), ("y", "tensor"), 0, 0).reshape(n // 2, RANK)
-    sketch, keep, send, gram = factor_terms(own, swap(own), g, e)
-    parts = pack(keep, swap(send), gram, ny * nx, RANK // ny)
+    sketch, s12, s3, gram, send = factor_send(own, swap(own), g, e)
+    got = swap(send)
+    parts = pack(factor_keep(s12, s3, g, e), got, gram, ny * nx, RANK // ny)
     parts = lax.all_to_all(parts, ("y", "fsdp"), 0, 0)
     basis_one, inv_one, parts = first_pass(parts, sketch)
     parts = lax.all_to_all(parts, ("y", "fsdp"), 0, 0)

time: 118 us -> 109 us (0.924)
  local copies, waits for them, and re-layouts: 5.25 us -> 0.01 us
  Pallas kernels: 29.4 us -> 26.9 us
  waiting for transfers between devices: 3.78 us -> 2.33 us
    unnamed x8 -> x4, local copies, waits for them, and re-layouts: 5.25 us -> 0.01 us
    pallas_call x3 -> x4, Pallas kernels: 17.1 us -> 14.6 us  [the longest x1 6.3 us: local_sketch(): pl.pallas_call(sketch_kernel, in_specs=[pl.BlockSpec(memory_space=pltpu.H...]
    ppermute x4, waiting for transfers between devices: 3.78 us -> 2.33 us  [swap(): return lax.ppermute(x, 'core', [(0, 1), (1, 0)])]
  transfers between devices with their start and end apart: 4 -> 4, of which waited for: 3 -> 2; matrix products, arithmetic and copies ran while one was open for 0% -> 0% of each run, Pallas kernels for 5% -> 7%
where the time goes in v2:
time: 109 us
  blocking collectives  68.7 us (63%)
  Pallas kernels  26.9 us (25%)
  starting transfers between devices  9.86 us (9%)
  waiting for transfers between devices  2.33 us (2%)
    all_to_all x2, blocking collectives, shards(): parts = lax.all_to_all(parts, ('y', 'fsdp'), 0, 0)  33.3 us
    all_to_all x1, blocking collectives, shards(): pieces = lax.all_to_all(pieces, ('y', 'tensor'), 0, 0)  18.9 us
    all_to_all x1, blocking collectives, shards(): lax.all_to_all(total_for_all(pieces), ('y', 'tensor'), 0, 0)  16.4 us
    ppermute x4, starting transfers between devices, swap(): return lax.ppermute(x, 'core', [(0, 1), (1, 0)])  9.86 us
    pallas_call x1, Pallas kernels, first_pass(): pl.pallas_call(first_pass_kernel, out_shape=[jax.ShapeDtypeStruct(sketch....  6.74 us
    pallas_call x1, Pallas kernels, local_sketch(): pl.pallas_call(sketch_kernel, in_specs=[pl.BlockSpec(memory_space=pltpu.H...  6.3 us
    pallas_call x1, Pallas kernels, second_pass(): pl.pallas_call(second_pass_kernel, out_shape=[jax.ShapeDtypeStruct(basis_...  5.41 us
    pallas_call x1, Pallas kernels, residue(): pl.pallas_call(functools.partial(residue_kernel, replicas), in_specs=[pl....  4.55 us
  transfers between devices with their start and end apart: 4, of which 2 were waited for; matrix products, arithmetic and copies ran while one was open for 0% of the time, Pallas kernels for 7%

profile of v2, /device:TPU:1, one launch (start us, length us, event | category | flops | bytes accessed | tf_op | source)
XLA Modules:
  0.0 108.7 jit_solution(13596453824598676126)
XLA Ops:
  0.6 6.3 %local_sketch.1 = (f32[512,128]{1,0:T(8,128)S(1)}, f32[512,128]{1,0:T(8,128)S(1)}) custom-call(bf16[1024,1792]{1,0:T(8,128)(2,1)} %bitcast.5, bf16[1024,1792]{1,0:T(8,128)(2,1)} %bitcast.9, f32[1792,128]{1,0:T(8,128)} %p_hbm.1), custom_call_target="tpu_custom_call" | custom-call | tf_op jit(solution)/shard_map/local_sketch/pallas_call | solution.py:89
  6.9 3.3 %collective-permute-start = (f32[512,128]{1,0:T(8,128)S(1)}, f32[512,128]{1,0:T(8,128)S(1)}, u32[]{:S(2)}, u32[]{:S(2)}) collective-permute-start(f32[512,128]{1,0:T(8,128)S(1)} %get-tuple-element.17), channel_id=1, source_target_pairs={{0,32},{32,0},{1,33},{33,1},{2,34},{34,2},{3,35},{35,3},{4,36},{36... | collective-permute-start | bytes 786440 | tf_op jit(solution)/shard_map/ppermute | solution.py:370
  10.3 1.2 %collective-permute-done = f32[512,128]{1,0:T(8,128)S(1)} collective-permute-done((f32[512,128]{1,0:T(8,128)S(1)}, f32[512,128]{1,0:T(8,128)S(1)}, u32[]{:S(2)}, u32[]{:S(2)}) %collective-permute-start) | collective-permute-done | bytes 262176 | tf_op jit(solution)/shard_map/ppermute | solution.py:370
  11.5 18.9 %all_to_all.20.parts_ref = f32[32,16,128]{2,1,0:T(8,128)S(1)} all-to-all(f32[32,16,128]{2,1,0:T(8,128)S(1)} %bitcast.15), channel_id=1, replica_groups=mesh['y'=4,'core'=2,'fsdp'=4,'tensor'=8] {'y','tensor'}, dimensions={0} | all-to-all | bytes 524288 | tf_op jit(solution)/shard_map/all_to_all | solution.py:379
  30.4 0.0 copy-start
  30.4 0.0 copy-start.1
  30.4 0.1 sketch_total.1
  30.5 16.4 %all_to_all.21 = f32[32,16,128]{2,1,0:T(8,128)S(1)} all-to-all(f32[32,16,128]{2,1,0:T(8,128)S(1)} %sketch_total.1), channel_id=1, replica_groups=mesh['y'=4,'core'=2,'fsdp'=4,'tensor'=8] {'y','tensor'}, dimensions={0} | all-to-all | bytes 524288 | tf_op jit(solution)/shard_map/all_to_all | solution.py:380
  46.9 3.6 %collective-permute-start.1 = (f32[512,128]{1,0:T(8,128)S(1)}, f32[512,128]{1,0:T(8,128)S(1)}, u32[]{:S(2)}, u32[]{:S(2)}) collective-permute-start(f32[512,128]{1,0:T(8,128)S(1)} %bitcast.13), channel_id=1, source_target_pairs={{0,32},{32,0},{1,33},{33,1},{2,34},{34,2},{3,35},{35,3},{4,36},{36... | collective-permute-start | bytes 786440 | tf_op jit(solution)/shard_map/ppermute | solution.py:370
  50.5 1.2 %collective-permute-done.1.other_ref = f32[512,128]{1,0:T(8,128)S(1)} collective-permute-done((f32[512,128]{1,0:T(8,128)S(1)}, f32[512,128]{1,0:T(8,128)S(1)}, u32[]{:S(2)}, u32[]{:S(2)}) %collective-permute-start.1) | collective-permute-done | bytes 262176 | tf_op jit(solution)/shard_map/ppermute | solution.py:370
  51.7 0.0 copy-done
  51.7 0.0 copy-done.1
  51.7 2.0 %factor_send.1 = (f32[1024,128]{1,0:T(8,128)S(1)}, bf16[256,1024]{1,0:T(8,128)(2,1)S(1)}, bf16[128,1024]{1,0:T(8,128)(2,1)S(1)}, f32[128,128]{1,0:T(8,128)S(1)}, f32[896,128]{1,0:T(8,128)S(1)}) custom-call(f32[512,128]{1,0:T(8,128)S(1)} %bitcast.14, f32[512,128]{1,0:T(8,128)S(1)} %collective-permute-done.1.other_ref, bf16[1024,1792]{1,0:T(8,128)(2,1)S(1)} %bitcast.6, ...), custom_call_target="tpu_custom_call" | custom-call | tf_op jit(solution)/shard_map/factor_send/pallas_call | solution.py:160
  53.7 0.5 collective-permute-start.2
  54.2 1.7 %factor_keep.1.keep_ref = f32[896,128]{1,0:T(8,128)S(1)} custom-call(bf16[256,1024]{1,0:T(8,128)(2,1)S(1)} %get-tuple-element.18.s12_ref, bf16[128,1024]{1,0:T(8,128)(2,1)S(1)} %get-tuple-element.19.s3_ref, bf16[1024,1792]{1,0:T(8,128)(2,1)S(1)} %bitcast.7, bf16[1024,1792]{1,0:T(8,128)(2,1)S(1)} %bitcast.11), custom_call_target="tpu_custom_call" | custom-call | flops 1000000000 | bytes 8000000 | tf_op jit(solution)/shard_map/factor_keep/pallas_call | solution.py:175
  55.9 0.0 collective-permute-done.2.got_ref
  55.9 0.1 pack.1
  56.0 18.3 %all_to_all.22.parts_ref = f32[16,88,128]{2,1,0:T(8,128)S(1)} all-to-all(f32[16,88,128]{2,1,0:T(8,128)S(1)} %pack.1), channel_id=1, replica_groups=mesh['y'=4,'core'=2,'fsdp'=4,'tensor'=8] {'y','fsdp'}, dimensions={0} | all-to-all | bytes 1441792 | tf_op jit(solution)/shard_map/all_to_all | solution.py:384
  74.3 6.7 %first_pass.1 = (f32[1024,128]{1,0:T(8,128)S(1)}, f32[128,128]{1,0:T(8,128)S(1)}, f32[16,88,128]{2,1,0:T(8,128)S(1)}) custom-call(f32[16,88,128]{2,1,0:T(8,128)S(1)} %all_to_all.22.parts_ref, f32[1024,128]{1,0:T(8,128)S(1)} %get-tuple-element.22.sketch_ref), custom_call_target="tpu_custom_call" | custom-call | tf_op jit(solution)/shard_map/first_pass/pallas_call | solution.py:286
  81.0 15.1 %all_to_all.23.parts_ref.own_ref = f32[16,88,128]{2,1,0:T(8,128)S(1)} all-to-all(f32[16,88,128]{2,1,0:T(8,128)S(1)} %get-tuple-element.23), channel_id=1, replica_groups=mesh['y'=4,'core'=2,'fsdp'=4,'tensor'=8] {'y','fsdp'}, dimensions={0} | all-to-all | bytes 1441792 | tf_op jit(solution)/shard_map/all_to_all | solution.py:386
  96.1 2.4 %collective-permute-start.3 = (f32[16,88,128]{2,1,0:T(8,128)S(1)}, f32[16,88,128]{2,1,0:T(8,128)S(1)}, u32[]{:S(2)}, u32[]{:S(2)}) collective-permute-start(f32[16,88,128]{2,1,0:T(8,128)S(1)} %all_to_all.23.parts_ref.own_ref), channel_id=1, source_target_pairs={{0,32},{32,0},{1,33},{33,1},{2,34},{34,2},{3,35},{35,3},{4,36},{36... | collective-permute-start | bytes 2162696 | tf_op jit(solution)/shard_map/ppermute | solution.py:370
  98.5 5.4 %second_pass.1 = (f32[1024,128]{1,0:T(8,128)S(1)}, f32[128,128]{1,0:T(8,128)S(1)}) custom-call(f32[16,88,128]{2,1,0:T(8,128)S(1)} %all_to_all.23.parts_ref.own_ref, f32[1024,128]{1,0:T(8,128)S(1)} %get-tuple-element.24.basis_one_ref, f32[128,128]{1,0:T(8,128)S(1)} %get-tuple-element.25.inv_one_ref), custom_call_target="tpu_custom_call" | custom-call | tf_op jit(solution)/shard_map/second_pass/pallas_call | solution.py:307
  103.9 0.0 collective-permute-done.3.other_ref
  103.9 4.6 %residue.1 = (f32[1792,128]{1,0:T(8,128)}, bf16[1024,1792]{1,0:T(8,128)(2,1)}) custom-call(f32[16,88,128]{2,1,0:T(8,128)S(1)} %all_to_all.23.parts_ref.own_ref, f32[16,88,128]{2,1,0:T(8,128)S(1)} %collective-permute-done.3.other_ref, f32[1024,128]{1,0:T(8,128)S(1)} %get-tuple-element.26.basis_ref, f32[128,128]{1,0:T(8,128)S(1)} %get-tuple-element.27.inv_ref, ...), custom_call_target="tpu_custom_call" | custom-call | tf_op jit(solution)/shard_map/residue/pallas_call | solution.py:352
  (1 shorter events, 0.0 us)
Async XLA Ops:
  6.9 4.5 %collective-permute-start = (f32[512,128]{1,0:T(8,128)S(1)}, f32[512,128]{1,0:T(8,128)S(1)}, u32[]{:S(2)}, u32[]{:S(2)}) collective-permute-start(f32[512,128]{1,0:T(8,128)S(1)} %get-tuple-element.17), channel_id=1, source_target_pairs={{0,32},{32,0},{1,33},{33,1},{2,34},{34,2},{3,35},{35,3},{4,36},{36... | collective-permute-start | bytes 786440 | tf_op jit(solution)/shard_map/ppermute | solution.py:370
  30.4 21.2 %copy-start = (bf16[1,1024,1792]{2,1,0:T(8,128)(2,1)S(1)}, bf16[1,1024,1792]{2,1,0:T(8,128)(2,1)}, u32[]{:S(2)}) copy-start(bf16[1,1024,1792]{2,1,0:T(8,128)(2,1)} %param.3) | copy-start | bytes 11010052
  30.4 21.2 %copy-start.1 = (bf16[1,1024,1792]{2,1,0:T(8,128)(2,1)S(1)}, bf16[1,1024,1792]{2,1,0:T(8,128)(2,1)}, u32[]{:S(2)}) copy-start(bf16[1,1024,1792]{2,1,0:T(8,128)(2,1)} %param.4) | copy-start | bytes 11010052
  46.9 4.8 %collective-permute-start.1 = (f32[512,128]{1,0:T(8,128)S(1)}, f32[512,128]{1,0:T(8,128)S(1)}, u32[]{:S(2)}, u32[]{:S(2)}) collective-permute-start(f32[512,128]{1,0:T(8,128)S(1)} %bitcast.13), channel_id=1, source_target_pairs={{0,32},{32,0},{1,33},{33,1},{2,34},{34,2},{3,35},{35,3},{4,36},{36... | collective-permute-start | bytes 786440 | tf_op jit(solution)/shard_map/ppermute | solution.py:370
  53.7 2.2 %collective-permute-start.2 = (f32[896,128]{1,0:T(8,128)S(1)}, f32[896,128]{1,0:T(8,128)S(1)}, u32[]{:S(2)}, u32[]{:S(2)}) collective-permute-start(f32[896,128]{1,0:T(8,128)S(1)} %get-tuple-element.20), channel_id=1, source_target_pairs={{0,32},{32,0},{1,33},{33,1},{2,34},{34,2},{3,35},{35,3},{4,36},{36... | collective-permute-start | bytes 1376264 | tf_op jit(solution)/shard_map/ppermute | solution.py:370
  96.1 7.9 %collective-permute-start.3 = (f32[16,88,128]{2,1,0:T(8,128)S(1)}, f32[16,88,128]{2,1,0:T(8,128)S(1)}, u32[]{:S(2)}, u32[]{:S(2)}) collective-permute-start(f32[16,88,128]{2,1,0:T(8,128)S(1)} %all_to_all.23.parts_ref.own_ref), channel_id=1, source_target_pairs={{0,32},{32,0},{1,33},{33,1},{2,34},{34,2},{3,35},{35,3},{4,36},{36... | collective-permute-start | bytes 2162696 | tf_op jit(solution)/shard_map/ppermute | solution.py:370

commit v3 on v2

--- a/solution.py
+++ b/solution.py
@@ -12,6 +12,9 @@
 ROWS = 256
 COLS = 256
 VMEM_LIMIT = 24 * 1024 * 1024
+TOP = 512
+FETCH_LIMIT = 51000000
+RESIDUE_LIMIT = 51000000
 STREAM_LIMIT = 55500000
 NT = (((1,), (1,)), ((), ()))
 NN = (((1,), (0,)), ((), ()))
@@ -32,6 +35,10 @@
     mid = rest.astype(BF16)
     low = (rest - mid.astype(F32)).astype(BF16)
     return hi, mid, low
+
+
+VMEM_SPEC = pl.BlockSpec(memory_space=pltpu.VMEM)
+HBM_SPEC = pl.BlockSpec(memory_space=pltpu.HBM)
 
 
 def params(limit=VMEM_LIMIT):
@@ -88,8 +95,8 @@
     half = jax.ShapeDtypeStruct((n // 2, RANK), F32)
     return pl.pallas_call(
         sketch_kernel,
-        in_specs=[pl.BlockSpec(memory_space=pltpu.HBM)] * 3,
-        out_specs=[pl.BlockSpec(memory_space=pltpu.VMEM)] * 2,
+        in_specs=[HBM_SPEC] * 3,
+        out_specs=[VMEM_SPEC] * 2,
         out_shape=[half, half],
         scratch_shapes=[
             pltpu.VMEM((n, m), BF16),
@@ -132,7 +139,7 @@
         out_ref[start : start + size, :] = (both[:RANK] + both[RANK:] + mm(s3, g + e)).T
 
 
-def factor_send_kernel(own_ref, other_ref, g_ref, e_ref, sketch_ref, s12_ref, s3_ref, gram_ref, send_ref):
+def prepare_kernel(own_ref, other_ref, sketch_ref, s12_ref, s3_ref, gram_ref):
     core = lax.axis_index("core")
     half = own_ref.shape[0]
     sketch_ref[pl.ds(pl.multiple_of(core * half, half), half), :] = own_ref[...]
@@ -148,69 +155,50 @@
         + (square[:RANK, RANK:] + square[RANK:, :RANK])
         + (cross + cross.T)
     )
-    factor_block(s12_ref[...], s3_ref[...], g_ref, e_ref, send_ref, 1 - core)
-
-
-def factor_keep_kernel(s12_ref, s3_ref, g_ref, e_ref, keep_ref):
-    factor_block(s12_ref[...], s3_ref[...], g_ref, e_ref, keep_ref, lax.axis_index("core"))
-
-
-def factor_send(own, other, g, e):
-    n, m = g.shape
-    return pl.pallas_call(
-        factor_send_kernel,
+
+
+def prepare(own, other):
+    n = 2 * own.shape[0]
+    return pl.pallas_call(
+        prepare_kernel,
         out_shape=[
             jax.ShapeDtypeStruct((n, RANK), F32),
             jax.ShapeDtypeStruct((2 * RANK, n), BF16),
             jax.ShapeDtypeStruct((RANK, n), BF16),
             jax.ShapeDtypeStruct((RANK, RANK), F32),
-            jax.ShapeDtypeStruct((m // 2, RANK), F32),
         ],
         compiler_params=params(),
-        name="factor_send",
-    )(own, other, g, e)
-
-
-def factor_keep(s12, s3, g, e):
-    return pl.pallas_call(
-        factor_keep_kernel,
+        name="prepare",
+    )(own, other)
+
+
+def factor_send_kernel(s12_ref, s3_ref, g_ref, e_ref, send_ref):
+    factor_block(s12_ref[...], s3_ref[...], g_ref, e_ref, send_ref, 1 - lax.axis_index("core"))
+
+
+def factor_keep_kernel(s12_ref, s3_ref, g_ref, e_ref, keep_ref):
+    factor_block(s12_ref[...], s3_ref[...], g_ref, e_ref, keep_ref, lax.axis_index("core"))
+
+
+def factor_half(kernel, name, s12, s3, g, e):
+    return pl.pallas_call(
+        kernel,
         out_shape=jax.ShapeDtypeStruct((g.shape[1] // 2, RANK), F32),
         compiler_params=params(),
         cost_estimate=pl.CostEstimate(flops=10**9, bytes_accessed=8 * 10**6, transcendentals=0),
-        name="factor_keep",
+        name=name,
     )(s12, s3, g, e)
 
 
-def pack_kernel(keep_ref, got_ref, gram_ref, out_ref):
-    count, chunk = out_ref.shape[0], out_ref.shape[1]
-    strip = RANK // lax.axis_size("y")
-    piece = chunk - strip
-    gram_rows = gram_ref[pl.ds(pl.multiple_of(lax.axis_index("y") * strip, strip), strip), :]
-    for i in range(count):
-        rows = pl.ds(i * piece, piece)
-        out_ref[i, :piece] = keep_ref[rows, :] + got_ref[rows, :]
-        out_ref[i, piece:] = gram_rows
-
-
-def pack(keep, got, gram, count, strip):
-    piece = keep.shape[0] // count
-    return pl.pallas_call(
-        pack_kernel,
-        out_shape=jax.ShapeDtypeStruct((count, piece + strip, RANK), F32),
-        compiler_params=params(),
-        name="pack",
-    )(keep, got, gram)
-
-
-def gather_gram(parts_ref, gram_ref):
-    strips, columns = lax.axis_size("y"), lax.axis_size("fsdp")
-    strip = RANK // strips
-    piece = parts_ref.shape[1] - strip
-    for i in range(strips):
-        total = parts_ref[i * columns, piece:]
-        for k in range(1, columns):
-            total = total + parts_ref[i * columns + k, piece:]
-        gram_ref[i * strip : (i + 1) * strip, :] = total
+def sum_in_order(parts, slots, out_ref):
+    count = len(parts)
+    place = lax.axis_index("fsdp")
+    for k in range(count):
+        slots[lax.rem(place + count - k, count)] = parts[k][...]
+    total = slots[0]
+    for k in range(1, count):
+        total = total + slots[k]
+    out_ref[...] = total
 
 
 def across(tile, lane):
@@ -263,111 +251,192 @@
             b_ref[there, :] = b_low
 
 
-def first_pass_kernel(parts_ref, sketch_ref, basis_ref, inv_ref, out_ref, a_ref, b_ref, gram_ref):
-    strip = RANK // lax.axis_size("y")
-    count, chunk = parts_ref.shape[0], parts_ref.shape[1]
-    piece = chunk - strip
-    gather_gram(parts_ref, a_ref)
+def pieces_kernel(parts_ref, out_ref):
+    count = parts_ref.shape[0]
+    total = parts_ref[0]
+    for i in range(1, count):
+        total = total + parts_ref[i]
+    for i in range(count):
+        out_ref[i] = total
+
+
+def total_pieces(parts):
+    return pl.pallas_call(
+        pieces_kernel,
+        out_shape=jax.ShapeDtypeStruct(parts.shape, F32),
+        compiler_params=params(),
+        name="total_pieces",
+    )(parts)
+
+
+def first_pass_kernel(*refs):
+    grams, (sketch_ref, basis_ref, inv_ref, gram_ref, a_ref, b_ref, slots) = refs[:-7], refs[-7:]
+    sum_in_order(grams, slots, a_ref)
     invert_cholesky(a_ref, b_ref, inv_ref)
     basis = mm32(sketch_ref[...], inv_ref[...], NT)
     basis_ref[...] = basis
     gram_ref[...] = mm32(basis, basis, TN)
-    total = parts_ref[0, :piece]
-    for i in range(1, count):
-        total = total + parts_ref[i, :piece]
-    gram_rows = gram_ref[pl.ds(pl.multiple_of(lax.axis_index("y") * strip, strip), strip), :]
-    for i in range(count):
-        out_ref[i, :piece] = total
-        out_ref[i, piece:] = gram_rows
-
-
-def first_pass(parts, sketch):
+
+
+def pass_scratch(count):
+    return [pltpu.VMEM((RANK, RANK), F32)] * 2 + [pltpu.VMEM((count, RANK, RANK), F32)]
+
+
+def pass_cost():
+    return pl.CostEstimate(flops=4 * 10**9, bytes_accessed=2 * 10**7, transcendentals=0)
+
+
+def first_pass(grams, sketch):
     square = jax.ShapeDtypeStruct((RANK, RANK), F32)
     return pl.pallas_call(
         first_pass_kernel,
-        out_shape=[
-            jax.ShapeDtypeStruct(sketch.shape, F32),
-            square,
-            jax.ShapeDtypeStruct(parts.shape, F32),
-        ],
-        scratch_shapes=[pltpu.VMEM((RANK, RANK), F32)] * 3,
-        compiler_params=params(),
+        out_shape=[jax.ShapeDtypeStruct(sketch.shape, F32), square, square],
+        scratch_shapes=pass_scratch(len(grams)),
+        compiler_params=params(),
+        cost_estimate=pass_cost(),
         name="first_pass",
-    )(parts, sketch)
-
-
-def second_pass_kernel(parts_ref, basis_one_ref, inv_one_ref, basis_ref, inv_ref, a_ref, b_ref, two_ref):
-    gather_gram(parts_ref, a_ref)
+    )(*grams, sketch)
+
+
+def second_pass_kernel(*refs):
+    grams, (basis_one_ref, inv_one_ref, basis_ref, inv_ref, two_ref, a_ref, b_ref, slots) = refs[:-8], refs[-8:]
+    sum_in_order(grams, slots, a_ref)
     invert_cholesky(a_ref, b_ref, two_ref)
     basis_ref[...] = mm32(basis_one_ref[...], two_ref[...], NT)
     inv_ref[...] = mm32(two_ref[...], inv_one_ref[...])
 
 
-def second_pass(parts, basis_one, inv_one):
+def second_pass(grams, basis_one, inv_one):
     return pl.pallas_call(
         second_pass_kernel,
         out_shape=[
             jax.ShapeDtypeStruct(basis_one.shape, F32),
             jax.ShapeDtypeStruct(inv_one.shape, F32),
         ],
-        scratch_shapes=[pltpu.VMEM((RANK, RANK), F32)] * 3,
-        compiler_params=params(),
+        scratch_shapes=[pltpu.VMEM((RANK, RANK), F32)] + pass_scratch(len(grams)),
+        compiler_params=params(),
+        cost_estimate=pass_cost(),
         name="second_pass",
-    )(parts, basis_one, inv_one)
-
-
-def residue_kernel(replicas, own_ref, other_ref, basis_ref, inv_ref, g_ref, e_ref, right_hbm, new_hbm, halves, q12, right_ref, new_ref, sems):
-    core = lax.axis_index("core")
-    strip = RANK // lax.axis_size("y")
-    count, chunk = own_ref.shape[0], own_ref.shape[1]
-    piece = chunk - strip
-    m = g_ref.shape[1]
-    for i in range(count):
-        halves[pl.ds(pl.multiple_of(core * (m // 2), 8) + i * piece, piece), :] = own_ref[i, :piece]
-        halves[pl.ds(pl.multiple_of((1 - core) * (m // 2), 8) + i * piece, piece), :] = other_ref[i, :piece]
+    )(*grams, basis_one, inv_one)
+
+
+def wide_nt(x, w):
+    x1, x2, x3 = split3(x)
+    w1, w2, w3 = split3(w)
+    front = jnp.concatenate(
+        [jnp.concatenate([w1, w1], axis=1), jnp.concatenate([w2, w2], axis=1)], axis=0
+    )
+    both = mm(jnp.concatenate([x1, x2], axis=1), front, NT)
+    rest = mm(jnp.concatenate([x1, x3], axis=1), jnp.concatenate([w3, w1], axis=1), NT)
+    return both[:, :RANK] + (both[:, RANK:] + rest)
+
+
+def row_loads(g_hbm, e_hbm, g_ref, e_ref, sems, first, last):
+    loads = []
+    for k, start in enumerate(range(first, last, ROWS)):
+        here, there = pl.ds(k * ROWS, ROWS), pl.ds(start, ROWS)
+        loads.append(pltpu.make_async_copy(g_hbm.at[there], g_ref.at[here], sems.at[2 * k]))
+        loads.append(pltpu.make_async_copy(e_hbm.at[there], e_ref.at[here], sems.at[2 * k + 1]))
+    return loads
+
+
+def fetch_kernel(basis_ref, g_hbm, e_hbm, q12_ref, g_ref, e_ref, sems):
+    loads = row_loads(g_hbm, e_hbm, g_ref, e_ref, sems, 0, g_ref.shape[0])
+    for load in loads:
+        load.start()
     basis = basis_ref[...]
     hi = basis.astype(BF16)
-    q12[:, :RANK] = hi
-    q12[:, RANK:] = (basis - hi.astype(F32)).astype(BF16)
-    steps = m // COLS
+    q12_ref[:, :RANK] = hi
+    q12_ref[:, RANK:] = (basis - hi.astype(F32)).astype(BF16)
+    for load in loads:
+        load.wait()
+
+
+def fetch(basis, g, e, top):
+    n, m = g.shape
+    rows = jax.ShapeDtypeStruct((top, m), BF16)
+    return pl.pallas_call(
+        fetch_kernel,
+        in_specs=[VMEM_SPEC, HBM_SPEC, HBM_SPEC],
+        out_specs=[VMEM_SPEC] * 3,
+        out_shape=[jax.ShapeDtypeStruct((n, 2 * RANK), BF16), rows, rows],
+        scratch_shapes=[pltpu.SemaphoreType.DMA((2 * (top // ROWS),))],
+        compiler_params=params(FETCH_LIMIT),
+        cost_estimate=pl.CostEstimate(flops=10**6, bytes_accessed=10**7, transcendentals=0),
+        name="fetch",
+    )(basis, g, e)
+
+
+def residue_kernel(replicas, own_ref, other_ref, q12, inv_ref, g_top, e_top, g_hbm, e_hbm, right_hbm, new_hbm, halves, r11, r2, right_ref, new_ref, g_ref, e_ref, in_sems, out_sems):
+    core = lax.axis_index("core")
+    count, piece = own_ref.shape[0], own_ref.shape[1]
+    n, m = new_ref.shape
+    top = g_top.shape[0]
+    loads = row_loads(g_hbm, e_hbm, g_ref, e_ref, in_sems, top, n)
+    for load in loads:
+        load.start()
+    for i in range(count):
+        halves[pl.ds(pl.multiple_of(core * (m // 2), 8) + i * piece, piece), :] = own_ref[i]
+        halves[pl.ds(pl.multiple_of((1 - core) * (m // 2), 8) + i * piece, piece), :] = other_ref[i]
+    right = wide_nt(halves[...], inv_ref[...]) * (1.0 / replicas)
+    right_ref[...] = right
+    right_copy = pltpu.make_async_copy(right_ref, right_hbm, out_sems.at[n // ROWS])
+    right_copy.start()
+    hi = right.astype(BF16)
+    r11[:, :RANK] = hi
+    r11[:, RANK:] = hi
+    r2[...] = (right - hi.astype(F32)).astype(BF16)
     copies = []
-    for j in range(steps):
-        cols = pl.ds(j * COLS, COLS)
-        right = mm32(halves[cols, :], inv_ref[...], NT) * (1.0 / replicas)
-        right_ref[cols, :] = right
-        hi = right.astype(BF16)
-        low = (right - hi.astype(F32)).astype(BF16)
-        update = mm(q12[...], jnp.concatenate([hi, hi], axis=1), NT) + mm(q12[:, :RANK], low, NT)
-        new_ref[:, cols] = (g_ref[:, cols].astype(F32) + e_ref[:, cols].astype(F32) - update).astype(BF16)
-        copies.append(pltpu.make_async_copy(right_ref.at[cols], right_hbm.at[cols], sems.at[2 * j]))
-        copies.append(pltpu.make_async_copy(new_ref.at[:, cols], new_hbm.at[:, cols], sems.at[2 * j + 1]))
-        copies[-2].start()
+    for k, first in enumerate(range(0, n, ROWS)):
+        rows = pl.ds(first, ROWS)
+        g_in, e_in, there = g_top, e_top, rows
+        if first >= top:
+            g_in, e_in, there = g_ref, e_ref, pl.ds(first - top, ROWS)
+            loads[2 * ((first - top) // ROWS)].wait()
+            loads[2 * ((first - top) // ROWS) + 1].wait()
+        for start in range(0, m, COLS):
+            cols = pl.ds(start, COLS)
+            update = mm(q12[rows, :], r11[cols, :], NT) + mm(q12[rows, :RANK], r2[cols, :], NT)
+            new_ref[rows, cols] = (g_in[there, cols].astype(F32) + e_in[there, cols].astype(F32) - update).astype(BF16)
+        copies.append(pltpu.make_async_copy(new_ref.at[rows], new_hbm.at[rows], out_sems.at[k]))
         copies[-1].start()
     for copy in copies:
         copy.wait()
-
-
-def residue(own, other, basis, inv, g, e, replicas):
+    right_copy.wait()
+
+
+def residue(own, other, q12, inv, g_top, e_top, g, e, replicas):
     n, m = g.shape
+    chunks, rest = n // ROWS, n - g_top.shape[0]
     return pl.pallas_call(
         functools.partial(residue_kernel, replicas),
-        in_specs=[pl.BlockSpec(memory_space=pltpu.VMEM)] * 6,
-        out_specs=[pl.BlockSpec(memory_space=pltpu.HBM)] * 2,
+        in_specs=[VMEM_SPEC] * 6 + [HBM_SPEC] * 2,
+        out_specs=[HBM_SPEC] * 2,
         out_shape=[jax.ShapeDtypeStruct((m, RANK), F32), jax.ShapeDtypeStruct((n, m), BF16)],
         scratch_shapes=[
             pltpu.VMEM((m, RANK), F32),
-            pltpu.VMEM((n, 2 * RANK), BF16),
+            pltpu.VMEM((m, 2 * RANK), BF16),
+            pltpu.VMEM((m, RANK), BF16),
             pltpu.VMEM((m, RANK), F32),
             pltpu.VMEM((n, m), BF16),
-            pltpu.SemaphoreType.DMA((2 * (m // COLS),)),
+            pltpu.VMEM((rest, m), BF16),
+            pltpu.VMEM((rest, m), BF16),
+            pltpu.SemaphoreType.DMA((2 * (rest // ROWS),)),
+            pltpu.SemaphoreType.DMA((chunks + 1,)),
         ],
-        compiler_params=params(),
+        compiler_params=params(RESIDUE_LIMIT),
         name="residue",
-    )(own, other, basis, inv, g, e)
+    )(own, other, q12, inv, g_top, e_top, g, e)
 
 
 def swap(x):
     return lax.ppermute(x, "core", [(0, 1), (1, 0)])
+
+
+def round_fsdp(x, count):
+    return [x] + [
+        lax.ppermute(x, "fsdp", [(i, (i + k) % count) for i in range(count)]) for k in range(1, count)
+    ]
 
 
 def shards(gradients, errors, start_factor):
@@ -378,15 +447,22 @@
     pieces = (keep + swap(send)).reshape(ny * nz, -1, RANK)
     pieces = lax.all_to_all(pieces, ("y", "tensor"), 0, 0)
     own = lax.all_to_all(total_for_all(pieces), ("y", "tensor"), 0, 0).reshape(n // 2, RANK)
-    sketch, s12, s3, gram, send = factor_send(own, swap(own), g, e)
+    sketch, s12, s3, gram = prepare(own, swap(own))
+    grams = round_fsdp(gram, nx)
+    send = factor_half(factor_send_kernel, "factor_send", s12, s3, g, e)
     got = swap(send)
-    parts = pack(factor_keep(s12, s3, g, e), got, gram, ny * nx, RANK // ny)
+    keep = factor_half(factor_keep_kernel, "factor_keep", s12, s3, g, e)
+    parts = (keep + got).reshape(ny * nx, -1, RANK)
     parts = lax.all_to_all(parts, ("y", "fsdp"), 0, 0)
-    basis_one, inv_one, parts = first_pass(parts, sketch)
-    parts = lax.all_to_all(parts, ("y", "fsdp"), 0, 0)
-    other = swap(parts)
-    basis, inv = second_pass(parts, basis_one, inv_one)
-    right_factor, new_errors = residue(parts, other, basis, inv, g, e, 2 * ny)
+    basis_one, inv_one, gram = first_pass(grams, sketch)
+    parts, gram = lax.optimization_barrier((parts, gram))
+    grams = round_fsdp(gram, nx)
+    own = lax.all_to_all(total_pieces(parts), ("y", "fsdp"), 0, 0)
+    basis, inv = second_pass(grams, basis_one, inv_one)
+    own, basis = lax.optimization_barrier((own, basis))
+    other = swap(own)
+    q12, g_top, e_top = fetch(basis, g, e, TOP)
+    right_factor, new_errors = residue(own, other, q12, inv, g_top, e_top, g, e, 2 * ny)
     return (right_factor, new_errors[None])
 
 

time: 109 us -> 103 us (0.945)
  blocking collectives: 68.7 us -> 35.4 us
  starting transfers between devices: 9.86 us -> 26.5 us
  waiting for transfers between devices: 2.33 us -> 8.48 us
  Pallas kernels: 26.9 us -> 30.9 us
    all_to_all x2 -> x0, blocking collectives: 33.3 us -> none  [shards(): parts = lax.all_to_all(parts, ('y', 'fsdp'), 0, 0)]
    all_to_all x0 -> x2, starting transfers between devices: none -> 9.23 us  [the longest x1 4.84 us: shards(): own = lax.all_to_all(total_pieces(parts), ('y', 'fsdp'), 0, 0)]
    all_to_all x0 -> x2, waiting for transfers between devices: none -> 6.14 us  [the longest x1 3.2 us: shards(): own = lax.all_to_all(total_pieces(parts), ('y', 'fsdp'), 0, 0)]
    ppermute x0 -> x6, starting transfers between devices: none -> 5.83 us  [round_fsdp(): lax.ppermute(x, 'fsdp', [(i, (i + k) % count) for i in range(count)])]
    pallas_call x5 -> x7, Pallas kernels: 14.7 us -> 18.8 us  [the longest x1 6.3 us: local_sketch(): pl.pallas_call(sketch_kernel, in_specs=[HBM_SPEC] * 3, out_specs=[VMEM_SP...]
    ppermute x4, starting transfers between devices: 9.86 us -> 11.5 us  [swap(): return lax.ppermute(x, 'core', [(0, 1), (1, 0)])]
  transfers between devices with their start and end apart: 4 -> 12, of which waited for: 2 -> 4; matrix products, arithmetic and copies ran while one was open for 0% -> 1% of each run, Pallas kernels for 7% -> 16%
where the time goes in v3:
time: 103 us
  blocking collectives  35.4 us (34%)
  Pallas kernels  30.9 us (30%)
  starting transfers between devices  26.5 us (26%)
  waiting for transfers between devices  8.48 us (8%)
    all_to_all x1, blocking collectives, shards(): pieces = lax.all_to_all(pieces, ('y', 'tensor'), 0, 0)  18.9 us
    all_to_all x1, blocking collectives, shards(): lax.all_to_all(total_for_all(pieces), ('y', 'tensor'), 0, 0)  16.4 us
    ppermute x4, starting transfers between devices, swap(): return lax.ppermute(x, 'core', [(0, 1), (1, 0)])  11.5 us
    pallas_call x1, Pallas kernels, first_pass(): pl.pallas_call(first_pass_kernel, out_shape=[jax.ShapeDtypeStruct(sketch....  6.67 us
    pallas_call x1, Pallas kernels, local_sketch(): pl.pallas_call(sketch_kernel, in_specs=[HBM_SPEC] * 3, out_specs=[VMEM_SP...  6.3 us
    ppermute x6, starting transfers between devices, round_fsdp(): lax.ppermute(x, 'fsdp', [(i, (i + k) % count) for i in range(count)])  5.83 us
    pallas_call x1, Pallas kernels, residue(): pl.pallas_call(functools.partial(residue_kernel, replicas), in_specs=[VME...  5.62 us
    pallas_call x1, Pallas kernels, second_pass(): pl.pallas_call(second_pass_kernel, out_shape=[jax.ShapeDtypeStruct(basis_...  5.35 us
  transfers between devices with their start and end apart: 12, of which 4 were waited for; matrix products, arithmetic and copies ran while one was open for 1% of the time, Pallas kernels for 16%

profile of v3, /device:TPU:1, one launch (start us, length us, event | category | flops | bytes accessed | tf_op | source)
XLA Modules:
  0.0 103.1 jit_solution(2763192611396894250)
XLA Ops:
  0.6 6.3 %local_sketch.1 = (f32[512,128]{1,0:T(8,128)S(1)}, f32[512,128]{1,0:T(8,128)S(1)}) custom-call(bf16[1024,1792]{1,0:T(8,128)(2,1)} %bitcast.6, bf16[1024,1792]{1,0:T(8,128)(2,1)} %bitcast.11, f32[1792,128]{1,0:T(8,128)} %p_hbm.1), custom_call_target="tpu_custom_call" | custom-call | tf_op jit(solution)/shard_map/local_sketch/pallas_call | solution.py:96
  6.9 3.3 %collective-permute-start = (f32[512,128]{1,0:T(8,128)S(1)}, f32[512,128]{1,0:T(8,128)S(1)}, u32[]{:S(2)}, u32[]{:S(2)}) collective-permute-start(f32[512,128]{1,0:T(8,128)S(1)} %get-tuple-element.23), channel_id=1, source_target_pairs={{0,32},{32,0},{1,33},{33,1},{2,34},{34,2},{3,35},{35,3},{4,36},{36... | collective-permute-start | bytes 786440 | tf_op jit(solution)/shard_map/ppermute | solution.py:433
  10.3 1.2 %collective-permute-done = f32[512,128]{1,0:T(8,128)S(1)} collective-permute-done((f32[512,128]{1,0:T(8,128)S(1)}, f32[512,128]{1,0:T(8,128)S(1)}, u32[]{:S(2)}, u32[]{:S(2)}) %collective-permute-start) | collective-permute-done | bytes 262176 | tf_op jit(solution)/shard_map/ppermute | solution.py:433
  11.5 18.9 %all_to_all.20.parts_ref = f32[32,16,128]{2,1,0:T(8,128)S(1)} all-to-all(f32[32,16,128]{2,1,0:T(8,128)S(1)} %bitcast.18), channel_id=1, replica_groups=mesh['y'=4,'core'=2,'fsdp'=4,'tensor'=8] {'y','tensor'}, dimensions={0} | all-to-all | bytes 524288 | tf_op jit(solution)/shard_map/all_to_all | solution.py:448
  30.4 0.1 sketch_total.1
  30.5 16.4 %all_to_all.21 = f32[32,16,128]{2,1,0:T(8,128)S(1)} all-to-all(f32[32,16,128]{2,1,0:T(8,128)S(1)} %sketch_total.1), channel_id=1, replica_groups=mesh['y'=4,'core'=2,'fsdp'=4,'tensor'=8] {'y','tensor'}, dimensions={0} | all-to-all | bytes 524288 | tf_op jit(solution)/shard_map/all_to_all | solution.py:449
  46.9 3.6 %collective-permute-start.1 = (f32[512,128]{1,0:T(8,128)S(1)}, f32[512,128]{1,0:T(8,128)S(1)}, u32[]{:S(2)}, u32[]{:S(2)}) collective-permute-start(f32[512,128]{1,0:T(8,128)S(1)} %bitcast.16), channel_id=1, source_target_pairs={{0,32},{32,0},{1,33},{33,1},{2,34},{34,2},{3,35},{35,3},{4,36},{36... | collective-permute-start | bytes 786440 | tf_op jit(solution)/shard_map/ppermute | solution.py:433
  50.5 1.2 %collective-permute-done.1.other_ref = f32[512,128]{1,0:T(8,128)S(1)} collective-permute-done((f32[512,128]{1,0:T(8,128)S(1)}, f32[512,128]{1,0:T(8,128)S(1)}, u32[]{:S(2)}, u32[]{:S(2)}) %collective-permute-start.1) | collective-permute-done | bytes 262176 | tf_op jit(solution)/shard_map/ppermute | solution.py:433
  51.7 0.6 prepare.1
  52.3 1.7 %factor_send.1 = f32[896,128]{1,0:T(8,128)S(1)} custom-call(bf16[256,1024]{1,0:T(8,128)(2,1)S(1)} %get-tuple-element.24.s12_ref, bf16[128,1024]{1,0:T(8,128)(2,1)S(1)} %get-tuple-element.25.s3_ref, bf16[1024,1792]{1,0:T(8,128)(2,1)S(1)} %bitcast.9, bf16[1024,1792]{1,0:T(8,128)(2,1)S(1)} %bitcast.14), custom_call_target="tpu_custom_call" | custom-call | flops 1000000000 | bytes 8000000 | tf_op jit(solution)/shard_map/factor_send/pallas_call | solution.py:184
  54.0 0.5 collective-permute-start.2
  54.5 2.5 %collective-permute-start.5 = (f32[128,128]{1,0:T(8,128)S(1)}, f32[128,128]{1,0:T(8,128)S(1)}, u32[]{:S(2)}, u32[]{:S(2)}) collective-permute-start(f32[128,128]{1,0:T(8,128)S(1)} %get-tuple-element.26.refs_0_), channel_id=1, source_target_pairs={{0,24},{8,0},{16,8},{24,16},{1,25},{9,1},{17,9},{25,17},{2,26},{10... | collective-permute-start | bytes 196616 | tf_op jit(solution)/shard_map/ppermute | solution.py:438
  57.0 0.5 collective-permute-start.4
  57.5 0.6 collective-permute-start.3
  58.1 1.7 %factor_keep.1 = f32[896,128]{1,0:T(8,128)S(1)} custom-call(bf16[256,1024]{1,0:T(8,128)(2,1)S(1)} %get-tuple-element.24.s12_ref, bf16[128,1024]{1,0:T(8,128)(2,1)S(1)} %get-tuple-element.25.s3_ref, bf16[1024,1792]{1,0:T(8,128)(2,1)S(1)} %bitcast.10, bf16[1024,1792]{1,0:T(8,128)(2,1)S(1)} %bitcast.15), custom_call_target="tpu_custom_call" | custom-call | flops 1000000000 | bytes 8000000 | tf_op jit(solution)/shard_map/factor_keep/pallas_call | solution.py:184
  59.8 0.0 collective-permute-done.2
  59.8 0.8 add.7
  60.7 4.4 %all-to-all-start.2 = ((f32[16,56,128]{2,1,0:T(8,128)}), f32[16,56,128]{2,1,0:T(8,128)S(1)}, u32[]{:S(2)}, u32[]{:S(2)}) async-start(f32[16,56,128]{2,1,0:T(8,128)} %bitcast.4), calls=%async_computation.2 | async-start | bytes 917504 | tf_op jit(solution)/shard_map/all_to_all | solution.py:456
  65.1 0.0 collective-permute-done.4.refs_2_
  65.1 6.7 %first_pass.1 = (f32[1024,128]{1,0:T(8,128)S(1)}, f32[128,128]{1,0:T(8,128)S(1)}, f32[128,128]{1,0:T(8,128)S(1)}) custom-call(f32[128,128]{1,0:T(8,128)S(1)} %get-tuple-element.26.refs_0_, f32[128,128]{1,0:T(8,128)S(1)} %collective-permute-done.3.refs_1_, f32[128,128]{1,0:T(8,128)S(1)} %collective-permute-done.4.refs_2_, ...), custom_call_target="tpu_custom_call" | custom-call | flops 4000000000 | bytes 20000000 | tf_op jit(solution)/shard_map/first_pass/pallas_call | solution.py:291
  71.8 2.9 %all-to-all-done.2.parts_ref = f32[16,56,128]{2,1,0:T(8,128)S(1)} async-done(((f32[16,56,128]{2,1,0:T(8,128)}), f32[16,56,128]{2,1,0:T(8,128)S(1)}, u32[]{:S(2)}, u32[]{:S(2)}) %all-to-all-start.2) | async-done | bytes 458784 | tf_op jit(solution)/shard_map/all_to_all | solution.py:456
  74.7 0.8 collective-permute-start.8
  75.5 1.4 %collective-permute-start.7 = (f32[128,128]{1,0:T(8,128)S(1)}, f32[128,128]{1,0:T(8,128)S(1)}, u32[]{:S(2)}, u32[]{:S(2)}) collective-permute-start(f32[128,128]{1,0:T(8,128)S(1)} %get-tuple-element.30.refs_0_), channel_id=1, source_target_pairs={{0,16},{8,24},{16,0},{24,8},{1,17},{9,25},{17,1},{25,9},{2,18},{10... | collective-permute-start | bytes 196616 | tf_op jit(solution)/shard_map/ppermute | solution.py:438
  76.9 0.8 total_pieces.1
  77.7 4.8 %all-to-all-start.3 = ((f32[16,56,128]{2,1,0:T(8,128)}), f32[16,56,128]{2,1,0:T(8,128)S(1)}, u32[]{:S(2)}, u32[]{:S(2)}) async-start(f32[16,56,128]{2,1,0:T(8,128)} %total_pieces.1), calls=%async_computation.3 | async-start | bytes 917504 | tf_op jit(solution)/shard_map/all_to_all | solution.py:460
  82.6 0.0 collective-permute-done.7.refs_2_
  82.6 0.0 collective-permute-done.6.refs_1_
  82.6 5.4 %second_pass.1 = (f32[1024,128]{1,0:T(8,128)S(1)}, f32[128,128]{1,0:T(8,128)S(1)}) custom-call(f32[128,128]{1,0:T(8,128)S(1)} %get-tuple-element.30.refs_0_, f32[128,128]{1,0:T(8,128)S(1)} %collective-permute-done.6.refs_1_, f32[128,128]{1,0:T(8,128)S(1)} %collective-permute-done.7.refs_2_, f32[128,128]{1,0:T(8,128)S(1)} %collective-permute-done.8.refs_3_, ...), custom_call_target="tpu_custom_call" | custom-call | flops 4000000000 | bytes 20000000 | tf_op jit(solution)/shard_map/second_pass/pallas_call | solution.py:310
  88.0 3.2 %all-to-all-done.3.own_ref = f32[16,56,128]{2,1,0:T(8,128)S(1)} async-done(((f32[16,56,128]{2,1,0:T(8,128)}), f32[16,56,128]{2,1,0:T(8,128)S(1)}, u32[]{:S(2)}, u32[]{:S(2)}) %all-to-all-start.3) | async-done | bytes 458784 | tf_op jit(solution)/shard_map/all_to_all | solution.py:460
  91.2 4.0 %collective-permute-start.9 = (f32[16,56,128]{2,1,0:T(8,128)S(1)}, f32[16,56,128]{2,1,0:T(8,128)S(1)}, u32[]{:S(2)}, u32[]{:S(2)}) collective-permute-start(f32[16,56,128]{2,1,0:T(8,128)S(1)} %all-to-all-done.3.own_ref), channel_id=1, source_target_pairs={{0,32},{32,0},{1,33},{33,1},{2,34},{34,2},{3,35},{35,3},{4,36},{36... | collective-permute-start | bytes 1376264 | tf_op jit(solution)/shard_map/ppermute | solution.py:433
  95.2 2.0 %fetch.1 = (bf16[1024,256]{1,0:T(8,128)(2,1)S(1)}, bf16[512,1792]{1,0:T(8,128)(2,1)S(1)}, bf16[512,1792]{1,0:T(8,128)(2,1)S(1)}) custom-call(f32[1024,128]{1,0:T(8,128)S(1)} %get-tuple-element.35.basis_ref, bf16[1024,1792]{1,0:T(8,128)(2,1)} %bitcast.7, bf16[1024,1792]{1,0:T(8,128)(2,1)} %bitcast.12), custom_call_target="tpu_custom_call" | custom-call | flops 1000000 | bytes 10000000 | tf_op jit(solution)/shard_map/fetch/pallas_call | solution.py:358
  97.3 5.6 %residue.1 = (f32[1792,128]{1,0:T(8,128)}, bf16[1024,1792]{1,0:T(8,128)(2,1)}) custom-call(f32[16,56,128]{2,1,0:T(8,128)S(1)} %all-to-all-done.3.own_ref, f32[16,56,128]{2,1,0:T(8,128)S(1)} %collective-permute-done.9.other_ref, bf16[1024,256]{1,0:T(8,128)(2,1)S(1)} %get-tuple-element.36.q12, f32[128,128]{1,0:T(8,128)S(1)} %get-tuple-element.37.inv_ref, ...), custom_call_target="tpu_custom_call" | custom-call | tf_op jit(solution)/shard_map/residue/pallas_call | solution.py:411
  (10 shorter events, 0.0 us)
Async XLA Ops:
  6.9 4.5 %collective-permute-start = (f32[512,128]{1,0:T(8,128)S(1)}, f32[512,128]{1,0:T(8,128)S(1)}, u32[]{:S(2)}, u32[]{:S(2)}) collective-permute-start(f32[512,128]{1,0:T(8,128)S(1)} %get-tuple-element.23), channel_id=1, source_target_pairs={{0,32},{32,0},{1,33},{33,1},{2,34},{34,2},{3,35},{35,3},{4,36},{36... | collective-permute-start | bytes 786440 | tf_op jit(solution)/shard_map/ppermute | solution.py:433
  30.4 21.8 %copy-start = (bf16[1,1024,1792]{2,1,0:T(8,128)(2,1)S(1)}, bf16[1,1024,1792]{2,1,0:T(8,128)(2,1)}, u32[]{:S(2)}) copy-start(bf16[1,1024,1792]{2,1,0:T(8,128)(2,1)} %param.3) | copy-start | bytes 11010052
  30.4 21.9 %copy-start.1 = (bf16[1,1024,1792]{2,1,0:T(8,128)(2,1)S(1)}, bf16[1,1024,1792]{2,1,0:T(8,128)(2,1)}, u32[]{:S(2)}) copy-start(bf16[1,1024,1792]{2,1,0:T(8,128)(2,1)} %param.4) | copy-start | bytes 11010052
  46.9 4.8 %collective-permute-start.1 = (f32[512,128]{1,0:T(8,128)S(1)}, f32[512,128]{1,0:T(8,128)S(1)}, u32[]{:S(2)}, u32[]{:S(2)}) collective-permute-start(f32[512,128]{1,0:T(8,128)S(1)} %bitcast.16), channel_id=1, source_target_pairs={{0,32},{32,0},{1,33},{33,1},{2,34},{34,2},{3,35},{35,3},{4,36},{36... | collective-permute-start | bytes 786440 | tf_op jit(solution)/shard_map/ppermute | solution.py:433
  54.0 5.9 %collective-permute-start.2 = (f32[896,128]{1,0:T(8,128)S(1)}, f32[896,128]{1,0:T(8,128)S(1)}, u32[]{:S(2)}, u32[]{:S(2)}) collective-permute-start(f32[896,128]{1,0:T(8,128)S(1)} %factor_send.1), channel_id=1, source_target_pairs={{0,32},{32,0},{1,33},{33,1},{2,34},{34,2},{3,35},{35,3},{4,36},{36... | collective-permute-start | bytes 1376264 | tf_op jit(solution)/shard_map/ppermute | solution.py:433
  54.5 10.6 %collective-permute-start.5 = (f32[128,128]{1,0:T(8,128)S(1)}, f32[128,128]{1,0:T(8,128)S(1)}, u32[]{:S(2)}, u32[]{:S(2)}) collective-permute-start(f32[128,128]{1,0:T(8,128)S(1)} %get-tuple-element.26.refs_0_), channel_id=1, source_target_pairs={{0,24},{8,0},{16,8},{24,16},{1,25},{9,1},{17,9},{25,17},{2,26},{10... | collective-permute-start | bytes 196616 | tf_op jit(solution)/shard_map/ppermute | solution.py:438
  57.0 8.1 %collective-permute-start.4 = (f32[128,128]{1,0:T(8,128)S(1)}, f32[128,128]{1,0:T(8,128)S(1)}, u32[]{:S(2)}, u32[]{:S(2)}) collective-permute-start(f32[128,128]{1,0:T(8,128)S(1)} %get-tuple-element.26.refs_0_), channel_id=1, source_target_pairs={{0,16},{8,24},{16,0},{24,8},{1,17},{9,25},{17,1},{25,9},{2,18},{10... | collective-permute-start | bytes 196616 | tf_op jit(solution)/shard_map/ppermute | solution.py:438
  57.5 7.6 %collective-permute-start.3 = (f32[128,128]{1,0:T(8,128)S(1)}, f32[128,128]{1,0:T(8,128)S(1)}, u32[]{:S(2)}, u32[]{:S(2)}) collective-permute-start(f32[128,128]{1,0:T(8,128)S(1)} %get-tuple-element.26.refs_0_), channel_id=1, source_target_pairs={{0,8},{8,16},{16,24},{24,0},{1,9},{9,17},{17,25},{25,1},{2,10},{10... | collective-permute-start | bytes 196616 | tf_op jit(solution)/shard_map/ppermute | solution.py:438
  60.7 14.0 %all-to-all-start.2 = ((f32[16,56,128]{2,1,0:T(8,128)}), f32[16,56,128]{2,1,0:T(8,128)S(1)}, u32[]{:S(2)}, u32[]{:S(2)}) async-start(f32[16,56,128]{2,1,0:T(8,128)} %bitcast.4), calls=%async_computation.2 | async-start | bytes 917504 | tf_op jit(solution)/shard_map/all_to_all | solution.py:456
  74.7 7.9 %collective-permute-start.8 = (f32[128,128]{1,0:T(8,128)S(1)}, f32[128,128]{1,0:T(8,128)S(1)}, u32[]{:S(2)}, u32[]{:S(2)}) collective-permute-start(f32[128,128]{1,0:T(8,128)S(1)} %get-tuple-element.30.refs_0_), channel_id=1, source_target_pairs={{0,24},{8,0},{16,8},{24,16},{1,25},{9,1},{17,9},{25,17},{2,26},{10... | collective-permute-start | bytes 196616 | tf_op jit(solution)/shard_map/ppermute | solution.py:438
  75.5 7.0 %collective-permute-start.7 = (f32[128,128]{1,0:T(8,128)S(1)}, f32[128,128]{1,0:T(8,128)S(1)}, u32[]{:S(2)}, u32[]{:S(2)}) collective-permute-start(f32[128,128]{1,0:T(8,128)S(1)} %get-tuple-element.30.refs_0_), channel_id=1, source_target_pairs={{0,16},{8,24},{16,0},{24,8},{1,17},{9,25},{17,1},{25,9},{2,18},{10... | collective-permute-start | bytes 196616 | tf_op jit(solution)/shard_map/ppermute | solution.py:438
  76.9 5.7 %collective-permute-start.6 = (f32[128,128]{1,0:T(8,128)S(1)}, f32[128,128]{1,0:T(8,128)S(1)}, u32[]{:S(2)}, u32[]{:S(2)}) collective-permute-start(f32[128,128]{1,0:T(8,128)S(1)} %get-tuple-element.30.refs_0_), channel_id=1, source_target_pairs={{0,8},{8,16},{16,24},{24,0},{1,9},{9,17},{17,25},{25,1},{2,10},{10... | collective-permute-start | bytes 196616 | tf_op jit(solution)/shard_map/ppermute | solution.py:438
  77.7 13.4 %all-to-all-start.3 = ((f32[16,56,128]{2,1,0:T(8,128)}), f32[16,56,128]{2,1,0:T(8,128)S(1)}, u32[]{:S(2)}, u32[]{:S(2)}) async-start(f32[16,56,128]{2,1,0:T(8,128)} %total_pieces.1), calls=%async_computation.3 | async-start | bytes 917504 | tf_op jit(solution)/shard_map/all_to_all | solution.py:460
  91.2 6.1 %collective-permute-start.9 = (f32[16,56,128]{2,1,0:T(8,128)S(1)}, f32[16,56,128]{2,1,0:T(8,128)S(1)}, u32[]{:S(2)}, u32[]{:S(2)}) collective-permute-start(f32[16,56,128]{2,1,0:T(8,128)S(1)} %all-to-all-done.3.own_ref), channel_id=1, source_target_pairs={{0,32},{32,0},{1,33},{33,1},{2,34},{34,2},{3,35},{35,3},{4,36},{36... | collective-permute-start | bytes 1376264 | tf_op jit(solution)/shard_map/ppermute | solution.py:433

commit v4 on v3

v4 whole, which is shorter than its diff:
```python
import functools

import jax
import jax.numpy as jnp
from jax import lax
from jax.experimental import pallas as pl
from jax.experimental.pallas import tpu as pltpu
from jax.sharding import Mesh, PartitionSpec as P

F32, BF16 = jnp.float32, jnp.bfloat16
RANK = 128
ROWS = 256
COLS = 256
GROUP = 8
VMEM_LIMIT = 24 * 1024 * 1024
TOP = 384
FETCH_LIMIT = 51000000
RESIDUE_LIMIT = 51000000
STREAM_LIMIT = 55500000
NT = (((1,), (1,)), ((), ()))
NN = (((1,), (0,)), ((), ()))


def mm(a, b, dims=NN):
    return lax.dot_general(a, b, dims, preferred_element_type=F32)


def mm32(a, b, dims=NN):
    return lax.dot_general(a, b, dims, precision=lax.Precision.HIGHEST, preferred_element_type=F32)


def split3(x):
    hi = x.astype(BF16)
    rest = x - hi.astype(F32)
    mid = rest.astype(BF16)
    low = (rest - mid.astype(F32)).astype(BF16)
    return hi, mid, low


VMEM_SPEC = pl.BlockSpec(memory_space=pltpu.VMEM)
HBM_SPEC = pl.BlockSpec(memory_space=pltpu.HBM)


def params(limit=VMEM_LIMIT):
    return pltpu.CompilerParams(vmem_limit_bytes=limit)


def chunks_of(first, last, tail):
    blocks = []
    while first < last:
        size = min(ROWS, last - first)
        if tail and first + size == last and size == ROWS:
            size = ROWS // 2
        blocks.append((first, size))
        first += size
    return blocks


def sketch_kernel(g_hbm, e_hbm, p_hbm, keep_ref, send_ref, both_ref, p_ref, p12, p3, sems):
    n = g_hbm.shape[0]
    steps, ahead = n // ROWS, 2
    core = lax.axis_index("core")

    def load(i):
        rows = pl.ds(i * ROWS, ROWS)
        return (
            pltpu.make_async_copy(g_hbm.at[rows], both_ref.at[pl.ds(2 * i * ROWS, ROWS)], sems.at[2 * i]),
            pltpu.make_async_copy(e_hbm.at[rows], both_ref.at[pl.ds((2 * i + 1) * ROWS, ROWS)], sems.at[2 * i + 1]),
        )

    half = p_ref.shape[0] // 2
    halves = [pl.ds(0, half), pl.ds(half, half)]
    firsts = [
        pltpu.make_async_copy(p_hbm.at[rows], p_ref.at[rows], sems.at[2 * steps + k])
        for k, rows in enumerate(halves)
    ]
    for copy in firsts:
        copy.start()
    copies = [load(i) for i in range(steps)]
    for i in range(ahead):
        copies[i][0].start()
        copies[i][1].start()
    for copy, rows in zip(firsts, halves):
        copy.wait()
        hi, mid, low = split3(p_ref[rows, :])
        p12[rows, :RANK] = hi
        p12[rows, RANK:] = mid
        p3[rows, :] = low
    for i in range(steps):
        copies[i][0].wait()
        copies[i][1].wait()
        if i + ahead < steps:
            copies[i + ahead][0].start()
            copies[i + ahead][1].start()
        stacked = both_ref[pl.ds(2 * i * ROWS, 2 * ROWS), :]
        wide = mm(stacked, p12[...])
        wide = wide[:ROWS] + wide[ROWS:]
        block = wide[:, :RANK] + wide[:, RANK:] + mm(stacked[:ROWS] + stacked[ROWS:], p3[...])
        half = i // (steps // 2)
        place = pl.ds((i - half * (steps // 2)) * ROWS, ROWS)

        @pl.when(core == half)
        def _():
            keep_ref[place, :] = block

        @pl.when(core != half)
        def _():
            send_ref[place, :] = block


def local_sketch(g, e, p):
    n, m = g.shape
    half = jax.ShapeDtypeStruct((n // 2, RANK), F32)
    return pl.pallas_call(
        sketch_kernel,
        in_specs=[HBM_SPEC] * 3,
        out_specs=[VMEM_SPEC] * 2,
        out_shape=[half, half],
        scratch_shapes=[
            pltpu.VMEM((2 * n, m), BF16),
            pltpu.VMEM((m, RANK), F32),
            pltpu.VMEM((m, 2 * RANK), BF16),
            pltpu.VMEM((m, RANK), BF16),
            pltpu.SemaphoreType.DMA((2 * (n // ROWS) + 2,)),
        ],
        compiler_params=params(STREAM_LIMIT),
        name="local_sketch",
    )(g, e, p)


def total_kernel(parts_ref, out_ref):
    total = parts_ref[0]
    for i in range(1, parts_ref.shape[0]):
        total = total + parts_ref[i]
    for i in range(parts_ref.shape[0]):
        out_ref[i] = total


def total_for_all(parts):
    return pl.pallas_call(
        total_kernel,
        out_shape=jax.ShapeDtypeStruct(parts.shape, F32),
        compiler_params=params(),
        cost_estimate=pl.CostEstimate(flops=2 * 10**10, bytes_accessed=5 * 10**7, transcendentals=0),
        name="sketch_total",
    )(parts)


def tiles_of(width):
    return [(start, min(COLS, width - start)) for start in range(0, width, COLS)]


def factor_tile(s12_ref, s3_ref, g_ref, e_ref, side, width, start, size):
    cols = pl.ds(pl.multiple_of(side * width + start, RANK), size)
    g, e = g_ref[:, cols], e_ref[:, cols]
    both = mm(s12_ref[...], g) + mm(s12_ref[...], e)
    return (both[:RANK] + both[RANK:] + mm(s3_ref[...], g + e)).T


def wide_nt(x, w):
    x1, x2, x3 = split3(x)
    w1, w2, w3 = split3(w)
    front = jnp.concatenate(
        [jnp.concatenate([w1, w1], axis=1), jnp.concatenate([w2, w2], axis=1)], axis=0
    )
    both = mm(jnp.concatenate([x1, x2], axis=1), front, NT)
    rest = mm(jnp.concatenate([x1, x3], axis=1), jnp.concatenate([w3, w1], axis=1), NT)
    return both[:, :RANK] + (both[:, RANK:] + rest)


def square_nt(hi_mid, low):
    square = mm(hi_mid, hi_mid, NT)
    cross = mm(hi_mid[:RANK], low, NT)
    return (
        square[:RANK, :RANK] + square[RANK:, RANK:]
        + (square[:RANK, RANK:] + square[RANK:, :RANK])
        + (cross + cross.T)
    )


def prepare_kernel(own_ref, other_ref, sketch_ref, s12_ref, s3_ref, gram_ref):
    core = lax.axis_index("core")
    half = own_ref.shape[0]
    sketch_ref[pl.ds(pl.multiple_of(core * half, half), half), :] = own_ref[...]
    sketch_ref[pl.ds(pl.multiple_of((1 - core) * half, half), half), :] = other_ref[...]
    hi, mid, low = split3(sketch_ref[...].T)
    s12_ref[:RANK, :] = hi
    s12_ref[RANK:, :] = mid
    s3_ref[...] = low
    gram_ref[...] = square_nt(s12_ref[...], low)


def prepare(own, other):
    n = 2 * own.shape[0]
    return pl.pallas_call(
        prepare_kernel,
        out_shape=[
            jax.ShapeDtypeStruct((n, RANK), F32),
            jax.ShapeDtypeStruct((2 * RANK, n), BF16),
            jax.ShapeDtypeStruct((RANK, n), BF16),
            jax.ShapeDtypeStruct((RANK, RANK), F32),
        ],
        compiler_params=params(),
        name="prepare",
    )(own, other)


def factor_send_kernel(s12_ref, s3_ref, g_ref, e_ref, send_ref):
    side, width = 1 - lax.axis_index("core"), send_ref.shape[0]
    for start, size in tiles_of(width):
        send_ref[start : start + size, :] = factor_tile(s12_ref, s3_ref, g_ref, e_ref, side, width, start, size)


def factor_keep_kernel(s12_ref, s3_ref, g_ref, e_ref, got_ref, out_hbm, sum_ref, sems):
    side, width = lax.axis_index("core"), got_ref.shape[0]
    copies = []
    for k, (start, size) in enumerate(tiles_of(width)):
        rows = pl.ds(start, size)
        sum_ref[rows, :] = got_ref[rows, :] + factor_tile(s12_ref, s3_ref, g_ref, e_ref, side, width, start, size)
        copies.append(pltpu.make_async_copy(sum_ref.at[rows], out_hbm.at[rows], sems.at[k]))
        copies[-1].start()
    for copy in copies:
        copy.wait()


def factor_cost():
    return pl.CostEstimate(flops=10**9, bytes_accessed=8 * 10**6, transcendentals=0)


def factor_send(s12, s3, g, e):
    return pl.pallas_call(
        factor_send_kernel,
        out_shape=jax.ShapeDtypeStruct((g.shape[1] // 2, RANK), F32),
        compiler_params=params(),
        cost_estimate=factor_cost(),
        name="factor_send",
    )(s12, s3, g, e)


def factor_keep(s12, s3, g, e, got):
    return pl.pallas_call(
        factor_keep_kernel,
        in_specs=[VMEM_SPEC] * 5,
        out_specs=HBM_SPEC,
        out_shape=jax.ShapeDtypeStruct(got.shape, F32),
        scratch_shapes=[
            pltpu.VMEM(got.shape, F32),
            pltpu.SemaphoreType.DMA((len(tiles_of(got.shape[0])),)),
        ],
        compiler_params=params(),
        cost_estimate=factor_cost(),
        name="factor_keep",
    )(s12, s3, g, e, got)


def sum_in_order(parts, slots, out_ref):
    count = len(parts)
    place = lax.axis_index("fsdp")
    for k in range(count):
        slots[lax.rem(place + count - k, count)] = parts[k][...]
    total = slots[0]
    for k in range(1, count):
        total = total + slots[k]
    out_ref[...] = total


def across(tile, lane):
    return jnp.broadcast_to(tile[:, lane : lane + 1], tile.shape)


def down(tile, row):
    return jnp.broadcast_to(tile[row : row + 1, :], tile.shape)


def tree_sum(terms):
    while len(terms) > 1:
        terms = [terms[i] + terms[i + 1] for i in range(0, len(terms), 2)]
    return terms[0]


def invert_cholesky(a_ref, b_ref, out_ref):
    tiles = RANK // 8
    lane = lax.broadcasted_iota(jnp.int32, (8, RANK), 1)
    row = lax.broadcasted_iota(jnp.int32, (8, RANK), 0)
    for t in range(tiles):
        b_ref[8 * t : 8 * t + 8, :] = jnp.where(lane == row + 8 * t, 1.0, 0.0)
    for first in range(0, RANK, GROUP):
        t, skip = first // 8, first % 8
        here = slice(8 * t, 8 * t + 8)
        a_tile, b_tile = a_ref[here, :], b_ref[here, :]
        columns = [across(a_tile, first + k) for k in range(GROUP)]
        value = {(i, k): down(columns[k], skip + i) for k in range(GROUP) for i in range(k, GROUP)}
        factor, inverse, root = {}, [], []
        for k in range(GROUP):
            inverse.append(1.0 / value[k, k])
            root.append(lax.rsqrt(value[k, k]))
            for i in range(k + 1, GROUP):
                factor[i, k] = value[i, k] * inverse[k]
            for j in range(k + 1, GROUP):
                for i in range(j, GROUP):
                    value[i, j] = value[i, j] - factor[j, k] * value[i, k]
        a_rows = [down(a_tile, skip + k) for k in range(GROUP)]
        b_rows = [down(b_tile, skip + k) for k in range(GROUP)]
        for k in range(GROUP):
            for i in range(k + 1, GROUP):
                a_rows[i] = a_rows[i] - factor[i, k] * a_rows[k]
                b_rows[i] = b_rows[i] - factor[i, k] * b_rows[k]
        for k in range(GROUP):
            out_ref[first + k : first + k + 1, :] = (b_rows[k] * root[k])[:1, :]
        a_rows = [a_rows[k] * inverse[k] for k in range(GROUP)]
        b_rows = [b_rows[k] * inverse[k] for k in range(GROUP)]
        for u in range(t if skip + GROUP < 8 else t + 1, tiles):
            there = slice(8 * u, 8 * u + 8)
            a_low, b_low = a_ref[there, :], b_ref[there, :]
            left = [across(a_low, first + k) for k in range(GROUP)]
            for k in range(GROUP):
                for i in range(k + 1, GROUP):
                    left[i] = left[i] - factor[i, k] * left[k]
            a_ref[there, :] = a_low - tree_sum([left[k] * a_rows[k] for k in range(GROUP)])
            b_ref[there, :] = b_low - tree_sum([left[k] * b_rows[k] for k in range(GROUP)])


def pieces_kernel(parts_ref, out_ref):
    count = parts_ref.shape[0]
    total = parts_ref[0]
    for i in range(1, count):
        total = total + parts_ref[i]
    for i in range(count):
        out_ref[i] = total


def total_pieces(parts):
    return pl.pallas_call(
        pieces_kernel,
        out_shape=jax.ShapeDtypeStruct(parts.shape, F32),
        compiler_params=params(),
        name="total_pieces",
    )(parts)


def first_pass_kernel(*refs):
    grams, (sketch_ref, basis_ref, inv_ref, gram_ref, a_ref, b_ref, slots) = refs[:-7], refs[-7:]
    sum_in_order(grams, slots, a_ref)
    invert_cholesky(a_ref, b_ref, inv_ref)
    basis = wide_nt(sketch_ref[...], inv_ref[...])
    basis_ref[...] = basis
    hi, mid, low = split3(basis.T)
    gram_ref[...] = square_nt(jnp.concatenate([hi, mid], axis=0), low)


def pass_scratch(count):
    return [pltpu.VMEM((RANK, RANK), F32)] * 2 + [pltpu.VMEM((count, RANK, RANK), F32)]


def pass_cost():
    return pl.CostEstimate(flops=4 * 10**9, bytes_accessed=2 * 10**7, transcendentals=0)


def first_pass(grams, sketch):
    square = jax.ShapeDtypeStruct((RANK, RANK), F32)
    return pl.pallas_call(
        first_pass_kernel,
        out_shape=[jax.ShapeDtypeStruct(sketch.shape, F32), square, square],
        scratch_shapes=pass_scratch(len(grams)),
        compiler_params=params(),
        cost_estimate=pass_cost(),
        name="first_pass",
    )(*grams, sketch)


def second_pass_kernel(*refs):
    grams, (basis_one_ref, inv_one_ref, basis_ref, inv_ref, two_ref, a_ref, b_ref, slots) = refs[:-8], refs[-8:]
    sum_in_order(grams, slots, a_ref)
    invert_cholesky(a_ref, b_ref, two_ref)
    basis_ref[...] = wide_nt(basis_one_ref[...], two_ref[...])
    inv_ref[...] = mm32(two_ref[...], inv_one_ref[...])


def second_pass(grams, basis_one, inv_one):
    return pl.pallas_call(
        second_pass_kernel,
        out_shape=[
            jax.ShapeDtypeStruct(basis_one.shape, F32),
            jax.ShapeDtypeStruct(inv_one.shape, F32),
        ],
        scratch_shapes=[pltpu.VMEM((RANK, RANK), F32)] + pass_scratch(len(grams)),
        compiler_params=params(),
        cost_estimate=pass_cost(),
        name="second_pass",
    )(*grams, basis_one, inv_one)


def row_loads(g_hbm, e_hbm, g_ref, e_ref, sems, blocks):
    loads = []
    for k, (start, size) in enumerate(blocks):
        here, there = pl.ds(start - blocks[0][0], size), pl.ds(start, size)
        loads.append(pltpu.make_async_copy(g_hbm.at[there], g_ref.at[here], sems.at[2 * k]))
        loads.append(pltpu.make_async_copy(e_hbm.at[there], e_ref.at[here], sems.at[2 * k + 1]))
    return loads


def fetch_kernel(basis_ref, g_hbm, e_hbm, q3_ref, g_ref, e_ref, sems):
    loads = row_loads(g_hbm, e_hbm, g_ref, e_ref, sems, chunks_of(0, g_ref.shape[0], False))
    for load in loads:
        load.start()
    basis = basis_ref[...]
    hi = basis.astype(BF16)
    q3_ref[:, :RANK] = hi
    q3_ref[:, RANK : 2 * RANK] = (basis - hi.astype(F32)).astype(BF16)
    q3_ref[:, 2 * RANK :] = hi
    for load in loads:
        load.wait()


def fetch(basis, g, e, top):
    n, m = g.shape
    rows = jax.ShapeDtypeStruct((top, m), BF16)
    return pl.pallas_call(
        fetch_kernel,
        in_specs=[VMEM_SPEC, HBM_SPEC, HBM_SPEC],
        out_specs=[VMEM_SPEC] * 3,
        out_shape=[jax.ShapeDtypeStruct((n, 3 * RANK), BF16), rows, rows],
        scratch_shapes=[pltpu.SemaphoreType.DMA((2 * len(chunks_of(0, top, False)),))],
        compiler_params=params(FETCH_LIMIT),
        cost_estimate=pl.CostEstimate(flops=10**6, bytes_accessed=10**7, transcendentals=0),
        name="fetch",
    )(basis, g, e)


def residue_kernel(replicas, own_ref, other_ref, q3, inv_ref, g_top, e_top, g_hbm, e_hbm, right_hbm, new_hbm, halves, right3, right_ref, new_ref, g_ref, e_ref, in_sems, out_sems):
    core = lax.axis_index("core")
    count, piece = own_ref.shape[0], own_ref.shape[1]
    n, m = new_ref.shape
    top = g_top.shape[0]
    early, late = chunks_of(0, top, False), chunks_of(top, n, True)
    loads = row_loads(g_hbm, e_hbm, g_ref, e_ref, in_sems, late)
    for load in loads:
        load.start()
    for i in range(count):
        halves[pl.ds(pl.multiple_of(core * (m // 2), 8) + i * piece, piece), :] = own_ref[i]
        halves[pl.ds(pl.multiple_of((1 - core) * (m // 2), 8) + i * piece, piece), :] = other_ref[i]
    right = wide_nt(halves[...], inv_ref[...]) * (1.0 / replicas)
    right_ref[...] = right
    right_copy = pltpu.make_async_copy(right_ref, right_hbm, out_sems.at[len(early) + len(late)])
    right_copy.start()
    hi = right.astype(BF16)
    right3[:, :RANK] = hi
    right3[:, RANK : 2 * RANK] = hi
    right3[:, 2 * RANK :] = (right - hi.astype(F32)).astype(BF16)
    copies = []
    for k, (first, size) in enumerate(early + late):
        rows = pl.ds(first, size)
        g_in, e_in, there = g_top, e_top, rows
        if first >= top:
            g_in, e_in, there = g_ref, e_ref, pl.ds(first - top, size)
            loads[2 * (k - len(early))].wait()
            loads[2 * (k - len(early)) + 1].wait()
        for start in range(0, m, COLS):
            cols = pl.ds(start, COLS)
            update = mm(q3[rows, :], right3[cols, :], NT)
            new_ref[rows, cols] = (g_in[there, cols].astype(F32) + e_in[there, cols].astype(F32) - update).astype(BF16)
        copies.append(pltpu.make_async_copy(new_ref.at[rows], new_hbm.at[rows], out_sems.at[k]))
        copies[-1].start()
    for copy in copies:
        copy.wait()
    right_copy.wait()


def residue(own, other, q3, inv, g_top, e_top, g, e, replicas):
    n, m = g.shape
    top = g_top.shape[0]
    early, late = chunks_of(0, top, False), chunks_of(top, n, True)
    return pl.pallas_call(
        functools.partial(residue_kernel, replicas),
        in_specs=[VMEM_SPEC] * 6 + [HBM_SPEC] * 2,
        out_specs=[HBM_SPEC] * 2,
        out_shape=[jax.ShapeDtypeStruct((m, RANK), F32), jax.ShapeDtypeStruct((n, m), BF16)],
        scratch_shapes=[
            pltpu.VMEM((m, RANK), F32),
            pltpu.VMEM((m, 3 * RANK), BF16),
            pltpu.VMEM((m, RANK), F32),
            pltpu.VMEM((n, m), BF16),
            pltpu.VMEM((n - top, m), BF16),
            pltpu.VMEM((n - top, m), BF16),
            pltpu.SemaphoreType.DMA((2 * len(late),)),
            pltpu.SemaphoreType.DMA((len(early) + len(late) + 1,)),
        ],
        compiler_params=params(RESIDUE_LIMIT),
        name="residue",
    )(own, other, q3, inv, g_top, e_top, g, e)


def swap(x):
    return lax.ppermute(x, "core", [(0, 1), (1, 0)])


def round_fsdp(x, count):
    return [x] + [
        lax.ppermute(x, "fsdp", [(i, (i + k) % count) for i in range(count)]) for k in range(1, count)
    ]


def shards(gradients, errors, start_factor):
    g, e = gradients[0], errors[0]
    n = g.shape[0]
    ny, nx, nz = lax.axis_size("y"), lax.axis_size("fsdp"), lax.axis_size("tensor")
    keep, send = local_sketch(g, e, start_factor)
    pieces = (keep + swap(send)).reshape(ny * nz, -1, RANK)
    pieces = lax.all_to_all(pieces, ("y", "tensor"), 0, 0)
    own = lax.all_to_all(total_for_all(pieces), ("y", "tensor"), 0, 0).reshape(n // 2, RANK)
    sketch, s12, s3, gram = prepare(own, swap(own))
    grams = round_fsdp(gram, nx)
    got = swap(factor_send(s12, s3, g, e))
    parts = factor_keep(s12, s3, g, e, got).reshape(ny * nx, -1, RANK)
    parts = lax.all_to_all(parts, ("y", "fsdp"), 0, 0)
    basis_one, inv_one, gram = first_pass(grams, sketch)
    parts, _ = lax.optimization_barrier((parts, gram))
    grams = round_fsdp(gram, nx)
    own = lax.all_to_all(total_pieces(parts), ("y", "fsdp"), 0, 0)
    basis, inv = second_pass(grams, basis_one, inv_one)
    own, basis = lax.optimization_barrier((own, basis))
    other = swap(own)
    q3, g_top, e_top = fetch(basis, g, e, TOP)
    right_factor, new_errors = residue(own, other, q3, inv, g_top, e_top, g, e, 2 * ny)
    return (right_factor, new_errors[None])


def solution(mesh):
    shape = mesh.devices.shape
    split = Mesh(
        mesh.devices.reshape(shape[0] // 2, 2, *shape[1:]), ("y", "core", "fsdp", "tensor")
    )
    big = P(("y", "core"), "fsdp", "tensor")
    return jax.shard_map(
        shards,
        mesh=split,
        in_specs=(big, big, P("tensor", None)),
        out_specs=(P("tensor", None), big),
        check_vma=False,
    )
```

time: 103 us -> 101 us (0.981)
  waiting for transfers between devices: 8.48 us -> 5.72 us
  starting transfers between devices: 26.5 us -> 28.8 us
  Pallas kernels: 30.9 us -> 29.7 us
    all_to_all x1, waiting for transfers between devices: 2.94 us -> 0.01 us  [shards(): parts = lax.all_to_all(parts, ('y', 'fsdp'), 0, 0)]
    ppermute x6, starting transfers between devices: 5.83 us -> 7.43 us  [round_fsdp(): lax.ppermute(x, 'fsdp', [(i, (i + k) % count) for i in range(count)])]
    all_to_all x1, starting transfers between devices: 4.84 us -> 5.89 us  [shards(): own = lax.all_to_all(total_pieces(parts), ('y', 'fsdp'), 0, 0)]
  transfers between devices with their start and end apart: 12 -> 12, of which waited for: 4 -> 3; matrix products, arithmetic and copies ran while one was open for 1% -> 0% of each run, Pallas kernels for 16% -> 16%
where the time goes in v4:
time: 101 us
  blocking collectives  35.4 us (35%)
  Pallas kernels  29.7 us (29%)
  starting transfers between devices  28.8 us (29%)
  waiting for transfers between devices  5.72 us (6%)
    all_to_all x1, blocking collectives, shards(): pieces = lax.all_to_all(pieces, ('y', 'tensor'), 0, 0)  18.9 us
    all_to_all x1, blocking collectives, shards(): lax.all_to_all(total_for_all(pieces), ('y', 'tensor'), 0, 0)  16.4 us
    ppermute x4, starting transfers between devices, swap(): return lax.ppermute(x, 'core', [(0, 1), (1, 0)])  11.1 us
    ppermute x6, starting transfers between devices, round_fsdp(): lax.ppermute(x, 'fsdp', [(i, (i + k) % count) for i in range(count)])  7.43 us
    pallas_call x1, Pallas kernels, local_sketch(): pl.pallas_call(sketch_kernel, in_specs=[HBM_SPEC] * 3, out_specs=[VMEM_SP...  6.3 us
    pallas_call x1, Pallas kernels, first_pass(): pl.pallas_call(first_pass_kernel, out_shape=[jax.ShapeDtypeStruct(sketch....  5.93 us
    all_to_all x1, starting transfers between devices, shards(): own = lax.all_to_all(total_pieces(parts), ('y', 'fsdp'), 0, 0)  5.89 us
    pallas_call x1, Pallas kernels, second_pass(): pl.pallas_call(second_pass_kernel, out_shape=[jax.ShapeDtypeStruct(basis_...  5.19 us
  transfers between devices with their start and end apart: 12, of which 3 were waited for; matrix products, arithmetic and copies ran while one was open for 0% of the time, Pallas kernels for 16%

profile of v4, /device:TPU:1, one launch (start us, length us, event | category | flops | bytes accessed | tf_op | source)
XLA Modules:
  0.0 100.7 jit_solution(435040087061876613)
XLA Ops:
  0.6 6.3 %local_sketch.1 = (f32[512,128]{1,0:T(8,128)S(1)}, f32[512,128]{1,0:T(8,128)S(1)}) custom-call(bf16[1024,1792]{1,0:T(8,128)(2,1)} %bitcast.6, bf16[1024,1792]{1,0:T(8,128)(2,1)} %bitcast.11, f32[1792,128]{1,0:T(8,128)} %p_hbm.1), custom_call_target="tpu_custom_call" | custom-call | tf_op jit(solution)/shard_map/local_sketch/pallas_call | solution.py:114
  6.9 3.3 %collective-permute-start = (f32[512,128]{1,0:T(8,128)S(1)}, f32[512,128]{1,0:T(8,128)S(1)}, u32[]{:S(2)}, u32[]{:S(2)}) collective-permute-start(f32[512,128]{1,0:T(8,128)S(1)} %get-tuple-element.22), channel_id=1, source_target_pairs={{0,32},{32,0},{1,33},{33,1},{2,34},{34,2},{3,35},{35,3},{4,36},{36... | collective-permute-start | bytes 786440 | tf_op jit(solution)/shard_map/ppermute | solution.py:494
  10.3 1.2 %collective-permute-done = f32[512,128]{1,0:T(8,128)S(1)} collective-permute-done((f32[512,128]{1,0:T(8,128)S(1)}, f32[512,128]{1,0:T(8,128)S(1)}, u32[]{:S(2)}, u32[]{:S(2)}) %collective-permute-start) | collective-permute-done | bytes 262176 | tf_op jit(solution)/shard_map/ppermute | solution.py:494
  11.5 18.9 %all_to_all.20.parts_ref = f32[32,16,128]{2,1,0:T(8,128)S(1)} all-to-all(f32[32,16,128]{2,1,0:T(8,128)S(1)} %bitcast.18), channel_id=1, replica_groups=mesh['y'=4,'core'=2,'fsdp'=4,'tensor'=8] {'y','tensor'}, dimensions={0} | all-to-all | bytes 524288 | tf_op jit(solution)/shard_map/all_to_all | solution.py:509
  30.4 0.1 sketch_total.1
  30.5 16.4 %all_to_all.21 = f32[32,16,128]{2,1,0:T(8,128)S(1)} all-to-all(f32[32,16,128]{2,1,0:T(8,128)S(1)} %sketch_total.1), channel_id=1, replica_groups=mesh['y'=4,'core'=2,'fsdp'=4,'tensor'=8] {'y','tensor'}, dimensions={0} | all-to-all | bytes 524288 | tf_op jit(solution)/shard_map/all_to_all | solution.py:510
  46.9 3.6 %collective-permute-start.1 = (f32[512,128]{1,0:T(8,128)S(1)}, f32[512,128]{1,0:T(8,128)S(1)}, u32[]{:S(2)}, u32[]{:S(2)}) collective-permute-start(f32[512,128]{1,0:T(8,128)S(1)} %bitcast.16), channel_id=1, source_target_pairs={{0,32},{32,0},{1,33},{33,1},{2,34},{34,2},{3,35},{35,3},{4,36},{36... | collective-permute-start | bytes 786440 | tf_op jit(solution)/shard_map/ppermute | solution.py:494
  50.5 1.2 %collective-permute-done.1.other_ref = f32[512,128]{1,0:T(8,128)S(1)} collective-permute-done((f32[512,128]{1,0:T(8,128)S(1)}, f32[512,128]{1,0:T(8,128)S(1)}, u32[]{:S(2)}, u32[]{:S(2)}) %collective-permute-start.1) | collective-permute-done | bytes 262176 | tf_op jit(solution)/shard_map/ppermute | solution.py:494
  51.7 0.6 prepare.1
  52.3 1.7 %factor_send.1 = f32[896,128]{1,0:T(8,128)S(1)} custom-call(bf16[256,1024]{1,0:T(8,128)(2,1)S(1)} %get-tuple-element.23.s12_ref, bf16[128,1024]{1,0:T(8,128)(2,1)S(1)} %get-tuple-element.24.s3_ref, bf16[1024,1792]{1,0:T(8,128)(2,1)S(1)} %bitcast.9, bf16[1024,1792]{1,0:T(8,128)(2,1)S(1)} %bitcast.14), custom_call_target="tpu_custom_call" | custom-call | flops 1000000000 | bytes 8000000 | tf_op jit(solution)/shard_map/factor_send/pallas_call | solution.py:231
  54.0 0.5 collective-permute-start.2
  54.5 2.5 %collective-permute-start.5 = (f32[128,128]{1,0:T(8,128)S(1)}, f32[128,128]{1,0:T(8,128)S(1)}, u32[]{:S(2)}, u32[]{:S(2)}) collective-permute-start(f32[128,128]{1,0:T(8,128)S(1)} %get-tuple-element.25.refs_0_), channel_id=1, source_target_pairs={{0,24},{8,0},{16,8},{24,16},{1,25},{9,1},{17,9},{25,17},{2,26},{10... | collective-permute-start | bytes 196616 | tf_op jit(solution)/shard_map/ppermute | solution.py:499
  57.0 0.5 collective-permute-start.4
  57.5 0.6 collective-permute-start.3
  58.1 0.0 collective-permute-done.2.got_ref
  58.1 2.4 %factor_keep.1 = f32[896,128]{1,0:T(8,128)} custom-call(bf16[256,1024]{1,0:T(8,128)(2,1)S(1)} %get-tuple-element.23.s12_ref, bf16[128,1024]{1,0:T(8,128)(2,1)S(1)} %get-tuple-element.24.s3_ref, bf16[1024,1792]{1,0:T(8,128)(2,1)S(1)} %bitcast.10, bf16[1024,1792]{1,0:T(8,128)(2,1)S(1)} %bitcast.15, f32[896,128]{1,0:T(8,128)S(1)} %collective-permute-done.2.got_ref), custom_call_target="tpu_custom_call" | custom-call | flops 1000000000 | bytes 8000000 | tf_op jit(solution)/shard_map/factor_keep/pallas_call | solution.py:241
  60.6 4.4 %all-to-all-start.2 = ((f32[16,56,128]{2,1,0:T(8,128)}), f32[16,56,128]{2,1,0:T(8,128)S(1)}, u32[]{:S(2)}, u32[]{:S(2)}) async-start(f32[16,56,128]{2,1,0:T(8,128)} %bitcast.4), calls=%async_computation.2 | async-start | bytes 917504 | tf_op jit(solution)/shard_map/all_to_all | solution.py:515
  65.0 0.0 collective-permute-done.5.refs_3_
  65.0 5.9 %first_pass.1 = (f32[1024,128]{1,0:T(8,128)S(1)}, f32[128,128]{1,0:T(8,128)S(1)}, f32[128,128]{1,0:T(8,128)S(1)}) custom-call(f32[128,128]{1,0:T(8,128)S(1)} %get-tuple-element.25.refs_0_, f32[128,128]{1,0:T(8,128)S(1)} %collective-permute-done.3.refs_1_, f32[128,128]{1,0:T(8,128)S(1)} %collective-permute-done.4.refs_2_, ...), custom_call_target="tpu_custom_call" | custom-call | flops 4000000000 | bytes 20000000 | tf_op jit(solution)/shard_map/first_pass/pallas_call | solution.py:361
  70.9 2.6 %collective-permute-start.8 = (f32[128,128]{1,0:T(8,128)S(1)}, f32[128,128]{1,0:T(8,128)S(1)}, u32[]{:S(2)}, u32[]{:S(2)}) collective-permute-start(f32[128,128]{1,0:T(8,128)S(1)} %get-tuple-element.27.refs_0_), channel_id=1, source_target_pairs={{0,24},{8,0},{16,8},{24,16},{1,25},{9,1},{17,9},{25,17},{2,26},{10... | collective-permute-start | bytes 196616 | tf_op jit(solution)/shard_map/ppermute | solution.py:499
  73.6 0.6 collective-permute-start.7
  74.2 0.6 collective-permute-start.6
  74.7 0.8 total_pieces.1
  75.6 5.9 %all-to-all-start.3 = ((f32[16,56,128]{2,1,0:T(8,128)}), f32[16,56,128]{2,1,0:T(8,128)S(1)}, u32[]{:S(2)}, u32[]{:S(2)}) async-start(f32[16,56,128]{2,1,0:T(8,128)} %total_pieces.1), calls=%async_computation.3 | async-start | bytes 917504 | tf_op jit(solution)/shard_map/all_to_all | solution.py:519
  81.5 0.0 collective-permute-done.8.refs_3_
  81.5 0.0 collective-permute-done.6.refs_1_
  81.5 5.2 %second_pass.1 = (f32[1024,128]{1,0:T(8,128)S(1)}, f32[128,128]{1,0:T(8,128)S(1)}) custom-call(f32[128,128]{1,0:T(8,128)S(1)} %get-tuple-element.27.refs_0_, f32[128,128]{1,0:T(8,128)S(1)} %collective-permute-done.6.refs_1_, f32[128,128]{1,0:T(8,128)S(1)} %collective-permute-done.7.refs_2_, f32[128,128]{1,0:T(8,128)S(1)} %collective-permute-done.8.refs_3_, ...), custom_call_target="tpu_custom_call" | custom-call | flops 4000000000 | bytes 20000000 | tf_op jit(solution)/shard_map/second_pass/pallas_call | solution.py:380
  86.7 3.4 %all-to-all-done.3.own_ref = f32[16,56,128]{2,1,0:T(8,128)S(1)} async-done(((f32[16,56,128]{2,1,0:T(8,128)}), f32[16,56,128]{2,1,0:T(8,128)S(1)}, u32[]{:S(2)}, u32[]{:S(2)}) %all-to-all-start.3) | async-done | bytes 458784 | tf_op jit(solution)/shard_map/all_to_all | solution.py:519
  90.1 3.7 %collective-permute-start.9 = (f32[16,56,128]{2,1,0:T(8,128)S(1)}, f32[16,56,128]{2,1,0:T(8,128)S(1)}, u32[]{:S(2)}, u32[]{:S(2)}) collective-permute-start(f32[16,56,128]{2,1,0:T(8,128)S(1)} %all-to-all-done.3.own_ref), channel_id=1, source_target_pairs={{0,32},{32,0},{1,33},{33,1},{2,34},{34,2},{3,35},{35,3},{4,36},{36... | collective-permute-start | bytes 1376264 | tf_op jit(solution)/shard_map/ppermute | solution.py:494
  93.8 1.7 %fetch.1 = (bf16[1024,384]{1,0:T(8,128)(2,1)S(1)}, bf16[384,1792]{1,0:T(8,128)(2,1)S(1)}, bf16[384,1792]{1,0:T(8,128)(2,1)S(1)}) custom-call(f32[1024,128]{1,0:T(8,128)S(1)} %get-tuple-element.33.basis_ref, bf16[1024,1792]{1,0:T(8,128)(2,1)} %bitcast.7, bf16[1024,1792]{1,0:T(8,128)(2,1)} %bitcast.12), custom_call_target="tpu_custom_call" | custom-call | flops 1000000 | bytes 10000000 | tf_op jit(solution)/shard_map/fetch/pallas_call | solution.py:418
  95.5 0.0 collective-permute-done.9.other_ref
  95.5 5.0 %residue.1 = (f32[1792,128]{1,0:T(8,128)}, bf16[1024,1792]{1,0:T(8,128)(2,1)}) custom-call(f32[16,56,128]{2,1,0:T(8,128)S(1)} %all-to-all-done.3.own_ref, f32[16,56,128]{2,1,0:T(8,128)S(1)} %collective-permute-done.9.other_ref, bf16[1024,384]{1,0:T(8,128)(2,1)S(1)} %get-tuple-element.34.q3, f32[128,128]{1,0:T(8,128)S(1)} %get-tuple-element.35.inv_ref, ...), custom_call_target="tpu_custom_call" | custom-call | tf_op jit(solution)/shard_map/residue/pallas_call | solution.py:473
  (9 shorter events, 0.0 us)
Async XLA Ops:
  6.9 4.5 %collective-permute-start = (f32[512,128]{1,0:T(8,128)S(1)}, f32[512,128]{1,0:T(8,128)S(1)}, u32[]{:S(2)}, u32[]{:S(2)}) collective-permute-start(f32[512,128]{1,0:T(8,128)S(1)} %get-tuple-element.22), channel_id=1, source_target_pairs={{0,32},{32,0},{1,33},{33,1},{2,34},{34,2},{3,35},{35,3},{4,36},{36... | collective-permute-start | bytes 786440 | tf_op jit(solution)/shard_map/ppermute | solution.py:494
  30.4 21.8 %copy-start = (bf16[1,1024,1792]{2,1,0:T(8,128)(2,1)S(1)}, bf16[1,1024,1792]{2,1,0:T(8,128)(2,1)}, u32[]{:S(2)}) copy-start(bf16[1,1024,1792]{2,1,0:T(8,128)(2,1)} %param.3) | copy-start | bytes 11010052
  30.4 21.9 %copy-start.1 = (bf16[1,1024,1792]{2,1,0:T(8,128)(2,1)S(1)}, bf16[1,1024,1792]{2,1,0:T(8,128)(2,1)}, u32[]{:S(2)}) copy-start(bf16[1,1024,1792]{2,1,0:T(8,128)(2,1)} %param.4) | copy-start | bytes 11010052
  46.9 4.8 %collective-permute-start.1 = (f32[512,128]{1,0:T(8,128)S(1)}, f32[512,128]{1,0:T(8,128)S(1)}, u32[]{:S(2)}, u32[]{:S(2)}) collective-permute-start(f32[512,128]{1,0:T(8,128)S(1)} %bitcast.16), channel_id=1, source_target_pairs={{0,32},{32,0},{1,33},{33,1},{2,34},{34,2},{3,35},{35,3},{4,36},{36... | collective-permute-start | bytes 786440 | tf_op jit(solution)/shard_map/ppermute | solution.py:494
  54.0 4.1 %collective-permute-start.2 = (f32[896,128]{1,0:T(8,128)S(1)}, f32[896,128]{1,0:T(8,128)S(1)}, u32[]{:S(2)}, u32[]{:S(2)}) collective-permute-start(f32[896,128]{1,0:T(8,128)S(1)} %factor_send.1), channel_id=1, source_target_pairs={{0,32},{32,0},{1,33},{33,1},{2,34},{34,2},{3,35},{35,3},{4,36},{36... | collective-permute-start | bytes 1376264 | tf_op jit(solution)/shard_map/ppermute | solution.py:494
  54.5 10.5 %collective-permute-start.5 = (f32[128,128]{1,0:T(8,128)S(1)}, f32[128,128]{1,0:T(8,128)S(1)}, u32[]{:S(2)}, u32[]{:S(2)}) collective-permute-start(f32[128,128]{1,0:T(8,128)S(1)} %get-tuple-element.25.refs_0_), channel_id=1, source_target_pairs={{0,24},{8,0},{16,8},{24,16},{1,25},{9,1},{17,9},{25,17},{2,26},{10... | collective-permute-start | bytes 196616 | tf_op jit(solution)/shard_map/ppermute | solution.py:499
  57.0 8.0 %collective-permute-start.4 = (f32[128,128]{1,0:T(8,128)S(1)}, f32[128,128]{1,0:T(8,128)S(1)}, u32[]{:S(2)}, u32[]{:S(2)}) collective-permute-start(f32[128,128]{1,0:T(8,128)S(1)} %get-tuple-element.25.refs_0_), channel_id=1, source_target_pairs={{0,16},{8,24},{16,0},{24,8},{1,17},{9,25},{17,1},{25,9},{2,18},{10... | collective-permute-start | bytes 196616 | tf_op jit(solution)/shard_map/ppermute | solution.py:499
  57.5 7.5 %collective-permute-start.3 = (f32[128,128]{1,0:T(8,128)S(1)}, f32[128,128]{1,0:T(8,128)S(1)}, u32[]{:S(2)}, u32[]{:S(2)}) collective-permute-start(f32[128,128]{1,0:T(8,128)S(1)} %get-tuple-element.25.refs_0_), channel_id=1, source_target_pairs={{0,8},{8,16},{16,24},{24,0},{1,9},{9,17},{17,25},{25,1},{2,10},{10... | collective-permute-start | bytes 196616 | tf_op jit(solution)/shard_map/ppermute | solution.py:499
  60.6 14.2 %all-to-all-start.2 = ((f32[16,56,128]{2,1,0:T(8,128)}), f32[16,56,128]{2,1,0:T(8,128)S(1)}, u32[]{:S(2)}, u32[]{:S(2)}) async-start(f32[16,56,128]{2,1,0:T(8,128)} %bitcast.4), calls=%async_computation.2 | async-start | bytes 917504 | tf_op jit(solution)/shard_map/all_to_all | solution.py:515
  70.9 10.5 %collective-permute-start.8 = (f32[128,128]{1,0:T(8,128)S(1)}, f32[128,128]{1,0:T(8,128)S(1)}, u32[]{:S(2)}, u32[]{:S(2)}) collective-permute-start(f32[128,128]{1,0:T(8,128)S(1)} %get-tuple-element.27.refs_0_), channel_id=1, source_target_pairs={{0,24},{8,0},{16,8},{24,16},{1,25},{9,1},{17,9},{25,17},{2,26},{10... | collective-permute-start | bytes 196616 | tf_op jit(solution)/shard_map/ppermute | solution.py:499
  73.6 7.9 %collective-permute-start.7 = (f32[128,128]{1,0:T(8,128)S(1)}, f32[128,128]{1,0:T(8,128)S(1)}, u32[]{:S(2)}, u32[]{:S(2)}) collective-permute-start(f32[128,128]{1,0:T(8,128)S(1)} %get-tuple-element.27.refs_0_), channel_id=1, source_target_pairs={{0,16},{8,24},{16,0},{24,8},{1,17},{9,25},{17,1},{25,9},{2,18},{10... | collective-permute-start | bytes 196616 | tf_op jit(solution)/shard_map/ppermute | solution.py:499
  74.2 7.3 %collective-permute-start.6 = (f32[128,128]{1,0:T(8,128)S(1)}, f32[128,128]{1,0:T(8,128)S(1)}, u32[]{:S(2)}, u32[]{:S(2)}) collective-permute-start(f32[128,128]{1,0:T(8,128)S(1)} %get-tuple-element.27.refs_0_), channel_id=1, source_target_pairs={{0,8},{8,16},{16,24},{24,0},{1,9},{9,17},{17,25},{25,1},{2,10},{10... | collective-permute-start | bytes 196616 | tf_op jit(solution)/shard_map/ppermute | solution.py:499
  75.6 14.5 %all-to-all-start.3 = ((f32[16,56,128]{2,1,0:T(8,128)}), f32[16,56,128]{2,1,0:T(8,128)S(1)}, u32[]{:S(2)}, u32[]{:S(2)}) async-start(f32[16,56,128]{2,1,0:T(8,128)} %total_pieces.1), calls=%async_computation.3 | async-start | bytes 917504 | tf_op jit(solution)/shard_map/all_to_all | solution.py:519
  90.1 5.5 %collective-permute-start.9 = (f32[16,56,128]{2,1,0:T(8,128)S(1)}, f32[16,56,128]{2,1,0:T(8,128)S(1)}, u32[]{:S(2)}, u32[]{:S(2)}) collective-permute-start(f32[16,56,128]{2,1,0:T(8,128)S(1)} %all-to-all-done.3.own_ref), channel_id=1, source_target_pairs={{0,32},{32,0},{1,33},{33,1},{2,34},{34,2},{3,35},{35,3},{4,36},{36... | collective-permute-start | bytes 1376264 | tf_op jit(solution)/shard_map/ppermute | solution.py:494

commit v5 on v4

--- a/solution.py
+++ b/solution.py
@@ -168,6 +168,16 @@
     return both[:, :RANK] + (both[:, RANK:] + rest)
 
 
+def wide_turned(w, x12, x1, x3):
+    w1, w2, w3 = split3(w)
+    front = jnp.concatenate(
+        [jnp.concatenate([w1, w1], axis=1), jnp.concatenate([w2, w2], axis=1)], axis=0
+    )
+    both = mm(front, x12)
+    rest = mm(w1, x3) + mm(w3, x1)
+    return both[:RANK] + (both[RANK:] + rest)
+
+
 def square_nt(hi_mid, low):
     square = mm(hi_mid, hi_mid, NT)
     cross = mm(hi_mid[:RANK], low, NT)
@@ -178,7 +188,7 @@
     )
 
 
-def prepare_kernel(own_ref, other_ref, sketch_ref, s12_ref, s3_ref, gram_ref):
+def prepare_kernel(own_ref, other_ref, s12_ref, s3_ref, gram_ref, sketch_ref):
     core = lax.axis_index("core")
     half = own_ref.shape[0]
     sketch_ref[pl.ds(pl.multiple_of(core * half, half), half), :] = own_ref[...]
@@ -195,11 +205,11 @@
     return pl.pallas_call(
         prepare_kernel,
         out_shape=[
-            jax.ShapeDtypeStruct((n, RANK), F32),
             jax.ShapeDtypeStruct((2 * RANK, n), BF16),
             jax.ShapeDtypeStruct((RANK, n), BF16),
             jax.ShapeDtypeStruct((RANK, RANK), F32),
         ],
+        scratch_shapes=[pltpu.VMEM((n, RANK), F32)],
         compiler_params=params(),
         name="prepare",
     )(own, other)
@@ -339,12 +349,12 @@
 
 
 def first_pass_kernel(*refs):
-    grams, (sketch_ref, basis_ref, inv_ref, gram_ref, a_ref, b_ref, slots) = refs[:-7], refs[-7:]
+    grams, (s12_ref, s3_ref, basis_ref, inv_ref, gram_ref, a_ref, b_ref, slots) = refs[:-8], refs[-8:]
     sum_in_order(grams, slots, a_ref)
     invert_cholesky(a_ref, b_ref, inv_ref)
-    basis = wide_nt(sketch_ref[...], inv_ref[...])
+    basis = wide_turned(inv_ref[...], s12_ref[...], s12_ref[:RANK, :], s3_ref[...])
     basis_ref[...] = basis
-    hi, mid, low = split3(basis.T)
+    hi, mid, low = split3(basis)
     gram_ref[...] = square_nt(jnp.concatenate([hi, mid], axis=0), low)
 
 
@@ -356,23 +366,23 @@
     return pl.CostEstimate(flops=4 * 10**9, bytes_accessed=2 * 10**7, transcendentals=0)
 
 
-def first_pass(grams, sketch):
+def first_pass(grams, s12, s3):
     square = jax.ShapeDtypeStruct((RANK, RANK), F32)
     return pl.pallas_call(
         first_pass_kernel,
-        out_shape=[jax.ShapeDtypeStruct(sketch.shape, F32), square, square],
+        out_shape=[jax.ShapeDtypeStruct(s3.shape, F32), square, square],
         scratch_shapes=pass_scratch(len(grams)),
         compiler_params=params(),
         cost_estimate=pass_cost(),
         name="first_pass",
-    )(*grams, sketch)
+    )(*grams, s12, s3)
 
 
 def second_pass_kernel(*refs):
     grams, (basis_one_ref, inv_one_ref, basis_ref, inv_ref, two_ref, a_ref, b_ref, slots) = refs[:-8], refs[-8:]
     sum_in_order(grams, slots, a_ref)
     invert_cholesky(a_ref, b_ref, two_ref)
-    basis_ref[...] = wide_nt(basis_one_ref[...], two_ref[...])
+    basis_ref[...] = wide_nt(basis_one_ref[...].T, two_ref[...])
     inv_ref[...] = mm32(two_ref[...], inv_one_ref[...])
 
 
@@ -380,7 +390,7 @@
     return pl.pallas_call(
         second_pass_kernel,
         out_shape=[
-            jax.ShapeDtypeStruct(basis_one.shape, F32),
+            jax.ShapeDtypeStruct(basis_one.shape[::-1], F32),
             jax.ShapeDtypeStruct(inv_one.shape, F32),
         ],
         scratch_shapes=[pltpu.VMEM((RANK, RANK), F32)] + pass_scratch(len(grams)),
@@ -432,7 +442,7 @@
     count, piece = own_ref.shape[0], own_ref.shape[1]
     n, m = new_ref.shape
     top = g_top.shape[0]
-    early, late = chunks_of(0, top, False), chunks_of(top, n, True)
+    early, late = [(0, top)], chunks_of(top, n, True)
     loads = row_loads(g_hbm, e_hbm, g_ref, e_ref, in_sems, late)
     for load in loads:
         load.start()
@@ -469,7 +479,7 @@
 def residue(own, other, q3, inv, g_top, e_top, g, e, replicas):
     n, m = g.shape
     top = g_top.shape[0]
-    early, late = chunks_of(0, top, False), chunks_of(top, n, True)
+    early, late = [(0, top)], chunks_of(top, n, True)
     return pl.pallas_call(
         functools.partial(residue_kernel, replicas),
         in_specs=[VMEM_SPEC] * 6 + [HBM_SPEC] * 2,
@@ -508,12 +518,12 @@
     pieces = (keep + swap(send)).reshape(ny * nz, -1, RANK)
     pieces = lax.all_to_all(pieces, ("y", "tensor"), 0, 0)
     own = lax.all_to_all(total_for_all(pieces), ("y", "tensor"), 0, 0).reshape(n // 2, RANK)
-    sketch, s12, s3, gram = prepare(own, swap(own))
+    s12, s3, gram = prepare(own, swap(own))
     grams = round_fsdp(gram, nx)
     got = swap(factor_send(s12, s3, g, e))
     parts = factor_keep(s12, s3, g, e, got).reshape(ny * nx, -1, RANK)
     parts = lax.all_to_all(parts, ("y", "fsdp"), 0, 0)
-    basis_one, inv_one, gram = first_pass(grams, sketch)
+    basis_one, inv_one, gram = first_pass(grams, s12, s3)
     parts, _ = lax.optimization_barrier((parts, gram))
     grams = round_fsdp(gram, nx)
     own = lax.all_to_all(total_pieces(parts), ("y", "fsdp"), 0, 0)

time: 101 us -> 101 us (level)
  no operation moved by 1% of the time
where the time goes in v5:
time: 101 us; the launch traced here: 100 us
  blocking collectives  35.4 us (35%)
  Pallas kernels  29 us (29%)
  starting transfers between devices  28.9 us (29%)
  waiting for transfers between devices  5.88 us (6%)
    all_to_all x1, blocking collectives, shards(): pieces = lax.all_to_all(pieces, ('y', 'tensor'), 0, 0)  18.9 us
    all_to_all x1, blocking collectives, shards(): lax.all_to_all(total_for_all(pieces), ('y', 'tensor'), 0, 0)  16.4 us
    ppermute x4, starting transfers between devices, swap(): return lax.ppermute(x, 'core', [(0, 1), (1, 0)])  11.2 us
    ppermute x6, starting transfers between devices, round_fsdp(): lax.ppermute(x, 'fsdp', [(i, (i + k) % count) for i in range(count)])  7.39 us
    pallas_call x1, Pallas kernels, local_sketch(): pl.pallas_call(sketch_kernel, in_specs=[HBM_SPEC] * 3, out_specs=[VMEM_SP...  6.3 us
    all_to_all x1, starting transfers between devices, shards(): own = lax.all_to_all(total_pieces(parts), ('y', 'fsdp'), 0, 0)  5.87 us
    pallas_call x1, Pallas kernels, first_pass(): pl.pallas_call(first_pass_kernel, out_shape=[jax.ShapeDtypeStruct(s3.shap...  5.7 us
    pallas_call x1, Pallas kernels, second_pass(): pl.pallas_call(second_pass_kernel, out_shape=[jax.ShapeDtypeStruct(basis_...  5.05 us
  transfers between devices with their start and end apart: 12, of which 3 were waited for; matrix products, arithmetic and copies ran while one was open for 0% of the time, Pallas kernels for 16%

profile of v5, /device:TPU:1, one launch (start us, length us, event | category | flops | bytes accessed | tf_op | source)
XLA Modules:
  0.0 100.2 jit_solution(4203786561620311562)
XLA Ops:
  0.6 6.3 %local_sketch.1 = (f32[512,128]{1,0:T(8,128)S(1)}, f32[512,128]{1,0:T(8,128)S(1)}) custom-call(bf16[1024,1792]{1,0:T(8,128)(2,1)} %bitcast.6, bf16[1024,1792]{1,0:T(8,128)(2,1)} %bitcast.11, f32[1792,128]{1,0:T(8,128)} %p_hbm.1), custom_call_target="tpu_custom_call" | custom-call | tf_op jit(solution)/shard_map/local_sketch/pallas_call | solution.py:114
  6.9 3.3 %collective-permute-start = (f32[512,128]{1,0:T(8,128)S(1)}, f32[512,128]{1,0:T(8,128)S(1)}, u32[]{:S(2)}, u32[]{:S(2)}) collective-permute-start(f32[512,128]{1,0:T(8,128)S(1)} %get-tuple-element.21), channel_id=1, source_target_pairs={{0,32},{32,0},{1,33},{33,1},{2,34},{34,2},{3,35},{35,3},{4,36},{36... | collective-permute-start | bytes 786440 | tf_op jit(solution)/shard_map/ppermute | solution.py:504
  10.3 1.2 %collective-permute-done = f32[512,128]{1,0:T(8,128)S(1)} collective-permute-done((f32[512,128]{1,0:T(8,128)S(1)}, f32[512,128]{1,0:T(8,128)S(1)}, u32[]{:S(2)}, u32[]{:S(2)}) %collective-permute-start) | collective-permute-done | bytes 262176 | tf_op jit(solution)/shard_map/ppermute | solution.py:504
  11.5 18.9 %all_to_all.20.parts_ref = f32[32,16,128]{2,1,0:T(8,128)S(1)} all-to-all(f32[32,16,128]{2,1,0:T(8,128)S(1)} %bitcast.18), channel_id=1, replica_groups=mesh['y'=4,'core'=2,'fsdp'=4,'tensor'=8] {'y','tensor'}, dimensions={0} | all-to-all | bytes 524288 | tf_op jit(solution)/shard_map/all_to_all | solution.py:519
  30.4 0.1 sketch_total.1
  30.5 16.4 %all_to_all.21 = f32[32,16,128]{2,1,0:T(8,128)S(1)} all-to-all(f32[32,16,128]{2,1,0:T(8,128)S(1)} %sketch_total.1), channel_id=1, replica_groups=mesh['y'=4,'core'=2,'fsdp'=4,'tensor'=8] {'y','tensor'}, dimensions={0} | all-to-all | bytes 524288 | tf_op jit(solution)/shard_map/all_to_all | solution.py:520
  46.9 3.6 %collective-permute-start.1 = (f32[512,128]{1,0:T(8,128)S(1)}, f32[512,128]{1,0:T(8,128)S(1)}, u32[]{:S(2)}, u32[]{:S(2)}) collective-permute-start(f32[512,128]{1,0:T(8,128)S(1)} %bitcast.16), channel_id=1, source_target_pairs={{0,32},{32,0},{1,33},{33,1},{2,34},{34,2},{3,35},{35,3},{4,36},{36... | collective-permute-start | bytes 786440 | tf_op jit(solution)/shard_map/ppermute | solution.py:504
  50.5 1.2 %collective-permute-done.1.other_ref = f32[512,128]{1,0:T(8,128)S(1)} collective-permute-done((f32[512,128]{1,0:T(8,128)S(1)}, f32[512,128]{1,0:T(8,128)S(1)}, u32[]{:S(2)}, u32[]{:S(2)}) %collective-permute-start.1) | collective-permute-done | bytes 262176 | tf_op jit(solution)/shard_map/ppermute | solution.py:504
  51.7 0.6 prepare.1
  52.3 1.7 %factor_send.1 = f32[896,128]{1,0:T(8,128)S(1)} custom-call(bf16[256,1024]{1,0:T(8,128)(2,1)S(1)} %get-tuple-element.22.s12_ref.refs_4_, bf16[128,1024]{1,0:T(8,128)(2,1)S(1)} %get-tuple-element.23.s3_ref.refs_5_, bf16[1024,1792]{1,0:T(8,128)(2,1)S(1)} %bitcast.9, bf16[1024,1792]{1,0:T(8,128)(2,1)S(1)} %bitcast.14), custom_call_target="tpu_custom_call" | custom-call | flops 1000000000 | bytes 8000000 | tf_op jit(solution)/shard_map/factor_send/pallas_call | solution.py:241
  54.0 0.5 collective-permute-start.2
  54.5 2.5 %collective-permute-start.5 = (f32[128,128]{1,0:T(8,128)S(1)}, f32[128,128]{1,0:T(8,128)S(1)}, u32[]{:S(2)}, u32[]{:S(2)}) collective-permute-start(f32[128,128]{1,0:T(8,128)S(1)} %get-tuple-element.24.refs_0_), channel_id=1, source_target_pairs={{0,24},{8,0},{16,8},{24,16},{1,25},{9,1},{17,9},{25,17},{2,26},{10... | collective-permute-start | bytes 196616 | tf_op jit(solution)/shard_map/ppermute | solution.py:509
  57.0 0.6 collective-permute-start.4
  57.5 0.6 collective-permute-start.3
  58.1 2.4 %factor_keep.1 = f32[896,128]{1,0:T(8,128)} custom-call(bf16[256,1024]{1,0:T(8,128)(2,1)S(1)} %get-tuple-element.22.s12_ref.refs_4_, bf16[128,1024]{1,0:T(8,128)(2,1)S(1)} %get-tuple-element.23.s3_ref.refs_5_, bf16[1024,1792]{1,0:T(8,128)(2,1)S(1)} %bitcast.10, bf16[1024,1792]{1,0:T(8,128)(2,1)S(1)} %bitcast.15, f32[896,128]{1,0:T(8,128)S(1)} %collective-permute-done.2.got_ref), custom_call_target="tpu_custom_call" | custom-call | flops 1000000000 | bytes 8000000 | tf_op jit(solution)/shard_map/factor_keep/pallas_call | solution.py:251
  60.5 4.4 %all-to-all-start.2 = ((f32[16,56,128]{2,1,0:T(8,128)}), f32[16,56,128]{2,1,0:T(8,128)S(1)}, u32[]{:S(2)}, u32[]{:S(2)}) async-start(f32[16,56,128]{2,1,0:T(8,128)} %bitcast.4), calls=%async_computation.2 | async-start | bytes 917504 | tf_op jit(solution)/shard_map/all_to_all | solution.py:525
  64.9 0.0 collective-permute-done.4.refs_2_
  65.0 0.0 collective-permute-done.3.refs_1_
  65.0 5.7 %first_pass.1 = (f32[128,1024]{1,0:T(8,128)S(1)}, f32[128,128]{1,0:T(8,128)S(1)}, f32[128,128]{1,0:T(8,128)S(1)}) custom-call(f32[128,128]{1,0:T(8,128)S(1)} %get-tuple-element.24.refs_0_, f32[128,128]{1,0:T(8,128)S(1)} %collective-permute-done.3.refs_1_, f32[128,128]{1,0:T(8,128)S(1)} %collective-permute-done.4.refs_2_, ...), custom_call_target="tpu_custom_call" | custom-call | flops 4000000000 | bytes 20000000 | tf_op jit(solution)/shard_map/first_pass/pallas_call | solution.py:371
  70.7 2.7 %collective-permute-start.8 = (f32[128,128]{1,0:T(8,128)S(1)}, f32[128,128]{1,0:T(8,128)S(1)}, u32[]{:S(2)}, u32[]{:S(2)}) collective-permute-start(f32[128,128]{1,0:T(8,128)S(1)} %get-tuple-element.25.refs_0_), channel_id=1, source_target_pairs={{0,24},{8,0},{16,8},{24,16},{1,25},{9,1},{17,9},{25,17},{2,26},{10... | collective-permute-start | bytes 196616 | tf_op jit(solution)/shard_map/ppermute | solution.py:509
  73.3 0.6 collective-permute-start.7
  73.9 0.6 collective-permute-start.6
  74.5 0.0 all-to-all-done.2.parts_ref
  74.5 0.8 total_pieces.1
  75.3 5.9 %all-to-all-start.3 = ((f32[16,56,128]{2,1,0:T(8,128)}), f32[16,56,128]{2,1,0:T(8,128)S(1)}, u32[]{:S(2)}, u32[]{:S(2)}) async-start(f32[16,56,128]{2,1,0:T(8,128)} %total_pieces.1), calls=%async_computation.3 | async-start | bytes 917504 | tf_op jit(solution)/shard_map/all_to_all | solution.py:529
  81.2 0.0 collective-permute-done.7.refs_2_
  81.2 5.1 %second_pass.1 = (f32[1024,128]{1,0:T(8,128)S(1)}, f32[128,128]{1,0:T(8,128)S(1)}) custom-call(f32[128,128]{1,0:T(8,128)S(1)} %get-tuple-element.25.refs_0_, f32[128,128]{1,0:T(8,128)S(1)} %collective-permute-done.6.refs_1_, f32[128,128]{1,0:T(8,128)S(1)} %collective-permute-done.7.refs_2_, f32[128,128]{1,0:T(8,128)S(1)} %collective-permute-done.8.refs_3_, ...), custom_call_target="tpu_custom_call" | custom-call | flops 4000000000 | bytes 20000000 | tf_op jit(solution)/shard_map/second_pass/pallas_call | solution.py:390
  86.3 3.5 %all-to-all-done.3.own_ref = f32[16,56,128]{2,1,0:T(8,128)S(1)} async-done(((f32[16,56,128]{2,1,0:T(8,128)}), f32[16,56,128]{2,1,0:T(8,128)S(1)}, u32[]{:S(2)}, u32[]{:S(2)}) %all-to-all-start.3) | async-done | bytes 458784 | tf_op jit(solution)/shard_map/all_to_all | solution.py:529
  89.8 3.8 %collective-permute-start.9 = (f32[16,56,128]{2,1,0:T(8,128)S(1)}, f32[16,56,128]{2,1,0:T(8,128)S(1)}, u32[]{:S(2)}, u32[]{:S(2)}) collective-permute-start(f32[16,56,128]{2,1,0:T(8,128)S(1)} %all-to-all-done.3.own_ref), channel_id=1, source_target_pairs={{0,32},{32,0},{1,33},{33,1},{2,34},{34,2},{3,35},{35,3},{4,36},{36... | collective-permute-start | bytes 1376264 | tf_op jit(solution)/shard_map/ppermute | solution.py:504
  93.6 1.7 %fetch.1 = (bf16[1024,384]{1,0:T(8,128)(2,1)S(1)}, bf16[384,1792]{1,0:T(8,128)(2,1)S(1)}, bf16[384,1792]{1,0:T(8,128)(2,1)S(1)}) custom-call(f32[1024,128]{1,0:T(8,128)S(1)} %get-tuple-element.31.basis_ref, bf16[1024,1792]{1,0:T(8,128)(2,1)} %bitcast.7, bf16[1024,1792]{1,0:T(8,128)(2,1)} %bitcast.12), custom_call_target="tpu_custom_call" | custom-call | flops 1000000 | bytes 10000000 | tf_op jit(solution)/shard_map/fetch/pallas_call | solution.py:428
  95.3 0.0 collective-permute-done.9.other_ref
  95.3 4.6 %residue.1 = (f32[1792,128]{1,0:T(8,128)}, bf16[1024,1792]{1,0:T(8,128)(2,1)}) custom-call(f32[16,56,128]{2,1,0:T(8,128)S(1)} %all-to-all-done.3.own_ref, f32[16,56,128]{2,1,0:T(8,128)S(1)} %collective-permute-done.9.other_ref, bf16[1024,384]{1,0:T(8,128)(2,1)S(1)} %get-tuple-element.32.q3, f32[128,128]{1,0:T(8,128)S(1)} %get-tuple-element.33.inv_ref, ...), custom_call_target="tpu_custom_call" | custom-call | tf_op jit(solution)/shard_map/residue/pallas_call | solution.py:483
  (9 shorter events, 0.0 us)
Async XLA Ops:
  6.9 4.5 %collective-permute-start = (f32[512,128]{1,0:T(8,128)S(1)}, f32[512,128]{1,0:T(8,128)S(1)}, u32[]{:S(2)}, u32[]{:S(2)}) collective-permute-start(f32[512,128]{1,0:T(8,128)S(1)} %get-tuple-element.21), channel_id=1, source_target_pairs={{0,32},{32,0},{1,33},{33,1},{2,34},{34,2},{3,35},{35,3},{4,36},{36... | collective-permute-start | bytes 786440 | tf_op jit(solution)/shard_map/ppermute | solution.py:504
  30.4 21.8 %copy-start = (bf16[1,1024,1792]{2,1,0:T(8,128)(2,1)S(1)}, bf16[1,1024,1792]{2,1,0:T(8,128)(2,1)}, u32[]{:S(2)}) copy-start(bf16[1,1024,1792]{2,1,0:T(8,128)(2,1)} %param.3) | copy-start | bytes 11010052
  30.4 21.8 %copy-start.1 = (bf16[1,1024,1792]{2,1,0:T(8,128)(2,1)S(1)}, bf16[1,1024,1792]{2,1,0:T(8,128)(2,1)}, u32[]{:S(2)}) copy-start(bf16[1,1024,1792]{2,1,0:T(8,128)(2,1)} %param.4) | copy-start | bytes 11010052
  46.9 4.8 %collective-permute-start.1 = (f32[512,128]{1,0:T(8,128)S(1)}, f32[512,128]{1,0:T(8,128)S(1)}, u32[]{:S(2)}, u32[]{:S(2)}) collective-permute-start(f32[512,128]{1,0:T(8,128)S(1)} %bitcast.16), channel_id=1, source_target_pairs={{0,32},{32,0},{1,33},{33,1},{2,34},{34,2},{3,35},{35,3},{4,36},{36... | collective-permute-start | bytes 786440 | tf_op jit(solution)/shard_map/ppermute | solution.py:504
  54.0 4.1 %collective-permute-start.2 = (f32[896,128]{1,0:T(8,128)S(1)}, f32[896,128]{1,0:T(8,128)S(1)}, u32[]{:S(2)}, u32[]{:S(2)}) collective-permute-start(f32[896,128]{1,0:T(8,128)S(1)} %factor_send.1), channel_id=1, source_target_pairs={{0,32},{32,0},{1,33},{33,1},{2,34},{34,2},{3,35},{35,3},{4,36},{36... | collective-permute-start | bytes 1376264 | tf_op jit(solution)/shard_map/ppermute | solution.py:504
  54.5 10.5 %collective-permute-start.5 = (f32[128,128]{1,0:T(8,128)S(1)}, f32[128,128]{1,0:T(8,128)S(1)}, u32[]{:S(2)}, u32[]{:S(2)}) collective-permute-start(f32[128,128]{1,0:T(8,128)S(1)} %get-tuple-element.24.refs_0_), channel_id=1, source_target_pairs={{0,24},{8,0},{16,8},{24,16},{1,25},{9,1},{17,9},{25,17},{2,26},{10... | collective-permute-start | bytes 196616 | tf_op jit(solution)/shard_map/ppermute | solution.py:509
  57.0 8.0 %collective-permute-start.4 = (f32[128,128]{1,0:T(8,128)S(1)}, f32[128,128]{1,0:T(8,128)S(1)}, u32[]{:S(2)}, u32[]{:S(2)}) collective-permute-start(f32[128,128]{1,0:T(8,128)S(1)} %get-tuple-element.24.refs_0_), channel_id=1, source_target_pairs={{0,16},{8,24},{16,0},{24,8},{1,17},{9,25},{17,1},{25,9},{2,18},{10... | collective-permute-start | bytes 196616 | tf_op jit(solution)/shard_map/ppermute | solution.py:509
  57.5 7.5 %collective-permute-start.3 = (f32[128,128]{1,0:T(8,128)S(1)}, f32[128,128]{1,0:T(8,128)S(1)}, u32[]{:S(2)}, u32[]{:S(2)}) collective-permute-start(f32[128,128]{1,0:T(8,128)S(1)} %get-tuple-element.24.refs_0_), channel_id=1, source_target_pairs={{0,8},{8,16},{16,24},{24,0},{1,9},{9,17},{17,25},{25,1},{2,10},{10... | collective-permute-start | bytes 196616 | tf_op jit(solution)/shard_map/ppermute | solution.py:509
  60.5 14.0 %all-to-all-start.2 = ((f32[16,56,128]{2,1,0:T(8,128)}), f32[16,56,128]{2,1,0:T(8,128)S(1)}, u32[]{:S(2)}, u32[]{:S(2)}) async-start(f32[16,56,128]{2,1,0:T(8,128)} %bitcast.4), calls=%async_computation.2 | async-start | bytes 917504 | tf_op jit(solution)/shard_map/all_to_all | solution.py:525
  70.7 10.5 %collective-permute-start.8 = (f32[128,128]{1,0:T(8,128)S(1)}, f32[128,128]{1,0:T(8,128)S(1)}, u32[]{:S(2)}, u32[]{:S(2)}) collective-permute-start(f32[128,128]{1,0:T(8,128)S(1)} %get-tuple-element.25.refs_0_), channel_id=1, source_target_pairs={{0,24},{8,0},{16,8},{24,16},{1,25},{9,1},{17,9},{25,17},{2,26},{10... | collective-permute-start | bytes 196616 | tf_op jit(solution)/shard_map/ppermute | solution.py:509
  73.3 7.9 %collective-permute-start.7 = (f32[128,128]{1,0:T(8,128)S(1)}, f32[128,128]{1,0:T(8,128)S(1)}, u32[]{:S(2)}, u32[]{:S(2)}) collective-permute-start(f32[128,128]{1,0:T(8,128)S(1)} %get-tuple-element.25.refs_0_), channel_id=1, source_target_pairs={{0,16},{8,24},{16,0},{24,8},{1,17},{9,25},{17,1},{25,9},{2,18},{10... | collective-permute-start | bytes 196616 | tf_op jit(solution)/shard_map/ppermute | solution.py:509
  73.9 7.3 %collective-permute-start.6 = (f32[128,128]{1,0:T(8,128)S(1)}, f32[128,128]{1,0:T(8,128)S(1)}, u32[]{:S(2)}, u32[]{:S(2)}) collective-permute-start(f32[128,128]{1,0:T(8,128)S(1)} %get-tuple-element.25.refs_0_), channel_id=1, source_target_pairs={{0,8},{8,16},{16,24},{24,0},{1,9},{9,17},{17,25},{25,1},{2,10},{10... | collective-permute-start | bytes 196616 | tf_op jit(solution)/shard_map/ppermute | solution.py:509
  75.3 14.5 %all-to-all-start.3 = ((f32[16,56,128]{2,1,0:T(8,128)}), f32[16,56,128]{2,1,0:T(8,128)S(1)}, u32[]{:S(2)}, u32[]{:S(2)}) async-start(f32[16,56,128]{2,1,0:T(8,128)} %total_pieces.1), calls=%async_computation.3 | async-start | bytes 917504 | tf_op jit(solution)/shard_map/all_to_all | solution.py:529
  89.8 5.5 %collective-permute-start.9 = (f32[16,56,128]{2,1,0:T(8,128)S(1)}, f32[16,56,128]{2,1,0:T(8,128)S(1)}, u32[]{:S(2)}, u32[]{:S(2)}) collective-permute-start(f32[16,56,128]{2,1,0:T(8,128)S(1)} %all-to-all-done.3.own_ref), channel_id=1, source_target_pairs={{0,32},{32,0},{1,33},{33,1},{2,34},{34,2},{3,35},{35,3},{4,36},{36... | collective-permute-start | bytes 1376264 | tf_op jit(solution)/shard_map/ppermute | solution.py:504

commit v6 on v5

--- a/solution.py
+++ b/solution.py
@@ -188,20 +188,45 @@
     )
 
 
-def prepare_kernel(own_ref, other_ref, s12_ref, s3_ref, gram_ref, sketch_ref):
+def prepare_own_kernel(own_ref, o12_ref, o3_ref, gram_ref):
+    hi, mid, low = split3(own_ref[...].T)
+    o12_ref[:RANK, :] = hi
+    o12_ref[RANK:, :] = mid
+    o3_ref[...] = low
+    gram_ref[...] = square_nt(o12_ref[...], low)
+
+
+def prepare_own(own):
+    half = own.shape[0]
+    return pl.pallas_call(
+        prepare_own_kernel,
+        out_shape=[
+            jax.ShapeDtypeStruct((2 * RANK, half), BF16),
+            jax.ShapeDtypeStruct((RANK, half), BF16),
+            jax.ShapeDtypeStruct((RANK, RANK), F32),
+        ],
+        compiler_params=params(),
+        cost_estimate=pl.CostEstimate(flops=10**9, bytes_accessed=8 * 10**6, transcendentals=0),
+        name="prepare_own",
+    )(own)
+
+
+def prepare_kernel(o12_ref, o3_ref, gram_own_ref, other_ref, s12_ref, s3_ref, gram_ref):
     core = lax.axis_index("core")
-    half = own_ref.shape[0]
-    sketch_ref[pl.ds(pl.multiple_of(core * half, half), half), :] = own_ref[...]
-    sketch_ref[pl.ds(pl.multiple_of((1 - core) * half, half), half), :] = other_ref[...]
-    hi, mid, low = split3(sketch_ref[...].T)
-    s12_ref[:RANK, :] = hi
-    s12_ref[RANK:, :] = mid
-    s3_ref[...] = low
-    gram_ref[...] = square_nt(s12_ref[...], low)
-
-
-def prepare(own, other):
-    n = 2 * own.shape[0]
+    half = other_ref.shape[0]
+    mine = pl.ds(pl.multiple_of(core * half, half), half)
+    theirs = pl.ds(pl.multiple_of((1 - core) * half, half), half)
+    s12_ref[:, mine] = o12_ref[...]
+    s3_ref[:, mine] = o3_ref[...]
+    hi, mid, low = split3(other_ref[...].T)
+    s12_ref[:RANK, theirs] = hi
+    s12_ref[RANK:, theirs] = mid
+    s3_ref[:, theirs] = low
+    gram_ref[...] = gram_own_ref[...] + square_nt(jnp.concatenate([hi, mid], axis=0), low)
+
+
+def prepare(o12, o3, gram_own, other):
+    n = 2 * other.shape[0]
     return pl.pallas_call(
         prepare_kernel,
         out_shape=[
@@ -209,10 +234,9 @@
             jax.ShapeDtypeStruct((RANK, n), BF16),
             jax.ShapeDtypeStruct((RANK, RANK), F32),
         ],
-        scratch_shapes=[pltpu.VMEM((n, RANK), F32)],
         compiler_params=params(),
         name="prepare",
-    )(own, other)
+    )(o12, o3, gram_own, other)
 
 
 def factor_send_kernel(s12_ref, s3_ref, g_ref, e_ref, send_ref):
@@ -518,7 +542,8 @@
     pieces = (keep + swap(send)).reshape(ny * nz, -1, RANK)
     pieces = lax.all_to_all(pieces, ("y", "tensor"), 0, 0)
     own = lax.all_to_all(total_for_all(pieces), ("y", "tensor"), 0, 0).reshape(n // 2, RANK)
-    s12, s3, gram = prepare(own, swap(own))
+    other = swap(own)
+    s12, s3, gram = prepare(*prepare_own(own), other)
     grams = round_fsdp(gram, nx)
     got = swap(factor_send(s12, s3, g, e))
     parts = factor_keep(s12, s3, g, e, got).reshape(ny * nx, -1, RANK)

time: 101 us -> 100 us (0.990)
  transfers between devices with their start and end apart: 12 -> 12, of which waited for: 3 -> 4; matrix products, arithmetic and copies ran while one was open for 0% -> 0% of each run, Pallas kernels for 16% -> 16%
where the time goes in v6:
time: 100 us
  blocking collectives  35.4 us (35%)
  Pallas kernels  29.3 us (29%)
  starting transfers between devices  28.8 us (29%)
  waiting for transfers between devices  5.52 us (6%)
    all_to_all x1, blocking collectives, shards(): pieces = lax.all_to_all(pieces, ('y', 'tensor'), 0, 0)  18.9 us
    all_to_all x1, blocking collectives, shards(): lax.all_to_all(total_for_all(pieces), ('y', 'tensor'), 0, 0)  16.4 us
    ppermute x4, starting transfers between devices, swap(): return lax.ppermute(x, 'core', [(0, 1), (1, 0)])  11.1 us
    ppermute x6, starting transfers between devices, round_fsdp(): lax.ppermute(x, 'fsdp', [(i, (i + k) % count) for i in range(count)])  7.44 us
    pallas_call x1, Pallas kernels, local_sketch(): pl.pallas_call(sketch_kernel, in_specs=[HBM_SPEC] * 3, out_specs=[VMEM_SP...  6.3 us
    all_to_all x1, starting transfers between devices, shards(): own = lax.all_to_all(total_pieces(parts), ('y', 'fsdp'), 0, 0)  5.8 us
    pallas_call x1, Pallas kernels, first_pass(): pl.pallas_call(first_pass_kernel, out_shape=[jax.ShapeDtypeStruct(s3.shap...  5.7 us
    pallas_call x1, Pallas kernels, second_pass(): pl.pallas_call(second_pass_kernel, out_shape=[jax.ShapeDtypeStruct(basis_...  5.05 us
  transfers between devices with their start and end apart: 12, of which 4 were waited for; matrix products, arithmetic and copies ran while one was open for 0% of the time, Pallas kernels for 16%

profile of v6, /device:TPU:1, one launch (start us, length us, event | category | flops | bytes accessed | tf_op | source)
XLA Modules:
  0.0 100.0 jit_solution(7559822516922678169)
XLA Ops:
  0.6 6.3 %local_sketch.1 = (f32[512,128]{1,0:T(8,128)S(1)}, f32[512,128]{1,0:T(8,128)S(1)}) custom-call(bf16[1024,1792]{1,0:T(8,128)(2,1)} %bitcast.6, bf16[1024,1792]{1,0:T(8,128)(2,1)} %bitcast.11, f32[1792,128]{1,0:T(8,128)} %p_hbm.1), custom_call_target="tpu_custom_call" | custom-call | tf_op jit(solution)/shard_map/local_sketch/pallas_call | solution.py:114
  6.9 3.3 %collective-permute-start = (f32[512,128]{1,0:T(8,128)S(1)}, f32[512,128]{1,0:T(8,128)S(1)}, u32[]{:S(2)}, u32[]{:S(2)}) collective-permute-start(f32[512,128]{1,0:T(8,128)S(1)} %get-tuple-element.24), channel_id=1, source_target_pairs={{0,32},{32,0},{1,33},{33,1},{2,34},{34,2},{3,35},{35,3},{4,36},{36... | collective-permute-start | bytes 786440 | tf_op jit(solution)/shard_map/ppermute | solution.py:528
  10.3 1.2 %collective-permute-done = f32[512,128]{1,0:T(8,128)S(1)} collective-permute-done((f32[512,128]{1,0:T(8,128)S(1)}, f32[512,128]{1,0:T(8,128)S(1)}, u32[]{:S(2)}, u32[]{:S(2)}) %collective-permute-start) | collective-permute-done | bytes 262176 | tf_op jit(solution)/shard_map/ppermute | solution.py:528
  11.5 18.9 %all_to_all.20.parts_ref = f32[32,16,128]{2,1,0:T(8,128)S(1)} all-to-all(f32[32,16,128]{2,1,0:T(8,128)S(1)} %bitcast.18), channel_id=1, replica_groups=mesh['y'=4,'core'=2,'fsdp'=4,'tensor'=8] {'y','tensor'}, dimensions={0} | all-to-all | bytes 524288 | tf_op jit(solution)/shard_map/all_to_all | solution.py:543
  30.4 0.1 sketch_total.1
  30.5 0.0 copy-start
  30.5 16.4 %all_to_all.21 = f32[32,16,128]{2,1,0:T(8,128)S(1)} all-to-all(f32[32,16,128]{2,1,0:T(8,128)S(1)} %sketch_total.1), channel_id=1, replica_groups=mesh['y'=4,'core'=2,'fsdp'=4,'tensor'=8] {'y','tensor'}, dimensions={0} | all-to-all | bytes 524288 | tf_op jit(solution)/shard_map/all_to_all | solution.py:544
  46.9 3.6 %collective-permute-start.1 = (f32[512,128]{1,0:T(8,128)S(1)}, f32[512,128]{1,0:T(8,128)S(1)}, u32[]{:S(2)}, u32[]{:S(2)}) collective-permute-start(f32[512,128]{1,0:T(8,128)S(1)} %bitcast.16), channel_id=1, source_target_pairs={{0,32},{32,0},{1,33},{33,1},{2,34},{34,2},{3,35},{35,3},{4,36},{36... | collective-permute-start | bytes 786440 | tf_op jit(solution)/shard_map/ppermute | solution.py:528
  50.5 0.4 prepare_own.1
  50.9 0.7 collective-permute-done.1.other_ref
  51.7 0.4 prepare.1
  52.1 1.7 %factor_send.1 = f32[896,128]{1,0:T(8,128)S(1)} custom-call(bf16[256,1024]{1,0:T(8,128)(2,1)S(1)} %get-tuple-element.28.s12_ref.refs_4_, bf16[128,1024]{1,0:T(8,128)(2,1)S(1)} %get-tuple-element.29.s3_ref.refs_5_, bf16[1024,1792]{1,0:T(8,128)(2,1)S(1)} %bitcast.9, bf16[1024,1792]{1,0:T(8,128)(2,1)S(1)} %bitcast.14), custom_call_target="tpu_custom_call" | custom-call | flops 1000000000 | bytes 8000000 | tf_op jit(solution)/shard_map/factor_send/pallas_call | solution.py:265
  53.9 0.5 collective-permute-start.2
  54.3 2.5 %collective-permute-start.5 = (f32[128,128]{1,0:T(8,128)S(1)}, f32[128,128]{1,0:T(8,128)S(1)}, u32[]{:S(2)}, u32[]{:S(2)}) collective-permute-start(f32[128,128]{1,0:T(8,128)S(1)} %get-tuple-element.30.refs_0_), channel_id=1, source_target_pairs={{0,24},{8,0},{16,8},{24,16},{1,25},{9,1},{17,9},{25,17},{2,26},{10... | collective-permute-start | bytes 196616 | tf_op jit(solution)/shard_map/ppermute | solution.py:533
  56.8 0.5 collective-permute-start.4
  57.3 0.6 collective-permute-start.3
  58.0 0.0 collective-permute-done.2.got_ref
  58.0 2.4 %factor_keep.1 = f32[896,128]{1,0:T(8,128)} custom-call(bf16[256,1024]{1,0:T(8,128)(2,1)S(1)} %get-tuple-element.28.s12_ref.refs_4_, bf16[128,1024]{1,0:T(8,128)(2,1)S(1)} %get-tuple-element.29.s3_ref.refs_5_, bf16[1024,1792]{1,0:T(8,128)(2,1)S(1)} %bitcast.10, bf16[1024,1792]{1,0:T(8,128)(2,1)S(1)} %bitcast.15, f32[896,128]{1,0:T(8,128)S(1)} %collective-permute-done.2.got_ref), custom_call_target="tpu_custom_call" | custom-call | flops 1000000000 | bytes 8000000 | tf_op jit(solution)/shard_map/factor_keep/pallas_call | solution.py:275
  60.4 4.4 %all-to-all-start.2 = ((f32[16,56,128]{2,1,0:T(8,128)}), f32[16,56,128]{2,1,0:T(8,128)S(1)}, u32[]{:S(2)}, u32[]{:S(2)}) async-start(f32[16,56,128]{2,1,0:T(8,128)} %bitcast.4), calls=%async_computation.2 | async-start | bytes 917504 | tf_op jit(solution)/shard_map/all_to_all | solution.py:550
  64.8 0.0 collective-permute-done.5.refs_3_
  64.9 5.7 %first_pass.1 = (f32[128,1024]{1,0:T(8,128)S(1)}, f32[128,128]{1,0:T(8,128)S(1)}, f32[128,128]{1,0:T(8,128)S(1)}) custom-call(f32[128,128]{1,0:T(8,128)S(1)} %get-tuple-element.30.refs_0_, f32[128,128]{1,0:T(8,128)S(1)} %collective-permute-done.3.refs_1_, f32[128,128]{1,0:T(8,128)S(1)} %collective-permute-done.4.refs_2_, ...), custom_call_target="tpu_custom_call" | custom-call | flops 4000000000 | bytes 20000000 | tf_op jit(solution)/shard_map/first_pass/pallas_call | solution.py:395
  70.6 2.6 %collective-permute-start.8 = (f32[128,128]{1,0:T(8,128)S(1)}, f32[128,128]{1,0:T(8,128)S(1)}, u32[]{:S(2)}, u32[]{:S(2)}) collective-permute-start(f32[128,128]{1,0:T(8,128)S(1)} %get-tuple-element.31.refs_0_), channel_id=1, source_target_pairs={{0,24},{8,0},{16,8},{24,16},{1,25},{9,1},{17,9},{25,17},{2,26},{10... | collective-permute-start | bytes 196616 | tf_op jit(solution)/shard_map/ppermute | solution.py:533
  73.2 0.6 collective-permute-start.7
  73.8 0.6 collective-permute-start.6
  74.4 0.1 all-to-all-done.2.parts_ref
  74.5 0.8 total_pieces.1
  75.3 5.8 %all-to-all-start.3 = ((f32[16,56,128]{2,1,0:T(8,128)}), f32[16,56,128]{2,1,0:T(8,128)S(1)}, u32[]{:S(2)}, u32[]{:S(2)}) async-start(f32[16,56,128]{2,1,0:T(8,128)} %total_pieces.1), calls=%async_computation.3 | async-start | bytes 917504 | tf_op jit(solution)/shard_map/all_to_all | solution.py:554
  81.1 5.0 %second_pass.1 = (f32[1024,128]{1,0:T(8,128)S(1)}, f32[128,128]{1,0:T(8,128)S(1)}) custom-call(f32[128,128]{1,0:T(8,128)S(1)} %get-tuple-element.31.refs_0_, f32[128,128]{1,0:T(8,128)S(1)} %collective-permute-done.6.refs_1_, f32[128,128]{1,0:T(8,128)S(1)} %collective-permute-done.7.refs_2_, f32[128,128]{1,0:T(8,128)S(1)} %collective-permute-done.8.refs_3_, ...), custom_call_target="tpu_custom_call" | custom-call | flops 4000000000 | bytes 20000000 | tf_op jit(solution)/shard_map/second_pass/pallas_call | solution.py:414
  86.2 3.5 %all-to-all-done.3.own_ref = f32[16,56,128]{2,1,0:T(8,128)S(1)} async-done(((f32[16,56,128]{2,1,0:T(8,128)}), f32[16,56,128]{2,1,0:T(8,128)S(1)}, u32[]{:S(2)}, u32[]{:S(2)}) %all-to-all-start.3) | async-done | bytes 458784 | tf_op jit(solution)/shard_map/all_to_all | solution.py:554
  89.7 3.7 %collective-permute-start.9 = (f32[16,56,128]{2,1,0:T(8,128)S(1)}, f32[16,56,128]{2,1,0:T(8,128)S(1)}, u32[]{:S(2)}, u32[]{:S(2)}) collective-permute-start(f32[16,56,128]{2,1,0:T(8,128)S(1)} %all-to-all-done.3.own_ref), channel_id=1, source_target_pairs={{0,32},{32,0},{1,33},{33,1},{2,34},{34,2},{3,35},{35,3},{4,36},{36... | collective-permute-start | bytes 1376264 | tf_op jit(solution)/shard_map/ppermute | solution.py:528
  93.4 1.7 %fetch.1 = (bf16[1024,384]{1,0:T(8,128)(2,1)S(1)}, bf16[384,1792]{1,0:T(8,128)(2,1)S(1)}, bf16[384,1792]{1,0:T(8,128)(2,1)S(1)}) custom-call(f32[1024,128]{1,0:T(8,128)S(1)} %get-tuple-element.37.basis_ref, bf16[1024,1792]{1,0:T(8,128)(2,1)} %bitcast.7, bf16[1024,1792]{1,0:T(8,128)(2,1)} %bitcast.12), custom_call_target="tpu_custom_call" | custom-call | flops 1000000 | bytes 10000000 | tf_op jit(solution)/shard_map/fetch/pallas_call | solution.py:452
  95.2 4.6 %residue.1 = (f32[1792,128]{1,0:T(8,128)}, bf16[1024,1792]{1,0:T(8,128)(2,1)}) custom-call(f32[16,56,128]{2,1,0:T(8,128)S(1)} %all-to-all-done.3.own_ref, f32[16,56,128]{2,1,0:T(8,128)S(1)} %collective-permute-done.9.other_ref, bf16[1024,384]{1,0:T(8,128)(2,1)S(1)} %get-tuple-element.38.q3, f32[128,128]{1,0:T(8,128)S(1)} %get-tuple-element.39.inv_ref, ...), custom_call_target="tpu_custom_call" | custom-call | tf_op jit(solution)/shard_map/residue/pallas_call | solution.py:507
  (10 shorter events, 0.1 us)
Async XLA Ops:
  6.9 4.5 %collective-permute-start = (f32[512,128]{1,0:T(8,128)S(1)}, f32[512,128]{1,0:T(8,128)S(1)}, u32[]{:S(2)}, u32[]{:S(2)}) collective-permute-start(f32[512,128]{1,0:T(8,128)S(1)} %get-tuple-element.24), channel_id=1, source_target_pairs={{0,32},{32,0},{1,33},{33,1},{2,34},{34,2},{3,35},{35,3},{4,36},{36... | collective-permute-start | bytes 786440 | tf_op jit(solution)/shard_map/ppermute | solution.py:528
  30.4 21.7 %copy-start.1 = (bf16[1,1024,1792]{2,1,0:T(8,128)(2,1)S(1)}, bf16[1,1024,1792]{2,1,0:T(8,128)(2,1)}, u32[]{:S(2)}) copy-start(bf16[1,1024,1792]{2,1,0:T(8,128)(2,1)} %param.4) | copy-start | bytes 11010052
  30.5 21.7 %copy-start = (bf16[1,1024,1792]{2,1,0:T(8,128)(2,1)S(1)}, bf16[1,1024,1792]{2,1,0:T(8,128)(2,1)}, u32[]{:S(2)}) copy-start(bf16[1,1024,1792]{2,1,0:T(8,128)(2,1)} %param.3) | copy-start | bytes 11010052
  46.9 4.8 %collective-permute-start.1 = (f32[512,128]{1,0:T(8,128)S(1)}, f32[512,128]{1,0:T(8,128)S(1)}, u32[]{:S(2)}, u32[]{:S(2)}) collective-permute-start(f32[512,128]{1,0:T(8,128)S(1)} %bitcast.16), channel_id=1, source_target_pairs={{0,32},{32,0},{1,33},{33,1},{2,34},{34,2},{3,35},{35,3},{4,36},{36... | collective-permute-start | bytes 786440 | tf_op jit(solution)/shard_map/ppermute | solution.py:528
  53.9 4.1 %collective-permute-start.2 = (f32[896,128]{1,0:T(8,128)S(1)}, f32[896,128]{1,0:T(8,128)S(1)}, u32[]{:S(2)}, u32[]{:S(2)}) collective-permute-start(f32[896,128]{1,0:T(8,128)S(1)} %factor_send.1), channel_id=1, source_target_pairs={{0,32},{32,0},{1,33},{33,1},{2,34},{34,2},{3,35},{35,3},{4,36},{36... | collective-permute-start | bytes 1376264 | tf_op jit(solution)/shard_map/ppermute | solution.py:528
  54.3 10.5 %collective-permute-start.5 = (f32[128,128]{1,0:T(8,128)S(1)}, f32[128,128]{1,0:T(8,128)S(1)}, u32[]{:S(2)}, u32[]{:S(2)}) collective-permute-start(f32[128,128]{1,0:T(8,128)S(1)} %get-tuple-element.30.refs_0_), channel_id=1, source_target_pairs={{0,24},{8,0},{16,8},{24,16},{1,25},{9,1},{17,9},{25,17},{2,26},{10... | collective-permute-start | bytes 196616 | tf_op jit(solution)/shard_map/ppermute | solution.py:533
  56.8 8.0 %collective-permute-start.4 = (f32[128,128]{1,0:T(8,128)S(1)}, f32[128,128]{1,0:T(8,128)S(1)}, u32[]{:S(2)}, u32[]{:S(2)}) collective-permute-start(f32[128,128]{1,0:T(8,128)S(1)} %get-tuple-element.30.refs_0_), channel_id=1, source_target_pairs={{0,16},{8,24},{16,0},{24,8},{1,17},{9,25},{17,1},{25,9},{2,18},{10... | collective-permute-start | bytes 196616 | tf_op jit(solution)/shard_map/ppermute | solution.py:533
  57.3 7.5 %collective-permute-start.3 = (f32[128,128]{1,0:T(8,128)S(1)}, f32[128,128]{1,0:T(8,128)S(1)}, u32[]{:S(2)}, u32[]{:S(2)}) collective-permute-start(f32[128,128]{1,0:T(8,128)S(1)} %get-tuple-element.30.refs_0_), channel_id=1, source_target_pairs={{0,8},{8,16},{16,24},{24,0},{1,9},{9,17},{17,25},{25,1},{2,10},{10... | collective-permute-start | bytes 196616 | tf_op jit(solution)/shard_map/ppermute | solution.py:533
  60.4 14.1 %all-to-all-start.2 = ((f32[16,56,128]{2,1,0:T(8,128)}), f32[16,56,128]{2,1,0:T(8,128)S(1)}, u32[]{:S(2)}, u32[]{:S(2)}) async-start(f32[16,56,128]{2,1,0:T(8,128)} %bitcast.4), calls=%async_computation.2 | async-start | bytes 917504 | tf_op jit(solution)/shard_map/all_to_all | solution.py:550
  70.6 10.5 %collective-permute-start.8 = (f32[128,128]{1,0:T(8,128)S(1)}, f32[128,128]{1,0:T(8,128)S(1)}, u32[]{:S(2)}, u32[]{:S(2)}) collective-permute-start(f32[128,128]{1,0:T(8,128)S(1)} %get-tuple-element.31.refs_0_), channel_id=1, source_target_pairs={{0,24},{8,0},{16,8},{24,16},{1,25},{9,1},{17,9},{25,17},{2,26},{10... | collective-permute-start | bytes 196616 | tf_op jit(solution)/shard_map/ppermute | solution.py:533
  73.2 7.9 %collective-permute-start.7 = (f32[128,128]{1,0:T(8,128)S(1)}, f32[128,128]{1,0:T(8,128)S(1)}, u32[]{:S(2)}, u32[]{:S(2)}) collective-permute-start(f32[128,128]{1,0:T(8,128)S(1)} %get-tuple-element.31.refs_0_), channel_id=1, source_target_pairs={{0,16},{8,24},{16,0},{24,8},{1,17},{9,25},{17,1},{25,9},{2,18},{10... | collective-permute-start | bytes 196616 | tf_op jit(solution)/shard_map/ppermute | solution.py:533
  73.8 7.3 %collective-permute-start.6 = (f32[128,128]{1,0:T(8,128)S(1)}, f32[128,128]{1,0:T(8,128)S(1)}, u32[]{:S(2)}, u32[]{:S(2)}) collective-permute-start(f32[128,128]{1,0:T(8,128)S(1)} %get-tuple-element.31.refs_0_), channel_id=1, source_target_pairs={{0,8},{8,16},{16,24},{24,0},{1,9},{9,17},{17,25},{25,1},{2,10},{10... | collective-permute-start | bytes 196616 | tf_op jit(solution)/shard_map/ppermute | solution.py:533
  75.3 14.4 %all-to-all-start.3 = ((f32[16,56,128]{2,1,0:T(8,128)}), f32[16,56,128]{2,1,0:T(8,128)S(1)}, u32[]{:S(2)}, u32[]{:S(2)}) async-start(f32[16,56,128]{2,1,0:T(8,128)} %total_pieces.1), calls=%async_computation.3 | async-start | bytes 917504 | tf_op jit(solution)/shard_map/all_to_all | solution.py:554
  89.7 5.5 %collective-permute-start.9 = (f32[16,56,128]{2,1,0:T(8,128)S(1)}, f32[16,56,128]{2,1,0:T(8,128)S(1)}, u32[]{:S(2)}, u32[]{:S(2)}) collective-permute-start(f32[16,56,128]{2,1,0:T(8,128)S(1)} %all-to-all-done.3.own_ref), channel_id=1, source_target_pairs={{0,32},{32,0},{1,33},{33,1},{2,34},{34,2},{3,35},{35,3},{4,36},{36... | collective-permute-start | bytes 1376264 | tf_op jit(solution)/shard_map/ppermute | solution.py:528
